TPU v7x, 128 devices: a whole 4x4x4 slice. The times are simulated.
128 devices in a mesh: scene: 4 (over y), tile: 32 (over x, z, core).
Axes of the slice: x: 4, y: 4, z: 4, core: 2. Of those that a mesh axis runs over, the one named last changes fastest.
Arguments:
- features: bfloat16 [128, 32, 64, 768], P(('scene', 'tile')), parts along dimension 0, may hold values from -120 to 120
- dw_kernel: bfloat16 [3, 3, 3, 768], replicated, may hold values from -2 to 2
- se_reduce: bfloat16 [3, 768, 192], replicated, may hold values from -0.21875 to 0.21875
- se_expand: bfloat16 [3, 192, 768], replicated, may hold values from -0.4375 to 0.4375
- mix_weight: bfloat16 [3, 768, 768], replicated, may hold values from -0.21875 to 0.21875
- norm_gain: float32 [768], replicated, may hold values from 0.5 to 2
- kv_weight: bfloat16 [768, 1536], replicated, may hold values from -0.21875 to 0.21875
- kv_bias: float32 [1536], replicated, may hold values from -3 to 3
- proj_weight: bfloat16 [768, 768], replicated, may hold values from -0.21875 to 0.21875
- proj_bias: float32 [768], replicated, may hold values from -3 to 3
Outputs:
- blocked: bfloat16 [128, 32, 64, 768], P(('scene', 'tile')), parts along dimension 0
There are 4 independent parts, one for each index of `scene`. A program takes and returns all parts, laid end to end along the dimension named above; an argument that names none is the same for every part. Nothing has to cross between parts.
All inputs are finite; a program needn't handle non-finite values.
Results may differ from a plain program's by a relative error of at most 0.008.
The roundings to bfloat16 on the way count: a program that leaves them out, or rounds other values in their place, can miss the bound.
Values may be sent and summed in bfloat16 or wider, within the bound.
No kernel may reach another device: no remote copies, remote signals or barrier semaphores. Data moves between devices by JAX's collectives and lax.ppermute only.
A program may use at most 128 MiB of HBM per device.

v0:
```python
import jax
import jax.numpy as jnp
from jax import lax
from jax.sharding import PartitionSpec as P

HEADS = 24
TILE_COLS = 4


EPSILON = 1e-05


def shifted(value, axis, steps):
    count = lax.axis_size(axis)
    initial, last = (max(0, -steps), min(count, count - steps))
    return lax.ppermute(value, axis, [(source, source + steps) for source in range(initial, last)])


def mark_fill(piece, missing, fill_value):
    return jnp.where(missing, jnp.full_like(piece, fill_value), piece)


def strip_rims(inputs, grid_row, grid_col, grid_rows, fill_value, both_sides):
    if both_sides:
        move_list = ((TILE_COLS, True), (-TILE_COLS, False))
    else:
        move_list = ((TILE_COLS, True),)
    received = []
    for stride, from_above in move_list:
        edge_part = inputs[-1:] if from_above else inputs[:1]
        arrived = shifted(edge_part, "tile", stride)
        missing = grid_row == 0 if from_above else grid_row == grid_rows - 1
        received.append(mark_fill(arrived, missing, fill_value))
    stacked = jnp.concatenate([received[0], inputs] + received[1:], axis=0)
    received = []
    for stride, from_left in ((1, True), (-1, False))[: len(move_list)]:
        edge_part = stacked[:, -1:] if from_left else stacked[:, :1]
        arrived = shifted(edge_part, "tile", stride)
        missing = grid_col == 0 if from_left else grid_col == TILE_COLS - 1
        received.append(mark_fill(arrived, missing, fill_value))
    return jnp.concatenate([received[0], stacked] + received[1:], axis=1)


def squeeze_gate(channel_mean, reduce_matrix, expand_matrix):
    inner = jax.nn.gelu(
        jnp.dot(channel_mean, reduce_matrix.astype(jnp.float32), precision=lax.Precision.HIGHEST),
        approximate=False,
    )
    return jax.nn.sigmoid(
        jnp.dot(inner, expand_matrix.astype(jnp.float32), precision=lax.Precision.HIGHEST)
    )


def pool_half(padded):
    height = padded.shape[0] - 1
    breadth = padded.shape[1] - 1
    paired = padded[:height].reshape(height // 2, 2, breadth + 1, padded.shape[2])
    rowmax = jnp.maximum(jnp.max(paired, axis=1), padded[2::2])
    paired = rowmax[:, :breadth].reshape(height // 2, breadth // 2, 2, padded.shape[2])
    return jnp.maximum(jnp.max(paired, axis=2), rowmax[:, 2::2])


def level_step(
    inputs, kernel, reduce_matrix, expand_matrix, mix_matrix, rim_rule, sum_rule, cell_count
):
    height, breadth, channels = inputs.shape
    padded = rim_rule(inputs, 0.0, True)
    summed = jnp.zeros(inputs.shape, jnp.float32)
    for shift_row in range(3):
        for shift_col in range(3):
            window_part = padded[shift_row : shift_row + height, shift_col : shift_col + breadth]
            summed = summed + window_part.astype(jnp.float32) * kernel[shift_row, shift_col].astype(
                jnp.float32
            )
    response = jax.nn.gelu(summed, approximate=False)
    channel_mean = sum_rule(jnp.sum(response, axis=(0, 1))) / cell_count
    gate_values = squeeze_gate(channel_mean, reduce_matrix, expand_matrix)
    scaled = (response * gate_values).astype(jnp.bfloat16)
    product = jnp.dot(
        scaled.reshape(-1, channels), mix_matrix, preferred_element_type=jnp.float32
    ).reshape(inputs.shape)
    mixed_map = (inputs.astype(jnp.float32) + product).astype(jnp.bfloat16)
    return pool_half(rim_rule(mixed_map, -jnp.inf, False))


def assemble(collected, grid_rows):
    tile_count, tile_high, tile_wide, channels = collected.shape
    arranged = collected.reshape(grid_rows, tile_count // grid_rows, tile_high, tile_wide, channels)
    return arranged.transpose(0, 2, 1, 3, 4).reshape(
        grid_rows * tile_high, tile_count // grid_rows * tile_wide, channels
    )


def body(
    features,
    dw_kernel,
    se_reduce,
    se_expand,
    mix_weight,
    norm_gain,
    kv_weight,
    kv_bias,
    proj_weight,
    proj_bias,
):
    tile_map = features[0]
    grid_size = lax.axis_size("tile")
    grid_rows = grid_size // TILE_COLS
    position = lax.axis_index("tile")
    grid_row = position // TILE_COLS
    grid_col = position % TILE_COLS
    level_count = dw_kernel.shape[0]

    def spread_rim(inputs, fill_value, both_sides):
        return strip_rims(inputs, grid_row, grid_col, grid_rows, fill_value, both_sides)

    def scene_sum(partial_sum):
        return lax.psum(partial_sum, "tile")

    coarse = tile_map
    for level_index in range(level_count):
        coarse = level_step(
            coarse,
            dw_kernel[level_index],
            se_reduce[level_index],
            se_expand[level_index],
            mix_weight[level_index],
            spread_rim,
            scene_sum,
            coarse.shape[0] * coarse.shape[1] * grid_size,
        )
    collected = lax.all_gather(coarse[None], "tile", axis=0, tiled=True)
    query_map = assemble(collected, grid_rows)
    height, breadth, channels = tile_map.shape
    win_side = query_map.shape[0]
    length = win_side * win_side
    window_rows = height // win_side
    window_cols = breadth // win_side
    window_count = window_rows * window_cols
    head_count = HEADS
    head_width = channels // head_count
    query_tokens = query_map.reshape(length, channels)
    windows = (
        tile_map.reshape(window_rows, win_side, window_cols, win_side, channels)
        .transpose(0, 2, 1, 3, 4)
        .reshape(window_count, length, channels)
    )
    flat_tokens = windows.astype(jnp.float32)
    centre = jnp.mean(flat_tokens, axis=-1, keepdims=True)
    spread = jnp.mean(jnp.square(flat_tokens - centre), axis=-1, keepdims=True)
    normed = ((flat_tokens - centre) * lax.rsqrt(spread + EPSILON) * norm_gain).astype(jnp.bfloat16)
    keyval = (
        jnp.dot(normed.reshape(-1, channels), kv_weight, preferred_element_type=jnp.float32)
        + kv_bias
    ).astype(jnp.bfloat16)
    keyval = keyval.reshape(window_count, length, 2, head_count, head_width)
    key_heads = keyval[:, :, 0].transpose(2, 0, 1, 3)
    value_heads = keyval[:, :, 1].transpose(2, 0, 1, 3)
    query_heads = query_tokens.reshape(length, head_count, head_width).transpose(1, 0, 2)
    score_scale = head_width ** (-0.5)

    def one_head(operands):
        query_head, key_head, value_head = operands
        scores = (
            jnp.einsum("qd,wkd->wqk", query_head, key_head, preferred_element_type=jnp.float32)
            * score_scale
        )
        weights = jax.nn.softmax(scores, axis=-1).astype(jnp.bfloat16)
        return jnp.einsum(
            "wqk,wkd->wqd", weights, value_head, preferred_element_type=jnp.float32
        ).astype(jnp.bfloat16)

    attended = lax.map(one_head, (query_heads, key_heads, value_heads))
    attended = attended.transpose(1, 2, 0, 3).reshape(-1, channels)
    output_rows = (
        flat_tokens.reshape(-1, channels)
        + jnp.dot(attended, proj_weight, preferred_element_type=jnp.float32)
        + proj_bias
    )
    output_rows = output_rows.astype(jnp.bfloat16)
    restored = (
        output_rows.reshape(window_rows, window_cols, win_side, win_side, channels)
        .transpose(0, 2, 1, 3, 4)
        .reshape(height, breadth, channels)
    )
    return restored[None]


def solution(mesh):
    in_specs = (P(("scene", "tile"), None, None, None), P(), P(), P(), P(), P(), P(), P(), P(), P())
    out_specs = P(("scene", "tile"), None, None, None)
    return jax.shard_map(body, mesh=mesh, in_specs=in_specs, out_specs=out_specs, check_vma=False)
```

profile of v0, /device:TPU:0, one launch (start us, length us, event | category | flops | bytes accessed | tf_op | source)
XLA Modules:
  0.0 713.5 jit_solution(16270690306401882168)
XLA Ops:
  7.6 5.9 collective-permute-start
  15.7 5.8 collective-permute-done.1
  33.7 24.0 %fusion.149 = (f32[768]{0:T(1024)S(1)}, f32[32,64,768]{2,1,0:T(8,128)}) fusion(f32[768]{0:T(1024)S(1)} %get-tuple-element.62, bf16[34,65,768]{2,1,0:T(8,128)(2,1)S(1)} %get-tuple-element.93, f32[768]{0:T(1024)S(1)} %get-tuple-element.63, bf16[1,64,768]{2,1,0:T(8,128)(2,1)S(1)} %broadcast_select_fusion.6, bf16[32,64,768]{2,1,0:T(8,128)(2,1)S(1)} %bitcast.172, ...), kind=kLoop, calls=%fused_computation.302 | loop fusion | flops 146275584 | bytes 28538880 | tf_op jit(solution)/shard_map/reduce_sum | solution.py:76
  57.7 65.9 %psum.21 = f32[768]{0:T(1024)S(1)} all-reduce(f32[768]{0:T(1024)S(1)} %get-tuple-element.84), channel_id=1, replica_groups=mesh['scene'=4,'tile'=32] {'tile'}, use_global_device_ids=true, to_apply=%region_1.2 | all-reduce | flops 768 | bytes 6144 | tf_op jit(solution)/shard_map/psum | solution.py:118
  126.3 6.7 fusion.32
  145.0 5.6 slice.348
  155.1 6.2 reduce_max.64
  162.8 9.6 %collective-permute-start.6 = (bf16[1,32,768]{2,1,0:T(8,128)(2,1)S(1)}, bf16[1,32,768]{2,1,0:T(8,128)(2,1)S(1)}, u32[]{:S(2)}, u32[]{:S(2)}) collective-permute-start(bf16[1,32,768]{2,1,0:T(8,128)(2,1)S(1)} %get-tuple-element.102), channel_id=1, source_target_pairs={{0,4},{1,5},{2,6},{3,7},{4,8},{5,9},{6,10},{7,11},{8,12},{9,13},{1... | collective-permute-start | bytes 147464 | tf_op jit(solution)/shard_map/ppermute | solution.py:16
  174.2 5.7 collective-permute-done.7
  186.0 6.5 fusion.147
  192.5 63.0 %psum.22 = f32[768]{0:T(1024)S(1)} all-reduce(f32[768]{0:T(1024)S(1)} %get-tuple-element.82), channel_id=1, replica_groups=mesh['scene'=4,'tile'=32] {'tile'}, use_global_device_ids=true, to_apply=%region_5.6 | all-reduce | flops 768 | bytes 6144 | tf_op jit(solution)/shard_map/psum | solution.py:118
  268.4 9.0 %collective-permute-start.12 = (bf16[1,16,768]{2,1,0:T(8,128)(2,1)S(1)}, bf16[1,16,768]{2,1,0:T(8,128)(2,1)S(1)}, u32[]{:S(2)}, u32[]{:S(2)}) collective-permute-start(bf16[1,16,768]{2,1,0:T(8,128)(2,1)S(1)} %get-tuple-element.108), channel_id=1, source_target_pairs={{0,4},{1,5},{2,6},{3,7},{4,8},{5,9},{6,10},{7,11},{8,12},{9,13},{1... | collective-permute-start | bytes 73736 | tf_op jit(solution)/shard_map/ppermute | solution.py:16
  277.4 5.4 bitcast_convert_fusion
  284.1 5.9 collective-permute-done.13
  296.7 63.0 %psum.23 = f32[768]{0:T(1024)S(1)} all-reduce(f32[768]{0:T(1024)S(1)} %get-tuple-element.80), channel_id=1, replica_groups=mesh['scene'=4,'tile'=32] {'tile'}, use_global_device_ids=true, to_apply=%region_9.10 | all-reduce | flops 768 | bytes 6144 | tf_op jit(solution)/shard_map/psum | solution.py:118
  382.3 6.9 add_convert_fusion
  389.2 8.6 %copy.28 = bf16[2048,1536]{0,1:T(8,128)(2,1)} copy(bf16[2048,1536]{1,0:T(8,128)(2,1)} %add_convert_fusion) | data formatting | bytes 12582912 | tf_op jit(solution)/shard_map/convert_element_type | solution.py:155
  397.9 11.1 %reshape.96 = bf16[2,1024,2,24,32]{1,0,4,3,2:T(2,128)(2,1)} reshape(bf16[2048,1536]{0,1:T(8,128)(2,1)} %copy.28) | data formatting | bytes 12582912 | tf_op jit(solution)/shard_map/reshape | solution.py:156
  409.0 8.5 %slice_bitcast_fusion = (bf16[24,2,1024,32]{2,1,3,0:T(2,128)(2,1)}, bf16[24,2,1024,32]{2,1,3,0:T(2,128)(2,1)}) fusion(bf16[2,1024,2,24,32]{1,0,4,3,2:T(2,128)(2,1)} %reshape.96), kind=kLoop, calls=%fused_computation.69 | loop fusion | bytes 12582912 | tf_op jit(solution)/shard_map/transpose | solution.py:158
  419.1 5.5 reshape_reshape_reshape.3
  424.6 6.4 copy.31
  431.0 261.4 %while.10 = (s32[]{:T(128)}, bf16[24,2,1024,32]{2,3,1,0:T(8,128)(2,1)}, bf16[24,2,1024,32]{2,1,3,0:T(2,128)(2,1)}, bf16[24,1024,32]{1,2,0:T(8,128)(2,1)S(1)}, bf16[24,2,1024,32]{2,1,3,0:T(2,128)(2,1)}, /*index=5*/s32[]{:T(128)}) while((s32[]{:T(128)}, bf16[24,2,1024,32]{2,3,1,0:T(8,128)(2,1)}, bf16[24,2,1024,32]{2,1,3,0:T(2,128)(2,1)}, ...), condition=%wide.region_17.18_spmd, body=%wide.region_14.17_spmd.sunk | while | flops 278987776 | bytes 17777228 | solution.py:173
  432.1 4.9 fusion.172
  443.0 4.9 fusion.172
  453.9 4.9 fusion.172
  464.8 4.9 fusion.172
  475.7 4.9 fusion.172
  486.5 4.9 fusion.172
  497.4 4.9 fusion.172
  508.3 4.9 fusion.172
  519.2 4.9 fusion.172
  692.3 5.1 copy.33
  (207 shorter events, 314.1 us)
Async XLA Ops:
  6.5 375.8 %copy-start = (bf16[768,1536]{1,0:T(8,128)(2,1)S(1)}, bf16[768,1536]{1,0:T(8,128)(2,1)}, u32[]{:S(2)}) copy-start(bf16[768,1536]{1,0:T(8,128)(2,1)} %param.18) | copy-start | bytes 7077892
  6.5 411.0 %all-gather.3.cloned.1.call-start = ((), (), s32[]{:S(2)}) async-start(), calls=%async_computation | async-start | bytes 1622016 | tf_op jit(solution)/shard_map/all_gather | solution.py:132
  7.6 8.1 %collective-permute-start = (bf16[1,64,768]{2,1,0:T(8,128)(2,1)S(1)}, bf16[1,64,768]{2,1,0:T(8,128)(2,1)S(1)}, u32[]{:S(2)}, u32[]{:S(2)}) collective-permute-start(bf16[1,64,768]{2,1,0:T(8,128)(2,1)S(1)} %get-tuple-element.96), channel_id=1, source_target_pairs={{0,4},{1,5},{2,6},{3,7},{4,8},{5,9},{6,10},{7,11},{8,12},{9,13},{1... | collective-permute-start | bytes 294920 | tf_op jit(solution)/shard_map/ppermute | solution.py:16
  13.5 8.0 %collective-permute-start.1 = (bf16[1,64,768]{2,1,0:T(8,128)(2,1)S(1)}, bf16[1,64,768]{2,1,0:T(8,128)(2,1)S(1)}, u32[]{:S(2)}, u32[]{:S(2)}) collective-permute-start(bf16[1,64,768]{2,1,0:T(8,128)(2,1)S(1)} %get-tuple-element.97), channel_id=1, source_target_pairs={{4,0},{5,1},{6,2},{7,3},{8,4},{9,5},{10,6},{11,7},{12,8},{13,9},{1... | collective-permute-start | bytes 294920 | tf_op jit(solution)/shard_map/ppermute | solution.py:16
  22.8 2.7 collective-permute-start.2
  24.2 4.5 collective-permute-start.3
  28.8 4.9 copy-start.2
  133.0 4.3 collective-permute-start.4
  137.4 2.2 collective-permute-start.5
  142.4 1.2 copy-start.4
  162.8 11.4 %collective-permute-start.6 = (bf16[1,32,768]{2,1,0:T(8,128)(2,1)S(1)}, bf16[1,32,768]{2,1,0:T(8,128)(2,1)S(1)}, u32[]{:S(2)}, u32[]{:S(2)}) collective-permute-start(bf16[1,32,768]{2,1,0:T(8,128)(2,1)S(1)} %get-tuple-element.102), channel_id=1, source_target_pairs={{0,4},{1,5},{2,6},{3,7},{4,8},{5,9},{6,10},{7,11},{8,12},{9,13},{1... | collective-permute-start | bytes 147464 | tf_op jit(solution)/shard_map/ppermute | solution.py:16
  172.5 7.5 %collective-permute-start.7 = (bf16[1,32,768]{2,1,0:T(8,128)(2,1)S(1)}, bf16[1,32,768]{2,1,0:T(8,128)(2,1)S(1)}, u32[]{:S(2)}, u32[]{:S(2)}) collective-permute-start(bf16[1,32,768]{2,1,0:T(8,128)(2,1)S(1)} %get-tuple-element.103), channel_id=1, source_target_pairs={{4,0},{5,1},{6,2},{7,3},{8,4},{9,5},{10,6},{11,7},{12,8},{13,9},{1... | collective-permute-start | bytes 147464 | tf_op jit(solution)/shard_map/ppermute | solution.py:16
  180.1 4.4 collective-permute-start.9
  181.5 3.9 collective-permute-start.8
  260.7 3.0 collective-permute-start.10
  263.8 2.2 collective-permute-start.11
  268.4 15.7 %collective-permute-start.12 = (bf16[1,16,768]{2,1,0:T(8,128)(2,1)S(1)}, bf16[1,16,768]{2,1,0:T(8,128)(2,1)S(1)}, u32[]{:S(2)}, u32[]{:S(2)}) collective-permute-start(bf16[1,16,768]{2,1,0:T(8,128)(2,1)S(1)} %get-tuple-element.108), channel_id=1, source_target_pairs={{0,4},{1,5},{2,6},{3,7},{4,8},{5,9},{6,10},{7,11},{8,12},{9,13},{1... | collective-permute-start | bytes 73736 | tf_op jit(solution)/shard_map/ppermute | solution.py:16
  282.8 7.2 %collective-permute-start.13 = (bf16[1,16,768]{2,1,0:T(8,128)(2,1)S(1)}, bf16[1,16,768]{2,1,0:T(8,128)(2,1)S(1)}, u32[]{:S(2)}, u32[]{:S(2)}) collective-permute-start(bf16[1,16,768]{2,1,0:T(8,128)(2,1)S(1)} %get-tuple-element.109), channel_id=1, source_target_pairs={{4,0},{5,1},{6,2},{7,3},{8,4},{9,5},{10,6},{11,7},{12,8},{13,9},{1... | collective-permute-start | bytes 73736 | tf_op jit(solution)/shard_map/ppermute | solution.py:16
  290.1 4.4 collective-permute-start.15
  291.5 3.9 collective-permute-start.14
  364.0 4.4 collective-permute-start.16
  368.5 2.3 collective-permute-start.17
  375.5 5.5 copy-start.5
  378.2 2.7 copy-start.3
  380.9 1.4 copy-start.7
  697.5 1.3 copy-start.6
  697.5 1.3 copy-start.8
  703.6 2.7 copy-start.1
Sparse Core Ops, SparseCore 0:
  372.1 44.2 all-gather.2
where the time goes:
time: 727 us; the launch traced here: 714 us
  matrix products  263 us (36%)
  blocking collectives  192 us (26%)
  local copies, waits for them, and re-layouts  99.3 us (14%)
  other arithmetic  66.5 us (9%)
  starting transfers between devices  47.9 us (7%)
  waiting for transfers between devices  29.5 us (4%)
  between operations  14.6 us (2%)
    psum x3, blocking collectives, scene_sum(): return lax.psum(partial_sum, 'tile')  192 us
    sub x24, matrix products, one_head(): weights = jax.nn.softmax(scores, axis=-1).astype(jnp.bfloat16)  117 us
    dot_general x24, matrix products, one_head(): jnp.einsum('wqk,wkd->wqd', weights, value_head, preferred_element_type=jn...  116 us
    ppermute x18, starting transfers between devices, shifted(): lax.ppermute(value, axis, [(source, source + steps) for source in range(i...  47.9 us
    reduce_sum x3, other arithmetic, level_step(): channel_mean = sum_rule(jnp.sum(response, axis=(0, 1))) / cell_count  31.6 us
    ppermute x18, waiting for transfers between devices, shifted(): lax.ppermute(value, axis, [(source, source + steps) for source in range(i...  29.5 us
    dynamic_slice x24, local copies, waits for them, and re-layouts, body(): attended = lax.map(one_head, (query_heads, key_heads, value_heads))  27.6 us
  transfers between devices with their start and end apart: 19, of which 13 were waited for; matrix products, arithmetic and copies ran while one was open for 7% of the time, Pallas kernels for 0%

commit v1 on v0

--- a/solution.py
+++ b/solution.py
@@ -1,13 +1,159 @@
 import jax
 import jax.numpy as jnp
 from jax import lax
+from jax.experimental import pallas as pl
+from jax.experimental.pallas import tpu as pltpu
 from jax.sharding import PartitionSpec as P
 
 HEADS = 24
 TILE_COLS = 4
-
-
 EPSILON = 1e-05
+BF = jnp.bfloat16
+F32 = jnp.float32
+VM = pl.BlockSpec(memory_space=pltpu.VMEM)
+LOG2E = 1.4426950408889634
+QB = 256
+KC = 512
+UNROLL = 8
+
+
+def kv_kernel(x_ref, gain_ref, w_ref, b_ref, kt_ref, vt_ref):
+    dim = x_ref.shape[-1]
+    tokens = x_ref.shape[0] * x_ref.shape[1]
+    x = x_ref[...].reshape(tokens, dim).astype(F32)
+    centre = jnp.mean(x, axis=1, keepdims=True)
+    moved = x - centre
+    spread = jnp.mean(jnp.square(moved), axis=1, keepdims=True)
+    normed = (moved * lax.rsqrt(spread + EPSILON) * gain_ref[...]).astype(BF)
+    keys = (jnp.dot(normed, w_ref[:, :dim], preferred_element_type=F32) + b_ref[:, :dim]).astype(BF)
+    for group in range(dim // 128):
+        kt_ref[group] = keys[:, 128 * group : 128 * group + 128]
+    vals = jnp.dot(normed, w_ref[:, dim:], preferred_element_type=F32) + b_ref[:, dim:]
+    vt_ref[...] = vals.T.astype(BF)
+
+
+def keys_values(tile_map, gain, weight, bias):
+    rows, cols, dim = tile_map.shape
+    win = rows
+    step = 8
+    tokens = step * win
+    windows = cols // win
+    per = rows // step
+    return pl.pallas_call(
+        kv_kernel,
+        grid=(windows, per),
+        in_specs=[
+            pl.BlockSpec((step, win, dim), lambda w, i: (i, w, 0)),
+            pl.BlockSpec((1, dim), lambda w, i: (0, 0)),
+            pl.BlockSpec((dim, 2 * dim), lambda w, i: (0, 0)),
+            pl.BlockSpec((1, 2 * dim), lambda w, i: (0, 0)),
+        ],
+        out_specs=[
+            pl.BlockSpec((dim // 128, tokens, 128), lambda w, i: (0, w * per + i, 0)),
+            pl.BlockSpec((dim, tokens), lambda w, i: (0, w * per + i)),
+        ],
+        out_shape=[
+            jax.ShapeDtypeStruct((dim // 128, rows * cols, 128), BF),
+            jax.ShapeDtypeStruct((dim, rows * cols), BF),
+        ],
+        compiler_params=pltpu.CompilerParams(vmem_limit_bytes=32 * 2**20),
+        cost_estimate=pl.CostEstimate(
+            flops=4 * rows * cols * dim * dim, bytes_accessed=12 * 2**20, transcendentals=0
+        ),
+        name="keys_values",
+    )(tile_map, gain.reshape(1, dim), weight, bias.reshape(1, 2 * dim))
+
+
+def attention_kernel(q_ref, kt_ref, vt_ref, x_ref, wp_ref, bp_ref, out_ref, qa, sb, mb, ot):
+    count, dim = q_ref.shape
+    length = kt_ref.shape[1] // 2
+    blocks = count // QB
+    units = HEADS * blocks
+    scale = (dim // HEADS) ** (-0.5) * LOG2E
+    lane = lax.broadcasted_iota(jnp.int32, (1, 128), 1)
+    for group in range(dim // 128):
+        q = q_ref[:, 128 * group : 128 * group + 128]
+        for part in range(4):
+            qa[4 * group + part] = jnp.where(lane // 32 == part, q, jnp.zeros_like(q))
+    ones = jnp.ones((16, KC), BF)
+
+    def score(unit, slot, start):
+        head = unit // blocks
+        rows = pl.ds(pl.multiple_of(unit % blocks * QB, QB), QB)
+        s = lax.dot_general(
+            kt_ref[head // 4, pl.ds(start, KC), :],
+            qa[head, rows, :],
+            (((1,), (1,)), ((), ())),
+            preferred_element_type=F32,
+        )
+        sb[slot, pl.ds(start, KC), :] = s
+        return jnp.max(s.reshape(KC // 8, 8, QB), axis=0)
+
+    def step(unit, slot, following):
+        if unit is not None:
+            head = unit // blocks
+            rows = pl.ds(pl.multiple_of(head * 32, 32), 32)
+            cols = pl.ds(pl.multiple_of(unit % blocks * QB, QB), QB)
+        for w in range(2):
+            top = total = None
+            if unit is not None:
+                peak = jnp.max(mb[slot, w], axis=0, keepdims=True)
+            for start in range(length * w, length * w + length, KC):
+                high = score(following, 1 - slot, start)
+                top = high if top is None else jnp.maximum(top, high)
+                if unit is not None:
+                    p = jnp.exp2((sb[slot, pl.ds(start, KC), :] - peak) * scale).astype(BF)
+                    v = jnp.concatenate([vt_ref[rows, pl.ds(start, KC)], ones], axis=0)
+                    o = jnp.dot(v, p, preferred_element_type=F32)
+                    total = o if total is None else total + o
+            mb[1 - slot, w] = top
+            if unit is not None:
+                ot[w, rows, cols] = (total[:32] / total[32:33]).astype(BF)
+
+    step(None, 1, 0)
+
+    def body(turn, _):
+        for j in range(UNROLL):
+            unit = UNROLL * turn + j
+            step(unit, j % 2, jnp.minimum(unit + 1, units - 1))
+        return 0
+
+    lax.fori_loop(0, units // UNROLL, body, 0)
+
+    win = out_ref.shape[1] // 2
+    lines = QB // win
+    for w in range(2):
+        for part in range(blocks):
+            o = ot[w, :, part * QB : part * QB + QB]
+            y = lax.dot_general(o, wp_ref[...], (((0,), (0,)), ((), ())), preferred_element_type=F32)
+            r = slice(part * lines, part * lines + lines)
+            x = x_ref[r, w * win : w * win + win, :].reshape(QB, dim).astype(F32)
+            y = x + y + bp_ref[...]
+            out_ref[r, w * win : w * win + win, :] = y.astype(BF).reshape(lines, win, dim)
+
+
+def attention(q, kt, vt, tile_map, wp, bp):
+    rows, cols, dim = tile_map.shape
+    count = q.shape[0]
+    return pl.pallas_call(
+        attention_kernel,
+        in_specs=[VM] * 6,
+        out_specs=VM,
+        out_shape=jax.ShapeDtypeStruct((count // 32, cols, dim), BF),
+        scratch_shapes=[
+            pltpu.VMEM((HEADS, count, 128), BF),
+            pltpu.VMEM((2, rows * cols, QB), F32),
+            pltpu.VMEM((2, 2, 8, QB), F32),
+            pltpu.VMEM((2, dim, count), BF),
+        ],
+        compiler_params=pltpu.CompilerParams(vmem_limit_bytes=56 * 2**20),
+        cost_estimate=pl.CostEstimate(
+            flops=8 * count * 1024 * dim,
+            bytes_accessed=16 * 2**20,
+            transcendentals=48 * count * 1024,
+        ),
+        name="attention",
+    )(q, kt, vt, tile_map, wp, bp.reshape(1, dim))
 
 
 def shifted(value, axis, steps):
@@ -115,7 +261,9 @@
         return strip_rims(inputs, grid_row, grid_col, grid_rows, fill_value, both_sides)
 
     def scene_sum(partial_sum):
-        return lax.psum(partial_sum, "tile")
+        count = lax.axis_size("tile")
+        copies = jnp.broadcast_to(partial_sum[None], (count,) + partial_sum.shape)
+        return jnp.sum(lax.all_to_all(copies, "tile", 0, 0, tiled=True), axis=0)
 
     coarse = tile_map
     for level_index in range(level_count):
@@ -131,59 +279,10 @@
         )
     collected = lax.all_gather(coarse[None], "tile", axis=0, tiled=True)
     query_map = assemble(collected, grid_rows)
-    height, breadth, channels = tile_map.shape
-    win_side = query_map.shape[0]
-    length = win_side * win_side
-    window_rows = height // win_side
-    window_cols = breadth // win_side
-    window_count = window_rows * window_cols
-    head_count = HEADS
-    head_width = channels // head_count
-    query_tokens = query_map.reshape(length, channels)
-    windows = (
-        tile_map.reshape(window_rows, win_side, window_cols, win_side, channels)
-        .transpose(0, 2, 1, 3, 4)
-        .reshape(window_count, length, channels)
-    )
-    flat_tokens = windows.astype(jnp.float32)
-    centre = jnp.mean(flat_tokens, axis=-1, keepdims=True)
-    spread = jnp.mean(jnp.square(flat_tokens - centre), axis=-1, keepdims=True)
-    normed = ((flat_tokens - centre) * lax.rsqrt(spread + EPSILON) * norm_gain).astype(jnp.bfloat16)
-    keyval = (
-        jnp.dot(normed.reshape(-1, channels), kv_weight, preferred_element_type=jnp.float32)
-        + kv_bias
-    ).astype(jnp.bfloat16)
-    keyval = keyval.reshape(window_count, length, 2, head_count, head_width)
-    key_heads = keyval[:, :, 0].transpose(2, 0, 1, 3)
-    value_heads = keyval[:, :, 1].transpose(2, 0, 1, 3)
-    query_heads = query_tokens.reshape(length, head_count, head_width).transpose(1, 0, 2)
-    score_scale = head_width ** (-0.5)
-
-    def one_head(operands):
-        query_head, key_head, value_head = operands
-        scores = (
-            jnp.einsum("qd,wkd->wqk", query_head, key_head, preferred_element_type=jnp.float32)
-            * score_scale
-        )
-        weights = jax.nn.softmax(scores, axis=-1).astype(jnp.bfloat16)
-        return jnp.einsum(
-            "wqk,wkd->wqd", weights, value_head, preferred_element_type=jnp.float32
-        ).astype(jnp.bfloat16)
-
-    attended = lax.map(one_head, (query_heads, key_heads, value_heads))
-    attended = attended.transpose(1, 2, 0, 3).reshape(-1, channels)
-    output_rows = (
-        flat_tokens.reshape(-1, channels)
-        + jnp.dot(attended, proj_weight, preferred_element_type=jnp.float32)
-        + proj_bias
-    )
-    output_rows = output_rows.astype(jnp.bfloat16)
-    restored = (
-        output_rows.reshape(window_rows, window_cols, win_side, win_side, channels)
-        .transpose(0, 2, 1, 3, 4)
-        .reshape(height, breadth, channels)
-    )
-    return restored[None]
+    channels = tile_map.shape[-1]
+    query_tokens = query_map.reshape(-1, channels)
+    kt, vt = keys_values(tile_map, norm_gain, kv_weight, kv_bias)
+    return attention(query_tokens, kt, vt, tile_map, proj_weight, proj_bias)[None]
 
 
 def solution(mesh):

time: 727 us -> 354 us (0.49); the launches traced: 714 us -> 352 us
  matrix products: 263 us -> 17.6 us
  blocking collectives: 192 us -> 51.4 us
  local copies, waits for them, and re-layouts: 99.3 us -> 28.9 us
  Pallas kernels: 0 us -> 64.4 us
  waiting for transfers between devices: 29.5 us -> 66.1 us
  other arithmetic: 66.5 us -> 54.9 us
    psum x3 -> x0, blocking collectives: 192 us -> none  [scene_sum(): return lax.psum(partial_sum, 'tile')]
    dot_general x26 -> x0, matrix products: 128 us -> none  [the longest x24 116 us: one_head(): jnp.einsum('wqk,wkd->wqd', weights, value_head, preferred_element_type=jn...]
    sub x24 -> x0, matrix products: 117 us -> none  [one_head(): weights = jax.nn.softmax(scores, axis=-1).astype(jnp.bfloat16)]
    pallas_call x0 -> x2, Pallas kernels: none -> 64.4 us  [the longest x1 54.7 us: attention(): pl.pallas_call(attention_kernel, in_specs=[VM] * 6, out_specs=VM, out_sha...]
    all_to_all x0 -> x3, blocking collectives: none -> 51.4 us  [scene_sum(): return jnp.sum(lax.all_to_all(copies, 'tile', 0, 0, tiled=True), axis=0)]
    all_gather x1, waiting for transfers between devices: 0.01 us -> 34.2 us  [body(): collected = lax.all_gather(coarse[None], 'tile', axis=0, tiled=True)]
    dynamic_slice x24 -> x0, local copies, waits for them, and re-layouts: 27.6 us -> none  [body(): attended = lax.map(one_head, (query_heads, key_heads, value_heads))]
    transpose x3 -> x0, local copies, waits for them, and re-layouts: 15.6 us -> none  [the longest x1 8.53 us: body(): value_heads = keyval[:, :, 1].transpose(2, 0, 1, 3)]
  transfers between devices with their start and end apart: 19 -> 19, of which waited for: 13 -> 15; matrix products, arithmetic and copies ran while one was open for 7% -> 1% of each run, Pallas kernels for 0% -> 3%
where the time goes in v1:
time: 354 us; the launch traced here: 352 us
  waiting for transfers between devices  66.1 us (19%)
  Pallas kernels  64.4 us (18%)
  other arithmetic  54.9 us (16%)
  starting transfers between devices  54.5 us (15%)
  blocking collectives  51.4 us (15%)
  local copies, waits for them, and re-layouts  28.9 us (8%)
  matrix products  17.6 us (5%)
  between operations  14 us (4%)
    pallas_call x1, Pallas kernels, attention(): pl.pallas_call(attention_kernel, in_specs=[VM] * 6, out_specs=VM, out_sha...  54.7 us
    ppermute x18, starting transfers between devices, shifted(): lax.ppermute(value, axis, [(source, source + steps) for source in range(i...  54.5 us
    all_to_all x3, blocking collectives, scene_sum(): return jnp.sum(lax.all_to_all(copies, 'tile', 0, 0, tiled=True), axis=0)  51.4 us
    all_gather x1, waiting for transfers between devices, body(): collected = lax.all_gather(coarse[None], 'tile', axis=0, tiled=True)  34.2 us
    reduce_sum x3, other arithmetic, level_step(): channel_mean = sum_rule(jnp.sum(response, axis=(0, 1))) / cell_count  32.4 us
    ppermute x18, waiting for transfers between devices, shifted(): lax.ppermute(value, axis, [(source, source + steps) for source in range(i...  32 us
    dot_general x3, matrix products, level_step(): jnp.dot(scaled.reshape(-1, channels), mix_matrix, preferred_element_type=...  10.2 us
    pallas_call x1, Pallas kernels, keys_values(): pl.pallas_call(kv_kernel, grid=(windows, per), in_specs=[pl.BlockSpec((st...  9.65 us
  transfers between devices with their start and end apart: 19, of which 15 were waited for; matrix products, arithmetic and copies ran while one was open for 1% of the time, Pallas kernels for 3%

profile of v1, /device:TPU:0, one launch (start us, length us, event | category | flops | bytes accessed | tf_op | source)
XLA Modules:
  0.0 351.8 jit_solution(67002684550793765)
XLA Ops:
  8.3 5.9 %collective-permute-start = (bf16[1,64,768]{2,1,0:T(8,128)(2,1)S(1)}, bf16[1,64,768]{2,1,0:T(8,128)(2,1)S(1)}, u32[]{:S(2)}, u32[]{:S(2)}) collective-permute-start(bf16[1,64,768]{2,1,0:T(8,128)(2,1)S(1)} %get-tuple-element.46), channel_id=1, source_target_pairs={{0,4},{1,5},{2,6},{3,7},{4,8},{5,9},{6,10},{7,11},{8,12},{9,13},{1... | collective-permute-start | bytes 294920 | tf_op jit(solution)/shard_map/ppermute | solution.py:162
  16.8 5.5 %collective-permute-done.1 = bf16[1,64,768]{2,1,0:T(8,128)(2,1)S(1)} collective-permute-done((bf16[1,64,768]{2,1,0:T(8,128)(2,1)}, bf16[1,64,768]{2,1,0:T(8,128)(2,1)S(1)}, u32[]{:S(2)}, u32[]{:S(2)}) %collective-permute-start.1) | collective-permute-done | bytes 98336 | tf_op jit(solution)/shard_map/ppermute | solution.py:162
  22.4 2.0 pad_maximum_fusion.11
  25.7 3.0 collective-permute-start.2
  30.1 2.1 maximum_maximum_fusion
  32.2 24.0 %fusion.115 = (f32[768]{0:T(1024)S(1)}, f32[32,64,768]{2,1,0:T(8,128)}) fusion(f32[768]{0:T(1024)S(1)} %get-tuple-element.28, bf16[34,65,768]{2,1,0:T(8,128)(2,1)S(1)} %get-tuple-element.43, f32[768]{0:T(1024)S(1)} %get-tuple-element.29, bf16[1,64,768]{2,1,0:T(8,128)(2,1)S(1)} %broadcast_select_fusion.6, bf16[32,64,768]{2,1,0:T(8,128)(2,1)S(1)} %bitcast.70, ...), kind=kLoop, calls=%fused_computation.260 | loop fusion | flops 146275584 | bytes 28538880 | tf_op jit(solution)/shard_map/reduce_sum | solution.py:222
  56.2 17.4 %all_to_all.18 = f32[32,1,768]{2,1,0:T(1,128)S(1)} all-to-all(f32[32,1,768]{2,1,0:T(1,128)S(1)} %broadcast_in_dim.28), channel_id=1, replica_groups=mesh['scene'=4,'tile'=32] {'tile'}, dimensions={0} | all-to-all | bytes 196608 | tf_op jit(solution)/shard_map/all_to_all | solution.py:266
  76.3 5.7 %fusion.5 = bf16[32,64,768]{2,1,0:T(8,128)(2,1)S(1)} fusion(f32[32,64,768]{2,1,0:T(8,128)} %get-tuple-element.41, f32[768]{0:T(1024)S(1)} %add_divide_fusion.2, bf16[3,768,768]{2,1,0:T(8,128)(2,1)} %param.14, bf16[1,32,64,768]{3,2,1,0:T(8,128)(2,1)S(1)} %copy-done), kind=kOutput, calls=%fused_computation.8 | convolution fusion | flops 2423783424 | bytes 13765632 | tf_op jit(solution)/shard_map/dot_general | solution.py:225
  82.0 2.9 collective-permute-start.4
  85.0 2.3 collective-permute-done.4
  89.8 1.9 maximum_maximum_fusion.1
  95.0 5.6 %slice.341 = bf16[16,32,768]{2,1,0:T(8,128)(2,1)} slice(bf16[16,65,768]{2,1,0:T(8,128)(2,1)} %copy-done.5), slice={[0:16:1], [2:65:2], [0:768:1]} | slice | bytes 1572864 | tf_op jit(solution)/shard_map/slice | solution.py:206
  100.6 4.5 %reshape.66 = bf16[16,32,2,768]{3,2,1,0:T(2,128)(2,1)} reshape(bf16[16,64,768]{2,1,0:T(8,128)(2,1)} %slice.421) | data formatting | bytes 3145728 | tf_op jit(solution)/shard_map/reshape | solution.py:205
  105.1 6.2 %reduce_max.55 = bf16[16,32,768]{2,1,0:T(8,128)(2,1)} reduce(bf16[16,32,2,768]{3,2,1,0:T(2,128)(2,1)} %reshape.66, bf16[]{:T(256)} %constant.47.clone.1), dimensions={2}, to_apply=%region_3.4 | reduce | flops 393216 | bytes 2359298 | tf_op jit(solution)/shard_map/reduce_max | solution.py:206
  112.9 9.6 %collective-permute-start.6 = (bf16[1,32,768]{2,1,0:T(8,128)(2,1)S(1)}, bf16[1,32,768]{2,1,0:T(8,128)(2,1)S(1)}, u32[]{:S(2)}, u32[]{:S(2)}) collective-permute-start(bf16[1,32,768]{2,1,0:T(8,128)(2,1)S(1)} %get-tuple-element.52), channel_id=1, source_target_pairs={{0,4},{1,5},{2,6},{3,7},{4,8},{5,9},{6,10},{7,11},{8,12},{9,13},{1... | collective-permute-start | bytes 147464 | tf_op jit(solution)/shard_map/ppermute | solution.py:162
  124.2 7.8 %collective-permute-done.7 = bf16[1,32,768]{2,1,0:T(8,128)(2,1)S(1)} collective-permute-done((bf16[1,32,768]{2,1,0:T(8,128)(2,1)S(1)}, bf16[1,32,768]{2,1,0:T(8,128)(2,1)S(1)}, u32[]{:S(2)}, u32[]{:S(2)}) %collective-permute-start.7) | collective-permute-done | bytes 49184 | tf_op jit(solution)/shard_map/ppermute | solution.py:162
  133.5 3.0 collective-permute-start.8
  138.1 6.5 %fusion.113 = (f32[768]{0:T(1024)S(1)}, f32[16,32,768]{2,1,0:T(8,128)}) fusion(f32[768]{0:T(1024)S(1)} %get-tuple-element.19, bf16[18,33,768]{2,1,0:T(8,128)(2,1)S(1)} %get-tuple-element.49, f32[768]{0:T(1024)S(1)} %get-tuple-element.20, bf16[1,32,768]{2,1,0:T(8,128)(2,1)S(1)} %broadcast_select_fusion.12, bf16[16,32,768]{2,1,0:T(8,128)(2,1)S(1)} %max.19, ...), kind=kLoop, calls=%fused_computation.259 | loop fusion | flops 36568320 | bytes 7206912 | tf_op jit(solution)/shard_map/reduce_sum | solution.py:222
  144.6 17.1 %all_to_all.19 = f32[32,1,768]{2,1,0:T(1,128)S(1)} all-to-all(f32[32,1,768]{2,1,0:T(1,128)S(1)} %broadcast_in_dim.29), channel_id=1, replica_groups=mesh['scene'=4,'tile'=32] {'tile'}, dimensions={0} | all-to-all | bytes 196608 | tf_op jit(solution)/shard_map/all_to_all | solution.py:266
  164.5 2.7 fusion.22
  167.2 2.9 collective-permute-start.10
  175.6 2.7 slice.372
  179.1 2.0 reduce_max.57
  182.0 9.0 %collective-permute-start.12 = (bf16[1,16,768]{2,1,0:T(8,128)(2,1)S(1)}, bf16[1,16,768]{2,1,0:T(8,128)(2,1)S(1)}, u32[]{:S(2)}, u32[]{:S(2)}) collective-permute-start(bf16[1,16,768]{2,1,0:T(8,128)(2,1)S(1)} %get-tuple-element.58), channel_id=1, source_target_pairs={{0,4},{1,5},{2,6},{3,7},{4,8},{5,9},{6,10},{7,11},{8,12},{9,13},{1... | collective-permute-start | bytes 73736 | tf_op jit(solution)/shard_map/ppermute | solution.py:162
  192.6 7.7 %collective-permute-done.13 = bf16[1,16,768]{2,1,0:T(8,128)(2,1)S(1)} collective-permute-done((bf16[1,16,768]{2,1,0:T(8,128)(2,1)S(1)}, bf16[1,16,768]{2,1,0:T(8,128)(2,1)S(1)}, u32[]{:S(2)}, u32[]{:S(2)}) %collective-permute-start.13) | collective-permute-done | bytes 24608 | tf_op jit(solution)/shard_map/ppermute | solution.py:162
  202.6 3.0 collective-permute-start.14
  208.7 16.9 %all_to_all.20 = f32[32,1,768]{2,1,0:T(1,128)S(1)} all-to-all(f32[32,1,768]{2,1,0:T(1,128)S(1)} %broadcast_in_dim.30), channel_id=1, replica_groups=mesh['scene'=4,'tile'=32] {'tile'}, dimensions={0} | all-to-all | bytes 196608 | tf_op jit(solution)/shard_map/all_to_all | solution.py:266
  230.0 2.9 collective-permute-start.16
  240.2 9.6 %keys_values.1 = (bf16[6,2048,128]{2,1,0:T(8,128)(2,1)S(1)}, bf16[768,2048]{1,0:T(8,128)(2,1)S(1)}) custom-call(bf16[32,64,768]{2,1,0:T(8,128)(2,1)S(1)} %bitcast.71, f32[1,768]{1,0:T(1,128)S(1)} %reshape.72.gain_ref, bf16[768,1536]{1,0:T(8,128)(2,1)S(1)} %copy-done.1, f32[1,1536]{1,0:T(1,128)S(1)} %reshape.73.b_ref), custom_call_target="tpu_custom_call" | custom-call | flops 4831838208 | bytes 12582912 | tf_op jit(solution)/shard_map/keys_values/pallas_call | solution.py:42
  253.2 34.2 %all-gather.3.cloned.1.call-done = bf16[128,8,768]{2,1,0:T(8,128)(2,1)} async-done(((bf16[4,8,768]{2,1,0:T(8,128)(2,1)}), bf16[128,8,768]{2,1,0:T(8,128)(2,1)}) %all-gather.3.cloned.1.call-update) | async-done | bytes 1572880 | tf_op jit(solution)/shard_map/all_gather | solution.py:280
  287.4 2.8 copy.17
  290.2 54.7 %attention.1 = bf16[32,64,768]{2,1,0:T(8,128)(2,1)} custom-call(bf16[1024,768]{1,0:T(8,128)(2,1)} %bitcast.73, bf16[6,2048,128]{2,1,0:T(8,128)(2,1)} %copy-done.2, bf16[768,2048]{1,0:T(8,128)(2,1)} %copy-done.3, bf16[32,64,768]{2,1,0:T(8,128)(2,1)} %bitcast.68, bf16[768,768]{1,0:T(8,128)(2,1)} %wp_ref.1, f32[1,768]{1,0:T(1,128)} %reshape.74.bp_ref), custom_call_target="tpu_custom_call" | custom-call | flops 6442450944 | bytes 16777216 | tf_op jit(solution)/shard_map/attention/pallas_call | solution.py:138
  (127 shorter events, 53.4 us)
Async XLA Ops:
  6.5 23.5 %copy-start = (bf16[1,32,64,768]{3,2,1,0:T(8,128)(2,1)S(1)}, bf16[1,32,64,768]{3,2,1,0:T(8,128)(2,1)}, u32[]{:S(2)}) copy-start(bf16[1,32,64,768]{3,2,1,0:T(8,128)(2,1)} %param.10) | copy-start | bytes 9437188
  6.5 280.8 %all-gather.3.cloned.1.call-start = ((), (), s32[]{:S(2)}) async-start(), calls=%async_computation.3 | async-start | bytes 1622016 | tf_op jit(solution)/shard_map/all_gather | solution.py:280
  8.3 8.5 %collective-permute-start = (bf16[1,64,768]{2,1,0:T(8,128)(2,1)S(1)}, bf16[1,64,768]{2,1,0:T(8,128)(2,1)S(1)}, u32[]{:S(2)}, u32[]{:S(2)}) collective-permute-start(bf16[1,64,768]{2,1,0:T(8,128)(2,1)S(1)} %get-tuple-element.46), channel_id=1, source_target_pairs={{0,4},{1,5},{2,6},{3,7},{4,8},{5,9},{6,10},{7,11},{8,12},{9,13},{1... | collective-permute-start | bytes 294920 | tf_op jit(solution)/shard_map/ppermute | solution.py:162
  14.1 8.2 %collective-permute-start.1 = (bf16[1,64,768]{2,1,0:T(8,128)(2,1)}, bf16[1,64,768]{2,1,0:T(8,128)(2,1)S(1)}, u32[]{:S(2)}, u32[]{:S(2)}) collective-permute-start(bf16[1,64,768]{2,1,0:T(8,128)(2,1)} %get-tuple-element.47), channel_id=1, source_target_pairs={{4,0},{5,1},{6,2},{7,3},{8,4},{9,5},{10,6},{11,7},{12,8},{13,9},{1... | collective-permute-start | bytes 294920 | tf_op jit(solution)/shard_map/ppermute | solution.py:162
  24.3 4.4 %collective-permute-start.3 = (bf16[34,1,768]{2,1,0:T(2,128)(2,1)}, bf16[34,1,768]{2,1,0:T(2,128)(2,1)S(1)}, u32[]{:S(2)}, u32[]{:S(2)}) collective-permute-start(bf16[34,1,768]{2,1,0:T(2,128)(2,1)} %get-tuple-element.45), channel_id=1, source_target_pairs={{1,0},{2,1},{3,2},{4,3},{5,4},{6,5},{7,6},{8,7},{9,8},{10,9},{11,1... | collective-permute-start | bytes 156680 | tf_op jit(solution)/shard_map/ppermute | solution.py:162
  25.7 4.2 %collective-permute-start.2 = (bf16[34,1,768]{2,1,0:T(2,128)(2,1)}, bf16[34,1,768]{2,1,0:T(2,128)(2,1)S(1)}, u32[]{:S(2)}, u32[]{:S(2)}) collective-permute-start(bf16[34,1,768]{2,1,0:T(2,128)(2,1)} %get-tuple-element.44), channel_id=1, source_target_pairs={{0,1},{1,2},{2,3},{3,4},{4,5},{5,6},{6,7},{7,8},{8,9},{9,10},{10,1... | collective-permute-start | bytes 156680 | tf_op jit(solution)/shard_map/ppermute | solution.py:162
  82.0 5.2 %collective-permute-start.4 = (bf16[1,64,768]{2,1,0:T(8,128)(2,1)S(1)}, bf16[1,64,768]{2,1,0:T(8,128)(2,1)S(1)}, u32[]{:S(2)}, u32[]{:S(2)}) collective-permute-start(bf16[1,64,768]{2,1,0:T(8,128)(2,1)S(1)} %slice.419), channel_id=1, source_target_pairs={{0,4},{1,5},{2,6},{3,7},{4,8},{5,9},{6,10},{7,11},{8,12},{9,13},{1... | collective-permute-start | bytes 294920 | tf_op jit(solution)/shard_map/ppermute | solution.py:162
  87.4 2.2 collective-permute-start.5
  92.5 1.2 copy-start.5
  112.8 31.7 %copy-start.4 = (bf16[16,32,768]{2,1,0:T(8,128)(2,1)}, bf16[16,32,768]{2,1,0:T(8,128)(2,1)S(1)}, u32[]{:S(2)}) copy-start(bf16[16,32,768]{2,1,0:T(8,128)(2,1)S(1)} %max.19) | copy-start | bytes 2359300
  112.9 11.4 %collective-permute-start.6 = (bf16[1,32,768]{2,1,0:T(8,128)(2,1)S(1)}, bf16[1,32,768]{2,1,0:T(8,128)(2,1)S(1)}, u32[]{:S(2)}, u32[]{:S(2)}) collective-permute-start(bf16[1,32,768]{2,1,0:T(8,128)(2,1)S(1)} %get-tuple-element.52), channel_id=1, source_target_pairs={{0,4},{1,5},{2,6},{3,7},{4,8},{5,9},{6,10},{7,11},{8,12},{9,13},{1... | collective-permute-start | bytes 147464 | tf_op jit(solution)/shard_map/ppermute | solution.py:162
  122.5 9.5 %collective-permute-start.7 = (bf16[1,32,768]{2,1,0:T(8,128)(2,1)S(1)}, bf16[1,32,768]{2,1,0:T(8,128)(2,1)S(1)}, u32[]{:S(2)}, u32[]{:S(2)}) collective-permute-start(bf16[1,32,768]{2,1,0:T(8,128)(2,1)S(1)} %get-tuple-element.53), channel_id=1, source_target_pairs={{4,0},{5,1},{6,2},{7,3},{8,4},{9,5},{10,6},{11,7},{12,8},{13,9},{1... | collective-permute-start | bytes 147464 | tf_op jit(solution)/shard_map/ppermute | solution.py:162
  132.1 4.4 %collective-permute-start.9 = (bf16[18,1,768]{2,1,0:T(2,128)(2,1)S(1)}, bf16[18,1,768]{2,1,0:T(2,128)(2,1)S(1)}, u32[]{:S(2)}, u32[]{:S(2)}) collective-permute-start(bf16[18,1,768]{2,1,0:T(2,128)(2,1)S(1)} %get-tuple-element.51), channel_id=1, source_target_pairs={{1,0},{2,1},{3,2},{4,3},{5,4},{6,5},{7,6},{8,7},{9,8},{10,9},{11,1... | collective-permute-start | bytes 82952 | tf_op jit(solution)/shard_map/ppermute | solution.py:162
  133.5 3.9 %collective-permute-start.8 = (bf16[18,1,768]{2,1,0:T(2,128)(2,1)S(1)}, bf16[18,1,768]{2,1,0:T(2,128)(2,1)S(1)}, u32[]{:S(2)}, u32[]{:S(2)}) collective-permute-start(bf16[18,1,768]{2,1,0:T(2,128)(2,1)S(1)} %get-tuple-element.50), channel_id=1, source_target_pairs={{0,1},{1,2},{2,3},{3,4},{4,5},{5,6},{6,7},{7,8},{8,9},{9,10},{10,1... | collective-permute-start | bytes 82952 | tf_op jit(solution)/shard_map/ppermute | solution.py:162
  167.2 4.7 %collective-permute-start.10 = (bf16[1,32,768]{2,1,0:T(8,128)(2,1)S(1)}, bf16[1,32,768]{2,1,0:T(8,128)(2,1)S(1)}, u32[]{:S(2)}, u32[]{:S(2)}) collective-permute-start(bf16[1,32,768]{2,1,0:T(8,128)(2,1)S(1)} %slice.439), channel_id=1, source_target_pairs={{0,4},{1,5},{2,6},{3,7},{4,8},{5,9},{6,10},{7,11},{8,12},{9,13},{1... | collective-permute-start | bytes 147464 | tf_op jit(solution)/shard_map/ppermute | solution.py:162
  172.0 2.2 collective-permute-start.11
  174.7 0.8 copy-start.6
  182.0 10.5 %collective-permute-start.12 = (bf16[1,16,768]{2,1,0:T(8,128)(2,1)S(1)}, bf16[1,16,768]{2,1,0:T(8,128)(2,1)S(1)}, u32[]{:S(2)}, u32[]{:S(2)}) collective-permute-start(bf16[1,16,768]{2,1,0:T(8,128)(2,1)S(1)} %get-tuple-element.58), channel_id=1, source_target_pairs={{0,4},{1,5},{2,6},{3,7},{4,8},{5,9},{6,10},{7,11},{8,12},{9,13},{1... | collective-permute-start | bytes 73736 | tf_op jit(solution)/shard_map/ppermute | solution.py:162
  191.1 9.2 %collective-permute-start.13 = (bf16[1,16,768]{2,1,0:T(8,128)(2,1)S(1)}, bf16[1,16,768]{2,1,0:T(8,128)(2,1)S(1)}, u32[]{:S(2)}, u32[]{:S(2)}) collective-permute-start(bf16[1,16,768]{2,1,0:T(8,128)(2,1)S(1)} %get-tuple-element.59), channel_id=1, source_target_pairs={{4,0},{5,1},{6,2},{7,3},{8,4},{9,5},{10,6},{11,7},{12,8},{13,9},{1... | collective-permute-start | bytes 73736 | tf_op jit(solution)/shard_map/ppermute | solution.py:162
  200.4 5.3 %collective-permute-start.15 = (bf16[10,1,768]{2,1,0:T(2,128)(2,1)S(1)}, bf16[10,1,768]{2,1,0:T(2,128)(2,1)S(1)}, u32[]{:S(2)}, u32[]{:S(2)}) collective-permute-start(bf16[10,1,768]{2,1,0:T(2,128)(2,1)S(1)} %get-tuple-element.57), channel_id=1, source_target_pairs={{1,0},{2,1},{3,2},{4,3},{5,4},{6,5},{7,6},{8,7},{9,8},{10,9},{11,1... | collective-permute-start | bytes 46088 | tf_op jit(solution)/shard_map/ppermute | solution.py:162
  202.6 3.9 %collective-permute-start.14 = (bf16[10,1,768]{2,1,0:T(2,128)(2,1)S(1)}, bf16[10,1,768]{2,1,0:T(2,128)(2,1)S(1)}, u32[]{:S(2)}, u32[]{:S(2)}) collective-permute-start(bf16[10,1,768]{2,1,0:T(2,128)(2,1)S(1)} %get-tuple-element.56), channel_id=1, source_target_pairs={{0,1},{1,2},{2,3},{3,4},{4,5},{5,6},{6,7},{7,8},{8,9},{9,10},{10,1... | collective-permute-start | bytes 46088 | tf_op jit(solution)/shard_map/ppermute | solution.py:162
  208.6 29.3 %copy-start.7 = (f32[1536]{0:T(1024)S(1)}, f32[1536]{0:T(1024)}, u32[]{:S(2)}) copy-start(f32[1536]{0:T(1024)} %param.17) | copy-start | bytes 18436
  208.6 29.3 %copy-start.8 = (f32[768]{0:T(1024)S(1)}, f32[768]{0:T(1024)}, u32[]{:S(2)}) copy-start(f32[768]{0:T(1024)} %param.15) | copy-start | bytes 9220
  208.6 29.3 %copy-start.9 = (f32[768]{0:T(1024)S(1)}, f32[768]{0:T(1024)}, u32[]{:S(2)}) copy-start(f32[768]{0:T(1024)} %param.19) | copy-start | bytes 9220
  230.0 4.4 %collective-permute-start.16 = (bf16[1,16,768]{2,1,0:T(8,128)(2,1)S(1)}, bf16[1,16,768]{2,1,0:T(8,128)(2,1)S(1)}, u32[]{:S(2)}, u32[]{:S(2)}) collective-permute-start(bf16[1,16,768]{2,1,0:T(8,128)(2,1)S(1)} %slice.459), channel_id=1, source_target_pairs={{0,4},{1,5},{2,6},{3,7},{4,8},{5,9},{6,10},{7,11},{8,12},{9,13},{1... | collective-permute-start | bytes 73736 | tf_op jit(solution)/shard_map/ppermute | solution.py:162
  234.5 2.1 collective-permute-start.17
  238.5 1.7 copy-start.1
  249.9 1.7 copy-start.2
  251.5 1.7 copy-start.3
Sparse Core Ops, SparseCore 0:
  238.0 49.3 all-gather.2

commit v2 on v1

v2 whole, which is shorter than its diff:
```python
import functools

import jax
import jax.numpy as jnp
from jax import lax
from jax.experimental import pallas as pl
from jax.experimental.pallas import tpu as pltpu
from jax.sharding import PartitionSpec as P

HEADS = 24
TILE_COLS = 4
EPSILON = 1e-05
BF = jnp.bfloat16
F32 = jnp.float32
VM = pl.BlockSpec(memory_space=pltpu.VMEM)
LOG2E = 1.4426950408889634
QB = 256
KC = 512
UNROLL = 8


def kv_kernel(x_ref, gain_ref, w_ref, b_ref, kt_ref, vt_ref):
    dim = x_ref.shape[-1]
    tokens = x_ref.shape[0] * x_ref.shape[1]
    x = x_ref[...].reshape(tokens, dim).astype(F32)
    centre = jnp.mean(x, axis=1, keepdims=True)
    moved = x - centre
    spread = jnp.mean(jnp.square(moved), axis=1, keepdims=True)
    normed = (moved * lax.rsqrt(spread + EPSILON) * gain_ref[...]).astype(BF)
    keys = (jnp.dot(normed, w_ref[:, :dim], preferred_element_type=F32) + b_ref[:, :dim]).astype(BF)
    for group in range(dim // 128):
        kt_ref[group] = keys[:, 128 * group : 128 * group + 128]
    vals = jnp.dot(normed, w_ref[:, dim:], preferred_element_type=F32) + b_ref[:, dim:]
    vt_ref[...] = vals.T.astype(BF)


def keys_values(tile_map, gain, weight, bias, window):
    win, _, dim = tile_map.shape
    step = 8
    tokens = step * win
    return pl.pallas_call(
        kv_kernel,
        grid=(win // step,),
        in_specs=[
            pl.BlockSpec((step, win, dim), lambda i: (i, window, 0)),
            pl.BlockSpec((1, dim), lambda i: (0, 0)),
            pl.BlockSpec((dim, 2 * dim), lambda i: (0, 0)),
            pl.BlockSpec((1, 2 * dim), lambda i: (0, 0)),
        ],
        out_specs=[
            pl.BlockSpec((dim // 128, tokens, 128), lambda i: (0, i, 0)),
            pl.BlockSpec((dim, tokens), lambda i: (0, i)),
        ],
        out_shape=[
            jax.ShapeDtypeStruct((dim // 128, win * win, 128), BF),
            jax.ShapeDtypeStruct((dim, win * win), BF),
        ],
        compiler_params=pltpu.CompilerParams(vmem_limit_bytes=24 * 2**20),
        cost_estimate=pl.CostEstimate(
            flops=8 * win * win * dim * dim, bytes_accessed=8 * 2**20, transcendentals=0
        ),
        name="keys_values",
    )(tile_map, gain, weight, bias)


def attention_kernel(slabs, slab_ref, *refs):
    q_refs = refs[:slabs]
    kt_refs, vt_refs = refs[slabs : slabs + 2], refs[slabs + 2 : slabs + 4]
    x_ref, wp_ref, bp_ref = refs[slabs + 4 : slabs + 7]
    out_ref, qa, sb, mb, ot, stage, sems = refs[-7:]
    dim = x_ref.shape[2]
    length = kt_refs[0].shape[1]
    units = HEADS * slabs
    scale = (dim // HEADS) ** (-0.5) * LOG2E
    lane = lax.broadcasted_iota(jnp.int32, (1, 128), 1)
    for slab in range(slabs):
        for group in range(dim // 128):
            q = q_refs[slab][:, 128 * group : 128 * group + 128]
            for part in range(4):
                qa[slab, 4 * group + part] = jnp.where(lane // 32 == part, q, jnp.zeros_like(q))
    ones = jnp.ones((16, KC), BF)

    def score(unit, slot, w, start):
        head = unit // slabs
        s = lax.dot_general(
            kt_refs[w][head // 4, pl.ds(start, KC), :],
            qa[unit % slabs, head],
            (((1,), (1,)), ((), ())),
            preferred_element_type=F32,
        )
        sb[slot, w, pl.ds(start, KC), :] = s
        return jnp.max(s.reshape(KC // 8, 8, QB), axis=0)

    def step(unit, slot, following):
        if unit is not None:
            head = unit // slabs
            rows = pl.ds(pl.multiple_of(head * 32, 32), 32)
        for w in range(2):
            top = total = None
            if unit is not None:
                peak = jnp.max(mb[slot, w], axis=0, keepdims=True)
            for start in range(0, length, KC):
                high = score(following, 1 - slot, w, start)
                top = high if top is None else jnp.maximum(top, high)
                if unit is not None:
                    p = jnp.exp2((sb[slot, w, pl.ds(start, KC), :] - peak) * scale).astype(BF)
                    v = jnp.concatenate([vt_refs[w][rows, pl.ds(start, KC)], ones], axis=0)
                    o = jnp.dot(v, p, preferred_element_type=F32)
                    total = o if total is None else total + o
            mb[1 - slot, w] = top
            if unit is not None:
                ot[unit % slabs, w, rows, :] = (total[:32] / total[32:33]).astype(BF)

    step(None, 1, 0)

    def body(turn, _):
        for j in range(UNROLL):
            unit = UNROLL * turn + j
            step(unit, j % 2, jnp.minimum(unit + 1, units - 1))
        return 0

    lax.fori_loop(0, units // UNROLL, body, 0)

    win = x_ref.shape[1] // 2
    lines = QB // win
    copies = []
    for slab in range(slabs):
        place = pl.ds(pl.multiple_of(slab_ref[slab] * lines, lines), lines)
        for w in range(2):
            cols = slice(w * win, w * win + win)
            y = lax.dot_general(
                ot[slab, w], wp_ref[...], (((0,), (0,)), ((), ())), preferred_element_type=F32
            )
            y = y.reshape(2, 4, lines // 2, win // 4, dim).transpose(0, 2, 1, 3, 4).reshape(lines, win, dim)
            y = x_ref[place, cols, :].astype(F32) + y + bp_ref[...]
            stage[slab, :, cols, :] = y.astype(BF)
        copy = pltpu.make_async_copy(stage.at[slab], out_ref.at[place], sems.at[slab])
        copy.start()
        copies.append(copy)
    for copy in copies:
        copy.wait()


def attention(place, queries, keys, values, tile_map, wp, bp, started=None):
    rows, cols, dim = tile_map.shape
    slabs = len(queries)
    lines = QB * 2 // cols
    more = [] if started is None else [started]
    anywhere = pl.BlockSpec(memory_space=pl.ANY)
    return pl.pallas_call(
        functools.partial(attention_kernel, slabs),
        in_specs=[pl.BlockSpec(memory_space=pltpu.SMEM)] + [VM] * (slabs + 7) + [anywhere] * len(more),
        out_specs=anywhere,
        out_shape=jax.ShapeDtypeStruct(tile_map.shape, BF),
        input_output_aliases={slabs + 8: 0} if more else {},
        scratch_shapes=[
            pltpu.VMEM((slabs, HEADS, QB, 128), BF),
            pltpu.VMEM((2, 2, rows * cols // 2, QB), F32),
            pltpu.VMEM((2, 2, 8, QB), F32),
            pltpu.VMEM((slabs, 2, dim, QB), BF),
            pltpu.VMEM((slabs, lines, cols, dim), BF),
            pltpu.SemaphoreType.DMA((slabs,)),
        ],
        compiler_params=pltpu.CompilerParams(vmem_limit_bytes=40 * 2**20),
        cost_estimate=pl.CostEstimate(
            flops=8 * slabs * QB * 1024 * dim * 8,
            bytes_accessed=12 * 2**20,
            transcendentals=48 * slabs * QB * 1024,
        ),
        name="attention",
    )(place, *queries, *keys, *values, tile_map, wp, bp, *more)


def whole(array):
    return pl.BlockSpec(array.shape, lambda *i: (0,) * len(array.shape), pipeline_mode=pl.Buffered(1))


def wholes(*arrays):
    return [whole(array) for array in arrays]


def at_level(array, level):
    shape = (None,) + array.shape[1:]
    return pl.BlockSpec(shape, lambda *i: (level,) + (0,) * (len(shape) - 1), pipeline_mode=pl.Buffered(1))


POSITION = pl.BlockSpec(memory_space=pltpu.SMEM)


def params(mib):
    return pltpu.CompilerParams(vmem_limit_bytes=mib * 2**20)


def cost(flops, size):
    return pl.CostEstimate(flops=flops, bytes_accessed=size, transcendentals=0)


def round_up(count, unit):
    return -(-count // unit) * unit


def side_pieces_kernel(before, after, left_ref, right_ref, to_right, to_left, keep_r, keep_l):
    high = left_ref.shape[0]
    span = right_ref.shape[1]
    for r in range(high):
        keep_r[r * before : r * before + before, :] = right_ref[r].astype(F32)[span - before :]
        keep_l[r * after : r * after + after, :] = left_ref[r].astype(F32)[:after]
    to_right[...] = keep_r[...].astype(BF)
    to_left[...] = keep_l[...].astype(BF)


def side_pieces(tile, before, after):
    high, wide, dim = tile.shape
    return pl.pallas_call(
        functools.partial(side_pieces_kernel, before, after),
        grid=(1,),
        in_specs=[
            pl.BlockSpec((high, 16, dim), lambda i: (0, 0, 0)),
            pl.BlockSpec((high, 16, dim), lambda i: (0, wide // 16 - 1, 0)),
        ],
        out_shape=[
            jax.ShapeDtypeStruct((high * before, dim), BF),
            jax.ShapeDtypeStruct((high * after, dim), BF),
        ],
        scratch_shapes=[pltpu.VMEM((high * before, dim), F32), pltpu.VMEM((high * after, dim), F32)],
        compiler_params=params(16),
        cost_estimate=cost(0, 2 * 2**20),
        name="side_pieces",
    )(tile, tile)


def line_pieces_kernel(before, after, high, top_ref, low_ref, left_ref, right_ref, to_low, to_up, keep_d, keep_u, side_l, side_r):
    wide = top_ref.shape[1]
    full = before + wide + after
    side_l[...] = left_ref[...].astype(F32)
    side_r[...] = right_ref[...].astype(F32)
    keep_d[...] = jnp.zeros_like(keep_d)
    keep_u[...] = jnp.zeros_like(keep_u)

    def fill(keep, line, r, values):
        base = line * full
        keep[base : base + before, :] = side_l[r * before : r * before + before, :]
        keep[base + before : base + before + wide, :] = values
        keep[base + before + wide : base + full, :] = side_r[r * after : r * after + after, :]

    for line in range(before):
        fill(keep_d, line, high - before + line, low_ref[line].astype(F32))
    for line in range(after):
        fill(keep_u, line, line, top_ref[line].astype(F32))
    to_low[...] = keep_d[...].astype(BF)
    to_up[...] = keep_u[...].astype(BF)


def line_pieces(tile, left, right, before, after):
    high, wide, dim = tile.shape
    full = before + wide + after
    down = round_up(before * full, 16)
    up = round_up(after * full, 16)
    low_size = before if high % before == 0 else 8
    assert high % low_size == 0
    return pl.pallas_call(
        functools.partial(line_low_kernel, low_size, before, after, high),
        grid=(1,),
        in_specs=[
            pl.BlockSpec((after if high % after == 0 else 8, wide, dim), lambda i: (0, 0, 0)),
            pl.BlockSpec((low_size, wide, dim), lambda i: (high // low_size - 1, 0, 0)),
            whole(left),
            whole(right),
        ],
        out_shape=[jax.ShapeDtypeStruct((down, dim), BF), jax.ShapeDtypeStruct((up, dim), BF)],
        scratch_shapes=[
            pltpu.VMEM((down, dim), F32),
            pltpu.VMEM((up, dim), F32),
            pltpu.VMEM(left.shape, F32),
            pltpu.VMEM(right.shape, F32),
        ],
        compiler_params=params(16),
        cost_estimate=cost(0, 2**20),
        name="line_pieces",
    )(tile, tile, left, right)


def line_low_kernel(low_size, before, after, high, top_ref, low_ref, *rest):
    line_pieces_kernel(before, after, high, top_ref, low_ref.at[pl.ds(low_size - before, before)], *rest)


def moved_by(value, rows, cols):
    count = lax.axis_size("tile")
    pairs = []
    for t in range(count):
        r, c = t // TILE_COLS + rows, t % TILE_COLS + cols
        if 0 <= r < count // TILE_COLS and 0 <= c < TILE_COLS:
            pairs.append((t, r * TILE_COLS + c))
    return lax.ppermute(value, "tile", pairs)


def after_these(value, *others):
    return lax.optimization_barrier((value,) + others)[0]


def exchange_rims(tile, pieces, before, after, beside):
    left = moved_by(pieces[0], 0, 1)
    right = moved_by(pieces[1], 0, -1)
    down, up = line_pieces(tile, left, right, before, after)
    above, below = moved_by(down, 1, 0), moved_by(up, -1, 0)
    result = beside(down)
    above, below, *result = lax.optimization_barrier((above, below, *result))
    return (left, right, above, below), result


def erf_gelu(y):
    return 0.5 * y * (1.0 + lax.erf(y * 0.7071067811865476))


def fill_padded(x_ref, rims, before, after, padded, stage):
    high, wide, _ = x_ref.shape
    full = before + wide + after
    left, right, above, below = rims

    def line(r, _):
        padded[r + before, before : before + wide, :] = x_ref[r].astype(F32)
        return 0

    lax.fori_loop(0, high, line, 0)
    stage[: left.shape[0], :] = left[...].astype(F32)
    for r in range(high):
        padded[r + before, 0:before, :] = stage[r * before : r * before + before, :]
    stage[: right.shape[0], :] = right[...].astype(F32)
    for r in range(high):
        padded[r + before, before + wide : full, :] = stage[r * after : r * after + after, :]
    stage[: above.shape[0], :] = above[...].astype(F32)
    for r in range(before):
        padded[r, 0:full, :] = stage[r * full : r * full + full, :]
    stage[: below.shape[0], :] = below[...].astype(F32)
    for r in range(after):
        padded[before + high + r, 0:full, :] = stage[r * full : r * full + full, :]


def conv_gelu(padded, kernel_ref, g_ref, own_rows, own_cols, part_ref):
    rows, cols, dim = g_ref.shape
    column = lax.broadcasted_iota(jnp.int32, (cols, 128), 0)
    mine = (column >= own_cols[0]) & (column < own_cols[1])
    for group in range(dim // 128):
        lanes = slice(128 * group, 128 * group + 128)
        taps = [[kernel_ref[a, b : b + 1, lanes].astype(F32) for b in range(3)] for a in range(3)]

        def line(r, total):
            y = None
            for a in range(3):
                for b in range(3):
                    term = padded[r + a, b : b + cols, lanes] * taps[a][b]
                    y = term if y is None else y + term
            g = erf_gelu(y)
            g_ref[r, :, lanes] = g
            counted = jnp.sum(jnp.where(mine, g, 0.0).reshape(cols // 8, 8, 128), axis=0)
            return total + jnp.where((r >= own_rows[0]) & (r < own_rows[1]), counted, 0.0)

        total = lax.fori_loop(0, rows, line, jnp.zeros((8, 128), F32))
        total = jnp.sum(total, axis=0, keepdims=True)
        part_ref[:, group, :] += jnp.broadcast_to(total, (part_ref.shape[0], 128))


def copy_centre(padded, rest_ref):
    rows, cols, _ = rest_ref.shape

    def line(r, _):
        rest_ref[r] = padded[r + 1, 1 : 1 + cols, :].astype(BF)
        return 0

    lax.fori_loop(0, rows, line, 0)


def thirds(row):
    high = row.astype(BF).astype(F32)
    mid = (row - high).astype(BF).astype(F32)
    low = row - high - mid
    index = lax.broadcasted_iota(jnp.int32, (16, row.shape[1]), 0)
    block = jnp.where(index == 0, high, jnp.where(index == 1, mid, jnp.where(index == 2, low, 0.0)))
    return block.astype(BF)


def gate_row(sums_ref, cells, reduce_ref, expand_ref):
    total = jnp.sum(sums_ref[...], axis=0)
    groups = reduce_ref.shape[0] // 128
    mean = jnp.concatenate([total[group : group + 1] for group in range(groups)], axis=1) / cells
    inner = jnp.sum(jnp.dot(thirds(mean), reduce_ref[...], preferred_element_type=F32), axis=0, keepdims=True)
    inner = erf_gelu(inner)
    outer = jnp.sum(jnp.dot(thirds(inner), expand_ref[...], preferred_element_type=F32), axis=0, keepdims=True)
    return 1.0 / (1.0 + jnp.exp(-outer))


def mix_lines(g_ref, gate, mix_ref, rest_ref, z_ref, first, bounds):
    rows, cols, dim = g_ref.shape
    row_low, row_high, col_low, col_high = bounds
    column = lax.broadcasted_iota(jnp.int32, (cols, 1), 0)
    inside = (column >= col_low) & (column < col_high)
    u = (g_ref[...] * gate).astype(BF).reshape(rows * cols, dim)
    product = jnp.dot(u, mix_ref[...], preferred_element_type=F32).reshape(rows, cols, dim)
    for k in range(rows):
        z = (rest_ref[k].astype(F32) + product[k]).astype(BF).astype(F32)
        keep = inside & (first + k >= row_low) & (first + k < row_high)
        z_ref[first + k] = jnp.where(keep, z, -jnp.inf)


def pooled_line(z_ref, line_ref, i, count):
    most = jnp.maximum(jnp.maximum(z_ref[2 * i], z_ref[2 * i + 1]), z_ref[2 * i + 2])
    groups = []
    for group in range(line_ref.shape[0]):
        line_ref[group] = most[:, 128 * group : 128 * group + 128]
        parts = [line_ref[group, pl.ds(s, count, stride=2), :] for s in range(3)]
        groups.append(jnp.maximum(jnp.maximum(parts[0], parts[1]), parts[2]))
    return jnp.concatenate(groups, axis=1)


def act_kernel(before, after, x_ref, l_ref, r_ref, a_ref, b_ref, kernel_ref, g_ref, rest_ref, part_ref, padded, stage):
    high, wide, _ = x_ref.shape
    step = g_ref.shape[0]
    turn = pl.program_id(0)

    @pl.when(turn == 0)
    def _():
        fill_padded(x_ref, (l_ref, r_ref, a_ref, b_ref), before, after, padded, stage)
        part_ref[...] = jnp.zeros_like(part_ref)

    own = before - 1
    block = padded.at[pl.ds(turn * step, step + 2)]
    copy_centre(block, rest_ref)
    conv_gelu(block, kernel_ref, g_ref, (own - turn * step, own + high - turn * step), (own, own + wide), part_ref)


def activate(tile, rims, kernels, level, before, after, step):
    high, wide, dim = tile.shape
    rows, cols = high + before + after - 2, round_up(wide + before + after - 2, 8)
    stage = max(r.shape[0] for r in rims)
    copies = lax.axis_size("tile")
    block = pl.BlockSpec((step, cols, dim), lambda i: (i, 0, 0))
    return pl.pallas_call(
        functools.partial(act_kernel, before, after),
        grid=(rows // step,),
        in_specs=wholes(tile, *rims) + [at_level(kernels, level)],
        out_specs=[block, block, pl.BlockSpec((copies, 8, 128), lambda i: (0, 0, 0))],
        out_shape=[
            jax.ShapeDtypeStruct((rows, cols, dim), F32),
            jax.ShapeDtypeStruct((rows, cols, dim), BF),
            jax.ShapeDtypeStruct((copies, 8, 128), F32),
        ],
        scratch_shapes=[
            pltpu.VMEM((rows + 2, round_up(cols + 2, 8), dim), F32),
            pltpu.VMEM((stage, dim), F32),
        ],
        compiler_params=params(28),
        cost_estimate=cost(400 * rows * cols * dim, 6 * rows * cols * dim),
        name="activate",
    )(tile, *rims, kernels)


def mix0_kernel(cells, before, after, pos, sums, red, exp, mix, g_ref, rest, x_out, to_right, to_left, gates, z, line, keep_r, keep_l):
    step, cols, dim = g_ref.shape
    high, wide, _ = x_out.shape
    turn = pl.program_id(0)

    @pl.when(turn == 0)
    def _():
        gates[...] = jnp.broadcast_to(gate_row(sums, cells, red, exp), gates.shape)

    bounds = (jnp.where(pos[0] == 0, 1, 0), z.shape[0], jnp.where(pos[1] == 0, 1, 0), cols)
    mix_lines(g_ref, gates[:1, :], mix, rest, z, turn * step, bounds)

    @pl.when(turn == pl.num_programs(0) - 1)
    def _():
        for i in range(high):
            out = pooled_line(z, line, i, wide)
            x_out[i] = out.astype(BF)
            keep_r[i * before : i * before + before, :] = out[wide - before :]
            keep_l[i * after : i * after + after, :] = out[:after]
        to_right[...] = keep_r[...].astype(BF)
        to_left[...] = keep_l[...].astype(BF)


def level_specs(sums, red, exp, mix, level):
    return [POSITION, whole(sums), at_level(red, level), at_level(exp, level), at_level(mix, level)]


def mix0(pos, sums, red, exp, mix, g, rest, cells, high, wide, before, after, step):
    rows, cols, dim = g.shape
    block = pl.BlockSpec((step, cols, dim), lambda i: (i, 0, 0))
    outs = [
        jax.ShapeDtypeStruct((high, wide, dim), BF),
        jax.ShapeDtypeStruct((high * before, dim), BF),
        jax.ShapeDtypeStruct((high * after, dim), BF),
    ]
    return pl.pallas_call(
        functools.partial(mix0_kernel, cells, before, after),
        grid=(rows // step,),
        in_specs=level_specs(sums, red, exp, mix, 0) + [block, block],
        out_specs=wholes(*outs),
        out_shape=outs,
        scratch_shapes=[
            pltpu.VMEM((8, dim), F32),
            pltpu.VMEM((rows, cols, dim), F32),
            pltpu.VMEM((dim // 128, cols, 128), F32),
            pltpu.VMEM((high * before, dim), F32),
            pltpu.VMEM((high * after, dim), F32),
        ],
        compiler_params=params(32),
        cost_estimate=cost(2 * rows * cols * dim * dim, 6 * rows * cols * dim),
        name="mix0",
    )(pos, sums, red, exp, mix, g, rest)


def mix1_kernel(cells, size, before, pos, sums, red, exp, mix, g_ref, rest, kernel, g_out, rest_out, part, z, line, padded):
    rows, cols, dim = g_ref.shape
    side_r, side_c, map_side = size
    gate = gate_row(sums, cells, red, exp)
    shift = before - 1
    row_low = shift - pos[0] * side_r
    col_low = shift - pos[1] * side_c
    mix_lines(g_ref, gate, mix, rest, z, 0, (row_low, row_low + map_side, col_low, col_low + map_side))
    count_r, count_c = padded.shape[0], (cols - 1) // 2
    row_two = 2 - pos[0] * (side_r // 2)
    col_two = 2 - pos[1] * (side_c // 2)
    column = lax.broadcasted_iota(jnp.int32, (count_c, 1), 0)
    inside = (column >= col_two) & (column < col_two + map_side // 2)
    for i in range(count_r):
        out = pooled_line(z, line, i, count_c)
        keep = inside & (i >= row_two) & (i < row_two + map_side // 2)
        padded[i, 0:count_c, :] = jnp.where(keep, out, 0.0)
    copy_centre(padded, rest_out)
    part[...] = jnp.zeros_like(part)
    conv_gelu(padded, kernel, g_out, (1, 1 + side_r // 2), (1, 1 + side_c // 2), part)


def mix1(pos, sums, red, exp, mix, g, rest, kernels, cells, size, before):
    rows, cols, dim = g.shape
    out_rows, out_cols = (rows - 1) // 2 - 2, round_up((cols - 1) // 2 - 2, 8)
    outs = [
        jax.ShapeDtypeStruct((out_rows, out_cols, dim), F32),
        jax.ShapeDtypeStruct((out_rows, out_cols, dim), BF),
        jax.ShapeDtypeStruct(sums.shape, F32),
    ]
    return pl.pallas_call(
        functools.partial(mix1_kernel, cells, size, before),
        grid=(1,),
        in_specs=level_specs(sums, red, exp, mix, 1) + wholes(g, rest) + [at_level(kernels, 2)],
        out_specs=wholes(*outs),
        out_shape=outs,
        scratch_shapes=[
            pltpu.VMEM((rows, cols, dim), F32),
            pltpu.VMEM((dim // 128, cols, 128), F32),
            pltpu.VMEM((out_rows + 2, round_up(out_cols + 2, 8), dim), F32),
        ],
        compiler_params=params(32),
        cost_estimate=cost(2 * rows * cols * dim * dim, 6 * rows * cols * dim),
        name="mix1",
    )(pos, sums, red, exp, mix, g, rest, kernels)


def mix2_kernel(cells, high, wide, pos, sums, red, exp, mix, g_ref, rest, x_out, z, line, keep):
    rows, cols, dim = g_ref.shape
    gate = gate_row(sums, cells, red, exp)
    bounds = (jnp.where(pos[0] == 0, 1, 0), rows, jnp.where(pos[1] == 0, 1, 0), cols)
    mix_lines(g_ref, gate, mix, rest, z, 0, bounds)
    for i in range(high):
        keep[i * wide : i * wide + wide, :] = pooled_line(z, line, i, wide)
    x_out[...] = jnp.broadcast_to(keep[...].astype(BF), x_out.shape)


def mix2(pos, sums, red, exp, mix, g, rest, cells, high, wide, copies):
    rows, cols, dim = g.shape
    out = jax.ShapeDtypeStruct((copies, high * wide, dim), BF)
    return pl.pallas_call(
        functools.partial(mix2_kernel, cells, high, wide),
        grid=(1,),
        in_specs=level_specs(sums, red, exp, mix, 2) + wholes(g, rest),
        out_specs=whole(out),
        out_shape=out,
        scratch_shapes=[
            pltpu.VMEM((rows, cols, dim), F32),
            pltpu.VMEM((dim // 128, cols, 128), F32),
            pltpu.VMEM((high * wide, dim), F32),
        ],
        compiler_params=params(24),
        cost_estimate=cost(2 * rows * cols * dim * dim, 6 * rows * cols * dim),
        name="mix2",
    )(pos, sums, red, exp, mix, g, rest)


def everyones(copies):
    return lax.all_to_all(copies, "tile", 0, 0, tiled=True)


def query_slab(tile_map, pos, dw_kernel, se_reduce, se_expand, mix_weight, keys_of):
    high, wide, dim = tile_map.shape
    tiles = lax.axis_size("tile")
    cells = high * wide * tiles
    group = 2 * TILE_COLS
    rims, first = exchange_rims(tile_map, side_pieces(tile_map, 2, 1), 2, 1, lambda held: keys_of(0, held))
    g, rest, part = activate(tile_map, rims, dw_kernel, 0, 2, 1, 11)
    coarse, to_right, to_left = mix0(
        pos, everyones(part), se_reduce, se_expand, mix_weight, g, rest, cells, high // 2, wide // 2, 6, 3, 11
    )
    rims, second = exchange_rims(coarse, (to_right, to_left), 6, 3, lambda held: keys_of(1, held))
    g, rest, part = activate(coarse, rims, dw_kernel, 1, 6, 3, high // 2 + 7)
    size = (high // 2, wide // 2, high // 2 * (tiles // TILE_COLS))
    g, rest, part = mix1(
        pos, everyones(part), se_reduce, se_expand, mix_weight, g, rest, dw_kernel, cells // 4, size, 6
    )
    query = mix2(
        pos, everyones(part), se_reduce, se_expand, mix_weight, g, rest, cells // 16, high // 8, wide // 8, group
    )
    groups = [list(range(group * x, group * x + group)) for x in range(tiles // group)]
    slab = lax.all_to_all(query, "tile", 0, 0, tiled=True, axis_index_groups=groups)
    return slab.reshape(-1, dim), first, second


def body(
    features,
    dw_kernel,
    se_reduce,
    se_expand,
    mix_weight,
    norm_gain,
    kv_weight,
    kv_bias,
    proj_weight,
    proj_bias,
):
    tile_map = features[0]
    dim = tile_map.shape[-1]
    position = lax.axis_index("tile")
    pos = jnp.stack([position // TILE_COLS, position % TILE_COLS]).astype(jnp.int32)
    gain, kv_row, proj_row = norm_gain.reshape(1, dim), kv_bias.reshape(1, 2 * dim), proj_bias.reshape(1, dim)

    def keys_of(window, held):
        return keys_values(after_these(tile_map, held), gain, kv_weight, kv_row, window)

    slab, (kt0, vt0), (kt1, vt1) = query_slab(
        tile_map, pos, dw_kernel, se_reduce, se_expand, mix_weight, keys_of
    )
    slabs = lax.axis_size("tile") // (2 * TILE_COLS)
    own = position // (2 * TILE_COLS)
    others = []
    for step in range(1, slabs):
        pairs = [(t, t ^ 2 * TILE_COLS * step) for t in range(lax.axis_size("tile"))]
        others.append(lax.ppermute(slab, "tile", pairs))
    keys, values = (kt0, kt1), (vt0, vt1)
    place = jnp.stack([own]).astype(jnp.int32)
    started = attention(place, [slab], keys, values, tile_map, proj_weight, proj_row)
    place = jnp.stack([own ^ step for step in range(1, slabs)]).astype(jnp.int32)
    return attention(place, others, keys, values, tile_map, proj_weight, proj_row, started)[None]


def solution(mesh):
    in_specs = (P(("scene", "tile"), None, None, None), P(), P(), P(), P(), P(), P(), P(), P(), P())
    out_specs = P(("scene", "tile"), None, None, None)
    return jax.shard_map(body, mesh=mesh, in_specs=in_specs, out_specs=out_specs, check_vma=False)
```

time: 354 us -> 213 us (0.60)
  other arithmetic: 54.9 us -> 0.15 us
  waiting for transfers between devices: 66.1 us -> 24.3 us
  Pallas kernels: 64.4 us -> 95.5 us
  blocking collectives: 51.4 us -> 26.9 us
  starting transfers between devices: 54.5 us -> 35.4 us
  matrix products: 17.6 us -> 0 us
  between operations: 14 us -> 0.5 us
    all_gather x1 -> x0, waiting for transfers between devices: 34.2 us -> none  [body(): collected = lax.all_gather(coarse[None], 'tile', axis=0, tiled=True)]
    reduce_sum x6 -> x0, other arithmetic: 32.6 us -> none  [the longest x3 32.4 us: level_step(): channel_mean = sum_rule(jnp.sum(response, axis=(0, 1))) / cell_count]
    ppermute x18 -> x11, starting transfers between devices: 54.5 us -> 22.9 us  [the longest x8 18.2 us: moved_by(): return lax.ppermute(value, 'tile', pairs)]
    pallas_call x2 -> x12, Pallas kernels: 64.4 us -> 95.5 us  [the longest x2 50.9 us: attention(): pl.pallas_call(functools.partial(attention_kernel, slabs), in_specs=[pl.B...]
    all_to_all x3 -> x2, blocking collectives: 51.4 us -> 26.9 us  [everyones(): return lax.all_to_all(copies, 'tile', 0, 0, tiled=True)]
    unnamed x20 -> x53, local copies, waits for them, and re-layouts: 7.02 us -> 29 us
    ppermute x18 -> x11, waiting for transfers between devices: 32 us -> 10.1 us  [the longest x8 10.1 us: moved_by(): return lax.ppermute(value, 'tile', pairs)]
    dot_general x9 -> x0, matrix products: 17.6 us -> none  [the longest x3 10.2 us: level_step(): jnp.dot(scaled.reshape(-1, channels), mix_matrix, preferred_element_type=...]
  transfers between devices with their start and end apart: 19 -> 13, of which waited for: 15 -> 7; matrix products, arithmetic and copies ran while one was open for 1% -> 1% of each run, Pallas kernels for 3% -> 11%
where the time goes in v2:
time: 213 us; the launch traced here: 212 us
  Pallas kernels  95.5 us (45%)
  starting transfers between devices  35.4 us (17%)
  local copies, waits for them, and re-layouts  29 us (14%)
  blocking collectives  26.9 us (13%)
  waiting for transfers between devices  24.3 us (11%)
    pallas_call x2, Pallas kernels, attention(): pl.pallas_call(functools.partial(attention_kernel, slabs), in_specs=[pl.B...  50.9 us
    unnamed x53, local copies, waits for them, and re-layouts  29 us
    all_to_all x2, blocking collectives, everyones(): return lax.all_to_all(copies, 'tile', 0, 0, tiled=True)  26.9 us
    pallas_call x2, Pallas kernels, activate(): pl.pallas_call(functools.partial(act_kernel, before, after), grid=(rows /...  22.2 us
    ppermute x8, starting transfers between devices, moved_by(): return lax.ppermute(value, 'tile', pairs)  18.2 us
    ppermute x8, waiting for transfers between devices, moved_by(): return lax.ppermute(value, 'tile', pairs)  10.1 us
    pallas_call x2, Pallas kernels, keys_values(): pl.pallas_call(kv_kernel, grid=(win // step,), in_specs=[pl.BlockSpec((st...  9.49 us
    all_to_all x1, starting transfers between devices, everyones(): return lax.all_to_all(copies, 'tile', 0, 0, tiled=True)  9.07 us
  transfers between devices with their start and end apart: 13, of which 7 were waited for; matrix products, arithmetic and copies ran while one was open for 1% of the time, Pallas kernels for 11%

profile of v2, /device:TPU:0, one launch (start us, length us, event | category | flops | bytes accessed | tf_op | source)
XLA Modules:
  0.0 211.7 jit_solution(14451009781667656394)
XLA Ops:
  0.0 1.9 copy-done
  4.7 4.0 %collective-permute-done.1.rest_1_.r_ref = bf16[32,768]{1,0:T(8,128)(2,1)S(1)} collective-permute-done((bf16[32,768]{1,0:T(8,128)(2,1)S(1)}, bf16[32,768]{1,0:T(8,128)(2,1)S(1)}, u32[]{:S(2)}, u32[]{:S(2)}) %collective-permute-start.1) | collective-permute-done | bytes 49184 | tf_op jit(solution)/shard_map/ppermute | solution.py:294
  8.8 5.5 %collective-permute-start.2 = (bf16[144,768]{1,0:T(8,128)(2,1)S(1)}, bf16[144,768]{1,0:T(8,128)(2,1)S(1)}, u32[]{:S(2)}, u32[]{:S(2)}) collective-permute-start(bf16[144,768]{1,0:T(8,128)(2,1)S(1)} %get-tuple-element.39), channel_id=1, source_target_pairs={{0,4},{1,5},{2,6},{3,7},{4,8},{5,9},{6,10},{7,11},{8,12},{9,13},{1... | collective-permute-start | bytes 663560 | tf_op jit(solution)/shard_map/ppermute | solution.py:294
  14.3 1.4 collective-permute-start.3
  15.8 4.7 %keys_values.2 = (bf16[6,1024,128]{2,1,0:T(8,128)(2,1)S(1)}, bf16[768,1024]{1,0:T(8,128)(2,1)S(1)}) custom-call(bf16[32,64,768]{2,1,0:T(8,128)(2,1)S(1)} %bitcast.13, f32[1,768]{1,0:T(1,128)S(1)} %reshape.12.gain_ref, bf16[768,1536]{1,0:T(8,128)(2,1)S(1)} %copy-done.12, f32[1,1536]{1,0:T(1,128)S(1)} %reshape.13.b_ref), custom_call_target="tpu_custom_call" | custom-call | flops 4831838208 | bytes 8388608 | tf_op jit(solution)/shard_map/keys_values/pallas_call | solution.py:41
  22.7 15.2 %activate.2 = (f32[33,72,768]{2,1,0:T(8,128)S(1)}, bf16[33,72,768]{2,1,0:T(8,128)(2,1)S(1)}, f32[32,8,128]{2,1,0:T(8,128)}) custom-call(bf16[32,64,768]{2,1,0:T(8,128)(2,1)S(1)} %bitcast.14, bf16[64,768]{1,0:T(8,128)(2,1)S(1)} %collective-permute-done.rest_0_.l_ref, bf16[32,768]{1,0:T(8,128)(2,1)S(1)} %collective-permute-done.1.rest_1_.r_ref, ...), custom_call_target="tpu_custom_call" | custom-call | flops 729907200 | bytes 10948608 | tf_op jit(solution)/shard_map/activate/pallas_call | solution.py:437
  37.9 2.9 %copy-done.7 = f32[33,72,768]{2,1,0:T(8,128)} copy-done((f32[33,72,768]{2,1,0:T(8,128)}, f32[33,72,768]{2,1,0:T(8,128)S(1)}, u32[]{:S(2)}) %copy-start.7) | copy-done | bytes 7299096
  40.8 1.9 copy-done.9
  42.7 9.1 %all-to-all-start = ((f32[32,8,128]{2,1,0:T(8,128)}), f32[32,8,128]{2,1,0:T(8,128)S(1)}, u32[]{:S(2)}, u32[]{:S(2)}) async-start(f32[32,8,128]{2,1,0:T(8,128)} %get-tuple-element.46), calls=%async_computation | async-start | bytes 262144 | tf_op jit(solution)/shard_map/all_to_all | solution.py:589
  51.8 2.3 %copy.12.red = bf16[3,768,192]{2,1,0:T(8,128)(2,1)} copy(bf16[3,768,192]{1,2,0:T(8,128)(2,1)} %param.12) | data formatting | bytes 1769472 | tf_op args[2]
  54.3 5.4 %all-to-all-done.sums = f32[32,8,128]{2,1,0:T(8,128)S(1)} async-done(((f32[32,8,128]{2,1,0:T(8,128)}), f32[32,8,128]{2,1,0:T(8,128)S(1)}, u32[]{:S(2)}, u32[]{:S(2)}) %all-to-all-start) | async-done | bytes 131104 | tf_op jit(solution)/shard_map/all_to_all | solution.py:589
  59.7 2.0 copy-done.2
  64.1 3.1 %copy-done.8 = f32[33,72,768]{2,1,0:T(8,128)S(1)} copy-done((f32[33,72,768]{2,1,0:T(8,128)S(1)}, f32[33,72,768]{2,1,0:T(8,128)}, u32[]{:S(2)}) %copy-start.8) | copy-done | bytes 7299096
  67.2 2.0 copy-done.10
  69.2 5.6 %mix0.1 = (bf16[16,32,768]{2,1,0:T(8,128)(2,1)S(1)}, bf16[96,768]{1,0:T(8,128)(2,1)S(1)}, bf16[48,768]{1,0:T(8,128)(2,1)S(1)}) custom-call(s32[2]{0:T(128)S(1)} %pad_add_fusion.1.pos, f32[32,8,128]{2,1,0:T(8,128)S(1)} %all-to-all-done.sums, bf16[3,768,192]{2,1,0:T(8,128)(2,1)S(1)} %copy-done.3, bf16[3,192,768]{2,1,0:T(8,128)(2,1)S(1)} %copy-done.5, ...), custom_call_target="tpu_custom_call" | custom-call | flops 2802843648 | bytes 10948608 | tf_op jit(solution)/shard_map/mix0/pallas_call | solution.py:492
  74.8 2.0 collective-permute-start.4
  78.1 1.9 collective-permute-done.5.rest_1_.r_ref
  80.3 4.1 %collective-permute-start.6 = (bf16[256,768]{1,0:T(8,128)(2,1)S(1)}, bf16[256,768]{1,0:T(8,128)(2,1)S(1)}, u32[]{:S(2)}, u32[]{:S(2)}) collective-permute-start(bf16[256,768]{1,0:T(8,128)(2,1)S(1)} %get-tuple-element.52), channel_id=1, source_target_pairs={{0,4},{1,5},{2,6},{3,7},{4,8},{5,9},{6,10},{7,11},{8,12},{9,13},{1... | collective-permute-start | bytes 1179656 | tf_op jit(solution)/shard_map/ppermute | solution.py:294
  85.7 4.7 %keys_values.3 = (bf16[6,1024,128]{2,1,0:T(8,128)(2,1)S(1)}, bf16[768,1024]{1,0:T(8,128)(2,1)S(1)}) custom-call(bf16[32,64,768]{2,1,0:T(8,128)(2,1)S(1)} %bitcast.15, f32[1,768]{1,0:T(1,128)S(1)} %reshape.12.gain_ref, bf16[768,1536]{1,0:T(8,128)(2,1)S(1)} %copy-done.13, f32[1,1536]{1,0:T(1,128)S(1)} %reshape.13.b_ref), custom_call_target="tpu_custom_call" | custom-call | flops 4831838208 | bytes 8388608 | tf_op jit(solution)/shard_map/keys_values/pallas_call | solution.py:41
  93.7 2.2 %collective-permute-done.6.a_ref = bf16[256,768]{1,0:T(8,128)(2,1)S(1)} collective-permute-done((bf16[256,768]{1,0:T(8,128)(2,1)S(1)}, bf16[256,768]{1,0:T(8,128)(2,1)S(1)}, u32[]{:S(2)}, u32[]{:S(2)}) %collective-permute-start.6) | collective-permute-done | bytes 393248 | tf_op jit(solution)/shard_map/ppermute | solution.py:294
  95.9 6.9 %activate.3 = (f32[23,40,768]{2,1,0:T(8,128)S(1)}, bf16[23,40,768]{2,1,0:T(8,128)(2,1)S(1)}, f32[32,8,128]{2,1,0:T(8,128)S(1)}) custom-call(bf16[16,32,768]{2,1,0:T(8,128)(2,1)S(1)} %get-tuple-element.49.top_ref.low_ref.x_ref, bf16[96,768]{1,0:T(8,128)(2,1)S(1)} %collective-permute-done.4.rest_0_.l_ref, ...), custom_call_target="tpu_custom_call" | custom-call | flops 282624000 | bytes 4239360 | tf_op jit(solution)/shard_map/activate/pallas_call | solution.py:437
  102.9 15.6 %all_to_all.20.sums = f32[32,8,128]{2,1,0:T(8,128)S(1)} all-to-all(f32[32,8,128]{2,1,0:T(8,128)S(1)} %get-tuple-element.59), channel_id=1, replica_groups=mesh['scene'=4,'tile'=32] {'tile'}, dimensions={0} | all-to-all | bytes 262144 | tf_op jit(solution)/shard_map/all_to_all | solution.py:589
  118.4 4.7 %mix1.1 = (f32[9,24,768]{2,1,0:T(8,128)S(1)}, bf16[9,24,768]{2,1,0:T(8,128)(2,1)S(1)}, f32[32,8,128]{2,1,0:T(8,128)S(1)}) custom-call(s32[2]{0:T(128)S(1)} %pad_add_fusion.1.pos, f32[32,8,128]{2,1,0:T(8,128)S(1)} %all_to_all.20.sums, bf16[3,768,192]{2,1,0:T(8,128)(2,1)S(1)} %copy-done.4, bf16[3,192,768]{2,1,0:T(8,128)(2,1)S(1)} %copy-done.6, ...), custom_call_target="tpu_custom_call" | custom-call | flops 1085276160 | bytes 4239360 | tf_op jit(solution)/shard_map/mix1/pallas_call | solution.py:541
  123.2 11.3 %all_to_all.21.sums = f32[32,8,128]{2,1,0:T(8,128)S(1)} all-to-all(f32[32,8,128]{2,1,0:T(8,128)S(1)} %get-tuple-element.62), channel_id=1, replica_groups=mesh['scene'=4,'tile'=32] {'tile'}, dimensions={0} | all-to-all | bytes 262144 | tf_op jit(solution)/shard_map/all_to_all | solution.py:589
  134.4 2.2 %mix2.1 = bf16[8,32,768]{2,1,0:T(8,128)(2,1)} custom-call(s32[2]{0:T(128)S(1)} %pad_add_fusion.1.pos, f32[32,8,128]{2,1,0:T(8,128)S(1)} %all_to_all.21.sums, bf16[3,768,192]{2,1,0:T(8,128)(2,1)S(1)} %copy-done.4, bf16[3,192,768]{2,1,0:T(8,128)(2,1)S(1)} %copy-done.6, bf16[3,768,768]{2,1,0:T(8,128)(2,1)S(1)} %copy-done.2, ...), custom_call_target="tpu_custom_call" | custom-call | flops 254803968 | bytes 995328 | tf_op jit(solution)/shard_map/mix2/pallas_call | solution.py:571
  136.6 3.5 %all-to-all-start.3 = ((bf16[8,32,768]{2,1,0:T(8,128)(2,1)}), bf16[8,32,768]{2,1,0:T(8,128)(2,1)S(1)}, u32[]{:S(2)}, u32[]{:S(2)}) async-start(bf16[8,32,768]{2,1,0:T(8,128)(2,1)} %mix2.1), calls=%async_computation.3 | async-start | bytes 786432 | tf_op jit(solution)/shard_map/all_to_all | solution.py:612
  140.2 8.7 %all-to-all-done.3 = bf16[8,32,768]{2,1,0:T(8,128)(2,1)S(1)} async-done(((bf16[8,32,768]{2,1,0:T(8,128)(2,1)}), bf16[8,32,768]{2,1,0:T(8,128)(2,1)S(1)}, u32[]{:S(2)}, u32[]{:S(2)}) %all-to-all-start.3) | async-done | bytes 393248 | tf_op jit(solution)/shard_map/all_to_all | solution.py:612
  149.5 2.0 collective-permute-start.9
  151.5 2.1 %collective-permute-start.10 = (bf16[256,768]{1,0:T(8,128)(2,1)S(1)}, bf16[256,768]{1,0:T(8,128)(2,1)S(1)}, u32[]{:S(2)}, u32[]{:S(2)}) collective-permute-start(bf16[256,768]{1,0:T(8,128)(2,1)S(1)} %bitcast.20), channel_id=1, source_target_pairs={{0,24},{1,25},{2,26},{3,27},{4,28},{5,29},{6,30},{7,31},{8,16},{9,... | collective-permute-start | bytes 1179656 | tf_op jit(solution)/shard_map/ppermute | solution.py:645
  156.3 1.4 copy-done.18
  160.5 13.3 %attention.2.refs_10_ = bf16[32,64,768]{2,1,0:T(8,128)(2,1)} custom-call(s32[1]{0:T(128)} %bitcast.7.slab_ref, bf16[256,768]{1,0:T(8,128)(2,1)S(1)} %bitcast.21, bf16[6,1024,128]{2,1,0:T(8,128)(2,1)S(1)} %copy-done.16, bf16[6,1024,128]{2,1,0:T(8,128)(2,1)S(1)} %copy-done.20, bf16[768,1024]{1,0:T(8,128)(2,1)S(1)} %copy-done.18, ...), custom_call_target="tpu_custom_call" | custom-call | flops 12884901888 | bytes 12582912 | tf_op jit(solution)/shard_map/attention/pallas_call | solution.py:150
  173.9 37.6 %attention.3 = bf16[32,64,768]{2,1,0:T(8,128)(2,1)} custom-call(s32[3]{0:T(128)S(1)} %pad_add_fusion.slab_ref, bf16[256,768]{1,0:T(8,128)(2,1)S(1)} %collective-permute-done.8.refs_0_, bf16[256,768]{1,0:T(8,128)(2,1)S(1)} %collective-permute-done.9.refs_1_, bf16[256,768]{1,0:T(8,128)(2,1)S(1)} %collective-permute-done.10.refs_2_, ...), custom_call_target="tpu_custom_call", output_to_operand_aliasing={{}: (11, {})} | custom-call | flops 38654705664 | bytes 12582912 | tf_op jit(solution)/shard_map/attention/pallas_call | solution.py:150
  (66 shorter events, 19.8 us)
Async XLA Ops:
  0.0 1.9 copy-start
  1.9 2.7 %copy-start.24 = (f32[768]{0:T(1024)S(1)}, f32[768]{0:T(1024)}, u32[]{:S(2)}) copy-start(f32[768]{0:T(1024)} %param.15) | copy-start | bytes 9220
  1.9 2.8 %copy-start.23 = (f32[1536]{0:T(1024)S(1)}, f32[1536]{0:T(1024)}, u32[]{:S(2)}) copy-start(f32[1536]{0:T(1024)} %param.17) | copy-start | bytes 18436
  2.0 6.7 %collective-permute-start = (bf16[64,768]{1,0:T(8,128)(2,1)S(1)}, bf16[64,768]{1,0:T(8,128)(2,1)S(1)}, u32[]{:S(2)}, u32[]{:S(2)}) collective-permute-start(bf16[64,768]{1,0:T(8,128)(2,1)S(1)} %get-tuple-element.37), channel_id=1, source_target_pairs={{0,1},{1,2},{2,3},{4,5},{5,6},{6,7},{8,9},{9,10},{10,11},{12,13},{... | collective-permute-start | bytes 294920 | tf_op jit(solution)/shard_map/ppermute | solution.py:294
  3.3 5.4 %collective-permute-start.1 = (bf16[32,768]{1,0:T(8,128)(2,1)S(1)}, bf16[32,768]{1,0:T(8,128)(2,1)S(1)}, u32[]{:S(2)}, u32[]{:S(2)}) collective-permute-start(bf16[32,768]{1,0:T(8,128)(2,1)S(1)} %get-tuple-element.38), channel_id=1, source_target_pairs={{1,0},{2,1},{3,2},{5,4},{6,5},{7,6},{9,8},{10,9},{11,10},{13,12},{... | collective-permute-start | bytes 147464 | tf_op jit(solution)/shard_map/ppermute | solution.py:294
  4.7 11.1 %copy-start.1 = (bf16[1,32,64,768]{3,2,1,0:T(8,128)(2,1)S(1)}, bf16[1,32,64,768]{3,2,1,0:T(8,128)(2,1)}, u32[]{:S(2)}) copy-start(bf16[1,32,64,768]{3,2,1,0:T(8,128)(2,1)} %param.10) | copy-start | bytes 9437188
  4.7 11.1 %copy-start.12 = (bf16[768,1536]{1,0:T(8,128)(2,1)S(1)}, bf16[768,1536]{1,0:T(8,128)(2,1)}, u32[]{:S(2)}) copy-start(bf16[768,1536]{1,0:T(8,128)(2,1)} %w_ref.3) | copy-start | bytes 7077892
  8.8 13.9 %collective-permute-start.2 = (bf16[144,768]{1,0:T(8,128)(2,1)S(1)}, bf16[144,768]{1,0:T(8,128)(2,1)S(1)}, u32[]{:S(2)}, u32[]{:S(2)}) collective-permute-start(bf16[144,768]{1,0:T(8,128)(2,1)S(1)} %get-tuple-element.39), channel_id=1, source_target_pairs={{0,4},{1,5},{2,6},{3,7},{4,8},{5,9},{6,10},{7,11},{8,12},{9,13},{1... | collective-permute-start | bytes 663560 | tf_op jit(solution)/shard_map/ppermute | solution.py:294
  14.3 8.4 %copy-start.11 = (bf16[3,3,3,768]{3,2,1,0:T(4,128)(2,1)S(1)}, bf16[3,3,3,768]{3,2,1,0:T(4,128)(2,1)}, u32[]{:S(2)}) copy-start(bf16[3,3,3,768]{3,2,1,0:T(4,128)(2,1)} %kernel.1) | copy-start | bytes 124420
  14.3 8.4 %collective-permute-start.3 = (bf16[80,768]{1,0:T(8,128)(2,1)S(1)}, bf16[80,768]{1,0:T(8,128)(2,1)S(1)}, u32[]{:S(2)}, u32[]{:S(2)}) collective-permute-start(bf16[80,768]{1,0:T(8,128)(2,1)S(1)} %get-tuple-element.40), channel_id=1, source_target_pairs={{4,0},{5,1},{6,2},{7,3},{8,4},{9,5},{10,6},{11,7},{12,8},{13,9},{1... | collective-permute-start | bytes 368648 | tf_op jit(solution)/shard_map/ppermute | solution.py:294
  21.7 16.3 %copy-start.17 = (bf16[768,1024]{1,0:T(8,128)(2,1)}, bf16[768,1024]{1,0:T(8,128)(2,1)S(1)}, u32[]{:S(2)}) copy-start(bf16[768,1024]{1,0:T(8,128)(2,1)S(1)} %get-tuple-element.67.refs_3_.refs_5_) | copy-start | bytes 4718596
  37.9 2.9 %copy-start.7 = (f32[33,72,768]{2,1,0:T(8,128)}, f32[33,72,768]{2,1,0:T(8,128)S(1)}, u32[]{:S(2)}) copy-start(f32[33,72,768]{2,1,0:T(8,128)S(1)} %get-tuple-element.47.g_ref) | copy-start | bytes 21897220
  40.8 1.9 copy-start.9
  42.7 16.9 %all-to-all-start = ((f32[32,8,128]{2,1,0:T(8,128)}), f32[32,8,128]{2,1,0:T(8,128)S(1)}, u32[]{:S(2)}, u32[]{:S(2)}) async-start(f32[32,8,128]{2,1,0:T(8,128)} %get-tuple-element.46), calls=%async_computation | async-start | bytes 262144 | tf_op jit(solution)/shard_map/all_to_all | solution.py:589
  59.7 2.0 copy-start.2
  64.1 3.1 %copy-start.8 = (f32[33,72,768]{2,1,0:T(8,128)S(1)}, f32[33,72,768]{2,1,0:T(8,128)}, u32[]{:S(2)}) copy-start(f32[33,72,768]{2,1,0:T(8,128)} %copy-done.7) | copy-start | bytes 21897220
  67.2 2.0 copy-start.10
  69.2 16.4 %copy-start.13 = (bf16[768,1536]{1,0:T(8,128)(2,1)S(1)}, bf16[768,1536]{1,0:T(8,128)(2,1)}, u32[]{:S(2)}) copy-start(bf16[768,1536]{1,0:T(8,128)(2,1)} %w_ref.3) | copy-start | bytes 7077892
  74.8 5.2 %collective-permute-start.4 = (bf16[96,768]{1,0:T(8,128)(2,1)S(1)}, bf16[96,768]{1,0:T(8,128)(2,1)S(1)}, u32[]{:S(2)}, u32[]{:S(2)}) collective-permute-start(bf16[96,768]{1,0:T(8,128)(2,1)S(1)} %get-tuple-element.50), channel_id=1, source_target_pairs={{0,1},{1,2},{2,3},{4,5},{5,6},{6,7},{8,9},{9,10},{10,11},{12,13},{... | collective-permute-start | bytes 442376 | tf_op jit(solution)/shard_map/ppermute | solution.py:294
  76.8 3.2 %collective-permute-start.5 = (bf16[48,768]{1,0:T(8,128)(2,1)S(1)}, bf16[48,768]{1,0:T(8,128)(2,1)S(1)}, u32[]{:S(2)}, u32[]{:S(2)}) collective-permute-start(bf16[48,768]{1,0:T(8,128)(2,1)S(1)} %get-tuple-element.51), channel_id=1, source_target_pairs={{1,0},{2,1},{3,2},{5,4},{6,5},{7,6},{9,8},{10,9},{11,10},{13,12},{... | collective-permute-start | bytes 221192 | tf_op jit(solution)/shard_map/ppermute | solution.py:294
  80.3 15.6 %collective-permute-start.6 = (bf16[256,768]{1,0:T(8,128)(2,1)S(1)}, bf16[256,768]{1,0:T(8,128)(2,1)S(1)}, u32[]{:S(2)}, u32[]{:S(2)}) collective-permute-start(bf16[256,768]{1,0:T(8,128)(2,1)S(1)} %get-tuple-element.52), channel_id=1, source_target_pairs={{0,4},{1,5},{2,6},{3,7},{4,8},{5,9},{6,10},{7,11},{8,12},{9,13},{1... | collective-permute-start | bytes 1179656 | tf_op jit(solution)/shard_map/ppermute | solution.py:294
  84.3 9.3 %collective-permute-start.7 = (bf16[128,768]{1,0:T(8,128)(2,1)S(1)}, bf16[128,768]{1,0:T(8,128)(2,1)S(1)}, u32[]{:S(2)}, u32[]{:S(2)}) collective-permute-start(bf16[128,768]{1,0:T(8,128)(2,1)S(1)} %get-tuple-element.53), channel_id=1, source_target_pairs={{4,0},{5,1},{6,2},{7,3},{8,4},{9,5},{10,6},{11,7},{12,8},{13,9},{1... | collective-permute-start | bytes 589832 | tf_op jit(solution)/shard_map/ppermute | solution.py:294
  85.6 32.8 %copy-start.6 = (bf16[3,192,768]{2,1,0:T(8,128)(2,1)S(1)}, bf16[3,192,768]{2,1,0:T(8,128)(2,1)}, u32[]{:S(2)}) copy-start(bf16[3,192,768]{2,1,0:T(8,128)(2,1)} %exp.5) | copy-start | bytes 2654212
  92.8 25.7 %copy-start.4 = (bf16[3,768,192]{2,1,0:T(8,128)(2,1)S(1)}, bf16[3,768,192]{2,1,0:T(8,128)(2,1)}, u32[]{:S(2)}) copy-start(bf16[3,768,192]{2,1,0:T(8,128)(2,1)} %copy.12.red) | copy-start | bytes 2654212
  134.4 5.7 %copy-start.25 = (f32[768]{0:T(1024)S(1)}, f32[768]{0:T(1024)}, u32[]{:S(2)}) copy-start(f32[768]{0:T(1024)} %param.19) | copy-start | bytes 9220
  136.6 12.3 %all-to-all-start.3 = ((bf16[8,32,768]{2,1,0:T(8,128)(2,1)}), bf16[8,32,768]{2,1,0:T(8,128)(2,1)S(1)}, u32[]{:S(2)}, u32[]{:S(2)}) async-start(bf16[8,32,768]{2,1,0:T(8,128)(2,1)} %mix2.1), calls=%async_computation.3 | async-start | bytes 786432 | tf_op jit(solution)/shard_map/all_to_all | solution.py:612
  148.9 24.9 %collective-permute-start.8 = (bf16[256,768]{1,0:T(8,128)(2,1)S(1)}, bf16[256,768]{1,0:T(8,128)(2,1)S(1)}, u32[]{:S(2)}, u32[]{:S(2)}) collective-permute-start(bf16[256,768]{1,0:T(8,128)(2,1)S(1)} %bitcast.18), channel_id=1, source_target_pairs={{0,8},{1,9},{2,10},{3,11},{4,12},{5,13},{6,14},{7,15},{8,0},{9,1},... | collective-permute-start | bytes 1179656 | tf_op jit(solution)/shard_map/ppermute | solution.py:645
  149.5 24.4 %collective-permute-start.9 = (bf16[256,768]{1,0:T(8,128)(2,1)S(1)}, bf16[256,768]{1,0:T(8,128)(2,1)S(1)}, u32[]{:S(2)}, u32[]{:S(2)}) collective-permute-start(bf16[256,768]{1,0:T(8,128)(2,1)S(1)} %bitcast.19), channel_id=1, source_target_pairs={{0,16},{1,17},{2,18},{3,19},{4,20},{5,21},{6,22},{7,23},{8,24},{9,... | collective-permute-start | bytes 1179656 | tf_op jit(solution)/shard_map/ppermute | solution.py:645
  151.5 22.4 %collective-permute-start.10 = (bf16[256,768]{1,0:T(8,128)(2,1)S(1)}, bf16[256,768]{1,0:T(8,128)(2,1)S(1)}, u32[]{:S(2)}, u32[]{:S(2)}) collective-permute-start(bf16[256,768]{1,0:T(8,128)(2,1)S(1)} %bitcast.20), channel_id=1, source_target_pairs={{0,24},{1,25},{2,26},{3,27},{4,28},{5,29},{6,30},{7,31},{8,16},{9,... | collective-permute-start | bytes 1179656 | tf_op jit(solution)/shard_map/ppermute | solution.py:645
  156.3 1.4 copy-start.18
  157.7 1.4 copy-start.20
  159.1 1.4 copy-start.22
  (7 other events, 8.6 us)

commit v3 on v2

--- a/solution.py
+++ b/solution.py
@@ -26,11 +26,11 @@
     centre = jnp.mean(x, axis=1, keepdims=True)
     moved = x - centre
     spread = jnp.mean(jnp.square(moved), axis=1, keepdims=True)
-    normed = (moved * lax.rsqrt(spread + EPSILON) * gain_ref[...]).astype(BF)
-    keys = (jnp.dot(normed, w_ref[:, :dim], preferred_element_type=F32) + b_ref[:, :dim]).astype(BF)
+    normed = (moved * lax.rsqrt(spread + EPSILON) * gain_ref[...].reshape(1, dim)).astype(BF)
+    keys = (jnp.dot(normed, w_ref[:, :dim], preferred_element_type=F32) + b_ref[:dim].reshape(1, dim)).astype(BF)
     for group in range(dim // 128):
         kt_ref[group] = keys[:, 128 * group : 128 * group + 128]
-    vals = jnp.dot(normed, w_ref[:, dim:], preferred_element_type=F32) + b_ref[:, dim:]
+    vals = jnp.dot(normed, w_ref[:, dim:], preferred_element_type=F32) + b_ref[dim:].reshape(1, dim)
     vt_ref[...] = vals.T.astype(BF)
 
 
@@ -43,9 +43,9 @@
         grid=(win // step,),
         in_specs=[
             pl.BlockSpec((step, win, dim), lambda i: (i, window, 0)),
-            pl.BlockSpec((1, dim), lambda i: (0, 0)),
+            pl.BlockSpec((dim,), lambda i: (0,)),
             pl.BlockSpec((dim, 2 * dim), lambda i: (0, 0)),
-            pl.BlockSpec((1, 2 * dim), lambda i: (0, 0)),
+            pl.BlockSpec((2 * dim,), lambda i: (0,)),
         ],
         out_specs=[
             pl.BlockSpec((dim // 128, tokens, 128), lambda i: (0, i, 0)),
@@ -63,7 +63,8 @@
     )(tile_map, gain, weight, bias)
 
 
-def attention_kernel(slabs, slab_ref, *refs):
+def attention_kernel(steps, *refs):
+    slabs = len(steps)
     q_refs = refs[:slabs]
     kt_refs, vt_refs = refs[slabs : slabs + 2], refs[slabs + 2 : slabs + 4]
     x_ref, wp_ref, bp_ref = refs[slabs + 4 : slabs + 7]
@@ -125,14 +126,15 @@
     lines = QB // win
     copies = []
     for slab in range(slabs):
-        place = pl.ds(pl.multiple_of(slab_ref[slab] * lines, lines), lines)
+        own = lax.axis_index("tile") // (2 * TILE_COLS)
+        place = pl.ds(pl.multiple_of((own ^ steps[slab]) * lines, lines), lines)
         for w in range(2):
             cols = slice(w * win, w * win + win)
             y = lax.dot_general(
                 ot[slab, w], wp_ref[...], (((0,), (0,)), ((), ())), preferred_element_type=F32
             )
             y = y.reshape(2, 4, lines // 2, win // 4, dim).transpose(0, 2, 1, 3, 4).reshape(lines, win, dim)
-            y = x_ref[place, cols, :].astype(F32) + y + bp_ref[...]
+            y = x_ref[place, cols, :].astype(F32) + y + bp_ref[...].reshape(1, dim)
             stage[slab, :, cols, :] = y.astype(BF)
         copy = pltpu.make_async_copy(stage.at[slab], out_ref.at[place], sems.at[slab])
         copy.start()
@@ -141,18 +143,18 @@
         copy.wait()
 
 
-def attention(place, queries, keys, values, tile_map, wp, bp, started=None):
+def attention(steps, queries, keys, values, tile_map, wp, bp, started=None):
     rows, cols, dim = tile_map.shape
     slabs = len(queries)
     lines = QB * 2 // cols
     more = [] if started is None else [started]
     anywhere = pl.BlockSpec(memory_space=pl.ANY)
     return pl.pallas_call(
-        functools.partial(attention_kernel, slabs),
-        in_specs=[pl.BlockSpec(memory_space=pltpu.SMEM)] + [VM] * (slabs + 7) + [anywhere] * len(more),
+        functools.partial(attention_kernel, steps),
+        in_specs=[VM] * (slabs + 7) + [anywhere] * len(more),
         out_specs=anywhere,
         out_shape=jax.ShapeDtypeStruct(tile_map.shape, BF),
-        input_output_aliases={slabs + 8: 0} if more else {},
+        input_output_aliases={slabs + 7: 0} if more else {},
         scratch_shapes=[
             pltpu.VMEM((slabs, HEADS, QB, 128), BF),
             pltpu.VMEM((2, 2, rows * cols // 2, QB), F32),
@@ -168,7 +170,7 @@
             transcendentals=48 * slabs * QB * 1024,
         ),
         name="attention",
-    )(place, *queries, *keys, *values, tile_map, wp, bp, *more)
+    )(*queries, *keys, *values, tile_map, wp, bp, *more)
 
 
 def whole(array):
@@ -184,7 +186,9 @@
     return pl.BlockSpec(shape, lambda *i: (level,) + (0,) * (len(shape) - 1), pipeline_mode=pl.Buffered(1))
 
 
-POSITION = pl.BlockSpec(memory_space=pltpu.SMEM)
+def position():
+    index = lax.axis_index("tile")
+    return index // TILE_COLS, index % TILE_COLS
 
 
 def params(mib):
@@ -223,7 +227,7 @@
             jax.ShapeDtypeStruct((high * after, dim), BF),
         ],
         scratch_shapes=[pltpu.VMEM((high * before, dim), F32), pltpu.VMEM((high * after, dim), F32)],
-        compiler_params=params(16),
+        compiler_params=params(12),
         cost_estimate=cost(0, 2 * 2**20),
         name="side_pieces",
     )(tile, tile)
@@ -274,7 +278,7 @@
             pltpu.VMEM(left.shape, F32),
             pltpu.VMEM(right.shape, F32),
         ],
-        compiler_params=params(16),
+        compiler_params=params(12),
         cost_estimate=cost(0, 2**20),
         name="line_pieces",
     )(tile, tile, left, right)
@@ -355,7 +359,7 @@
             counted = jnp.sum(jnp.where(mine, g, 0.0).reshape(cols // 8, 8, 128), axis=0)
             return total + jnp.where((r >= own_rows[0]) & (r < own_rows[1]), counted, 0.0)
 
-        total = lax.fori_loop(0, rows, line, jnp.zeros((8, 128), F32))
+        total = lax.fori_loop(0, rows, line, jnp.zeros((8, 128), F32), unroll=True)
         total = jnp.sum(total, axis=0, keepdims=True)
         part_ref[:, group, :] += jnp.broadcast_to(total, (part_ref.shape[0], 128))
 
@@ -381,9 +385,12 @@
 
 def gate_row(sums_ref, cells, reduce_ref, expand_ref):
     total = jnp.sum(sums_ref[...], axis=0)
-    groups = reduce_ref.shape[0] // 128
+    groups = reduce_ref.shape[1] // 128
     mean = jnp.concatenate([total[group : group + 1] for group in range(groups)], axis=1) / cells
-    inner = jnp.sum(jnp.dot(thirds(mean), reduce_ref[...], preferred_element_type=F32), axis=0, keepdims=True)
+    inner = lax.dot_general(
+        thirds(mean), reduce_ref[...], (((1,), (1,)), ((), ())), preferred_element_type=F32
+    )
+    inner = jnp.sum(inner, axis=0, keepdims=True)
     inner = erf_gelu(inner)
     outer = jnp.sum(jnp.dot(thirds(inner), expand_ref[...], preferred_element_type=F32), axis=0, keepdims=True)
     return 1.0 / (1.0 + jnp.exp(-outer))
@@ -448,13 +455,13 @@
             pltpu.VMEM((rows + 2, round_up(cols + 2, 8), dim), F32),
             pltpu.VMEM((stage, dim), F32),
         ],
-        compiler_params=params(28),
+        compiler_params=params(28 if level == 0 else 20),
         cost_estimate=cost(400 * rows * cols * dim, 6 * rows * cols * dim),
         name="activate",
     )(tile, *rims, kernels)
 
 
-def mix0_kernel(cells, before, after, pos, sums, red, exp, mix, g_ref, rest, x_out, to_right, to_left, gates, z, line, keep_r, keep_l):
+def mix0_kernel(cells, before, after, sums, red, exp, mix, g_ref, rest, x_out, to_right, to_left, gates, z, line, keep_r, keep_l):
     step, cols, dim = g_ref.shape
     high, wide, _ = x_out.shape
     turn = pl.program_id(0)
@@ -463,6 +470,7 @@
     def _():
         gates[...] = jnp.broadcast_to(gate_row(sums, cells, red, exp), gates.shape)
 
+    pos = position()
     bounds = (jnp.where(pos[0] == 0, 1, 0), z.shape[0], jnp.where(pos[1] == 0, 1, 0), cols)
     mix_lines(g_ref, gates[:1, :], mix, rest, z, turn * step, bounds)
 
@@ -478,10 +486,10 @@
 
 
 def level_specs(sums, red, exp, mix, level):
-    return [POSITION, whole(sums), at_level(red, level), at_level(exp, level), at_level(mix, level)]
-
-
-def mix0(pos, sums, red, exp, mix, g, rest, cells, high, wide, before, after, step):
+    return [whole(sums), at_level(red, level), at_level(exp, level), at_level(mix, level)]
+
+
+def mix0(sums, red, exp, mix, g, rest, cells, high, wide, before, after, step):
     rows, cols, dim = g.shape
     block = pl.BlockSpec((step, cols, dim), lambda i: (i, 0, 0))
     outs = [
@@ -505,14 +513,15 @@
         compiler_params=params(32),
         cost_estimate=cost(2 * rows * cols * dim * dim, 6 * rows * cols * dim),
         name="mix0",
-    )(pos, sums, red, exp, mix, g, rest)
-
-
-def mix1_kernel(cells, size, before, pos, sums, red, exp, mix, g_ref, rest, kernel, g_out, rest_out, part, z, line, padded):
+    )(sums, red, exp, mix, g, rest)
+
+
+def mix1_kernel(cells, size, before, sums, red, exp, mix, g_ref, rest, kernel, g_out, rest_out, part, z, line, padded):
     rows, cols, dim = g_ref.shape
     side_r, side_c, map_side = size
     gate = gate_row(sums, cells, red, exp)
     shift = before - 1
+    pos = position()
     row_low = shift - pos[0] * side_r
     col_low = shift - pos[1] * side_c
     mix_lines(g_ref, gate, mix, rest, z, 0, (row_low, row_low + map_side, col_low, col_low + map_side))
@@ -530,7 +539,7 @@
     conv_gelu(padded, kernel, g_out, (1, 1 + side_r // 2), (1, 1 + side_c // 2), part)
 
 
-def mix1(pos, sums, red, exp, mix, g, rest, kernels, cells, size, before):
+def mix1(sums, red, exp, mix, g, rest, kernels, cells, size, before):
     rows, cols, dim = g.shape
     out_rows, out_cols = (rows - 1) // 2 - 2, round_up((cols - 1) // 2 - 2, 8)
     outs = [
@@ -549,15 +558,16 @@
             pltpu.VMEM((dim // 128, cols, 128), F32),
             pltpu.VMEM((out_rows + 2, round_up(out_cols + 2, 8), dim), F32),
         ],
-        compiler_params=params(32),
+        compiler_params=params(18),
         cost_estimate=cost(2 * rows * cols * dim * dim, 6 * rows * cols * dim),
         name="mix1",
-    )(pos, sums, red, exp, mix, g, rest, kernels)
-
-
-def mix2_kernel(cells, high, wide, pos, sums, red, exp, mix, g_ref, rest, x_out, z, line, keep):
+    )(sums, red, exp, mix, g, rest, kernels)
+
+
+def mix2_kernel(cells, high, wide, sums, red, exp, mix, g_ref, rest, x_out, z, line, keep):
     rows, cols, dim = g_ref.shape
     gate = gate_row(sums, cells, red, exp)
+    pos = position()
     bounds = (jnp.where(pos[0] == 0, 1, 0), rows, jnp.where(pos[1] == 0, 1, 0), cols)
     mix_lines(g_ref, gate, mix, rest, z, 0, bounds)
     for i in range(high):
@@ -565,7 +575,7 @@
     x_out[...] = jnp.broadcast_to(keep[...].astype(BF), x_out.shape)
 
 
-def mix2(pos, sums, red, exp, mix, g, rest, cells, high, wide, copies):
+def mix2(sums, red, exp, mix, g, rest, cells, high, wide, copies):
     rows, cols, dim = g.shape
     out = jax.ShapeDtypeStruct((copies, high * wide, dim), BF)
     return pl.pallas_call(
@@ -579,17 +589,17 @@
             pltpu.VMEM((dim // 128, cols, 128), F32),
             pltpu.VMEM((high * wide, dim), F32),
         ],
-        compiler_params=params(24),
+        compiler_params=params(10),
         cost_estimate=cost(2 * rows * cols * dim * dim, 6 * rows * cols * dim),
         name="mix2",
-    )(pos, sums, red, exp, mix, g, rest)
+    )(sums, red, exp, mix, g, rest)
 
 
 def everyones(copies):
     return lax.all_to_all(copies, "tile", 0, 0, tiled=True)
 
 
-def query_slab(tile_map, pos, dw_kernel, se_reduce, se_expand, mix_weight, keys_of):
+def query_slab(tile_map, dw_kernel, se_reduce, se_expand, mix_weight, keys_of):
     high, wide, dim = tile_map.shape
     tiles = lax.axis_size("tile")
     cells = high * wide * tiles
@@ -597,16 +607,16 @@
     rims, first = exchange_rims(tile_map, side_pieces(tile_map, 2, 1), 2, 1, lambda held: keys_of(0, held))
     g, rest, part = activate(tile_map, rims, dw_kernel, 0, 2, 1, 11)
     coarse, to_right, to_left = mix0(
-        pos, everyones(part), se_reduce, se_expand, mix_weight, g, rest, cells, high // 2, wide // 2, 6, 3, 11
+        everyones(part), se_reduce, se_expand, mix_weight, g, rest, cells, high // 2, wide // 2, 6, 3, 11
     )
     rims, second = exchange_rims(coarse, (to_right, to_left), 6, 3, lambda held: keys_of(1, held))
     g, rest, part = activate(coarse, rims, dw_kernel, 1, 6, 3, high // 2 + 7)
     size = (high // 2, wide // 2, high // 2 * (tiles // TILE_COLS))
     g, rest, part = mix1(
-        pos, everyones(part), se_reduce, se_expand, mix_weight, g, rest, dw_kernel, cells // 4, size, 6
+        everyones(part), se_reduce, se_expand, mix_weight, g, rest, dw_kernel, cells // 4, size, 6
     )
     query = mix2(
-        pos, everyones(part), se_reduce, se_expand, mix_weight, g, rest, cells // 16, high // 8, wide // 8, group
+        everyones(part), se_reduce, se_expand, mix_weight, g, rest, cells // 16, high // 8, wide // 8, group
     )
     groups = [list(range(group * x, group * x + group)) for x in range(tiles // group)]
     slab = lax.all_to_all(query, "tile", 0, 0, tiled=True, axis_index_groups=groups)
@@ -626,28 +636,19 @@
     proj_bias,
 ):
     tile_map = features[0]
-    dim = tile_map.shape[-1]
-    position = lax.axis_index("tile")
-    pos = jnp.stack([position // TILE_COLS, position % TILE_COLS]).astype(jnp.int32)
-    gain, kv_row, proj_row = norm_gain.reshape(1, dim), kv_bias.reshape(1, 2 * dim), proj_bias.reshape(1, dim)
+    se_reduce = jnp.swapaxes(se_reduce, 1, 2)
 
     def keys_of(window, held):
-        return keys_values(after_these(tile_map, held), gain, kv_weight, kv_row, window)
-
-    slab, (kt0, vt0), (kt1, vt1) = query_slab(
-        tile_map, pos, dw_kernel, se_reduce, se_expand, mix_weight, keys_of
-    )
-    slabs = lax.axis_size("tile") // (2 * TILE_COLS)
-    own = position // (2 * TILE_COLS)
-    others = []
-    for step in range(1, slabs):
-        pairs = [(t, t ^ 2 * TILE_COLS * step) for t in range(lax.axis_size("tile"))]
-        others.append(lax.ppermute(slab, "tile", pairs))
-    keys, values = (kt0, kt1), (vt0, vt1)
-    place = jnp.stack([own]).astype(jnp.int32)
-    started = attention(place, [slab], keys, values, tile_map, proj_weight, proj_row)
-    place = jnp.stack([own ^ step for step in range(1, slabs)]).astype(jnp.int32)
-    return attention(place, others, keys, values, tile_map, proj_weight, proj_row, started)[None]
+        return keys_values(after_these(tile_map, held), norm_gain, kv_weight, kv_bias, window)
+
+    slab, (kt0, vt0), (kt1, vt1) = query_slab(tile_map, dw_kernel, se_reduce, se_expand, mix_weight, keys_of)
+    tiles = lax.axis_size("tile")
+    group = 2 * TILE_COLS
+    steps = tuple(range(1, tiles // group))
+    others = [lax.ppermute(slab, "tile", [(t, t ^ group * step) for t in range(tiles)]) for step in steps]
+    rest = ((kt0, kt1), (vt0, vt1), tile_map, proj_weight, proj_bias)
+    started = attention((0,), [slab], *rest)
+    return attention(steps, others, *rest, started)[None]
 
 
 def solution(mesh):

time: 213 us -> 184 us (0.86)
  blocking collectives: 26.9 us -> 54.9 us
  local copies, waits for them, and re-layouts: 29 us -> 3.09 us
  starting transfers between devices: 35.4 us -> 22.7 us
  waiting for transfers between devices: 24.3 us -> 15.5 us
  Pallas kernels: 95.5 us -> 86.8 us
    unnamed x53 -> x26, local copies, waits for them, and re-layouts: 29 us -> 3.09 us
    all_to_all x2 -> x3, blocking collectives: 26.9 us -> 43.6 us  [everyones(): return lax.all_to_all(copies, 'tile', 0, 0, tiled=True)]
    all_to_all x2 -> x0, waiting for transfers between devices: 14.2 us -> none  [the longest x1 8.75 us: query_slab(): lax.all_to_all(query, 'tile', 0, 0, tiled=True, axis_index_groups=groups)]
    all_to_all x2 -> x0, starting transfers between devices: 12.5 us -> none  [the longest x1 9.07 us: everyones(): return lax.all_to_all(copies, 'tile', 0, 0, tiled=True)]
    all_to_all x0 -> x1, blocking collectives: none -> 11.3 us  [query_slab(): lax.all_to_all(query, 'tile', 0, 0, tiled=True, axis_index_groups=groups)]
    pallas_call x2, Pallas kernels: 22.2 us -> 15.9 us  [activate(): pl.pallas_call(functools.partial(act_kernel, before, after), grid=(rows /...]
    ppermute x3, waiting for transfers between devices: 0.01 us -> 3.19 us  [body(): lax.ppermute(slab, 'tile', [(t, t ^ group * step) for t in range(tiles)])]
    ppermute x8, waiting for transfers between devices: 10.1 us -> 12.3 us  [moved_by(): return lax.ppermute(value, 'tile', pairs)]
  transfers between devices with their start and end apart: 13 -> 11, of which waited for: 7 -> 7; matrix products, arithmetic and copies ran while one was open for 1% -> 0% of each run, Pallas kernels for 11% -> 13%
where the time goes in v3:
time: 184 us; the launch traced here: 183 us
  Pallas kernels  86.8 us (47%)
  blocking collectives  54.9 us (30%)
  starting transfers between devices  22.7 us (12%)
  waiting for transfers between devices  15.5 us (8%)
  local copies, waits for them, and re-layouts  3.09 us (2%)
    pallas_call x2, Pallas kernels, attention(): pl.pallas_call(functools.partial(attention_kernel, steps), in_specs=[VM]...  51.6 us
    all_to_all x3, blocking collectives, everyones(): return lax.all_to_all(copies, 'tile', 0, 0, tiled=True)  43.6 us
    ppermute x8, starting transfers between devices, moved_by(): return lax.ppermute(value, 'tile', pairs)  18.6 us
    pallas_call x2, Pallas kernels, activate(): pl.pallas_call(functools.partial(act_kernel, before, after), grid=(rows /...  15.9 us
    ppermute x8, waiting for transfers between devices, moved_by(): return lax.ppermute(value, 'tile', pairs)  12.3 us
    all_to_all x1, blocking collectives, query_slab(): lax.all_to_all(query, 'tile', 0, 0, tiled=True, axis_index_groups=groups)  11.3 us
    pallas_call x2, Pallas kernels, keys_values(): pl.pallas_call(kv_kernel, grid=(win // step,), in_specs=[pl.BlockSpec((st...  9.62 us
    pallas_call x1, Pallas kernels, mix0(): pl.pallas_call(functools.partial(mix0_kernel, cells, before, after), grid...  5.09 us
  transfers between devices with their start and end apart: 11, of which 7 were waited for; matrix products, arithmetic and copies ran while one was open for 0% of the time, Pallas kernels for 13%

profile of v3, /device:TPU:0, one launch (start us, length us, event | category | flops | bytes accessed | tf_op | source)
XLA Modules:
  0.0 183.4 jit_solution(17642950835444972878)
XLA Ops:
  0.0 1.9 %copy-done = bf16[1,32,64,768]{3,2,1,0:T(8,128)(2,1)S(1)} copy-done((bf16[1,32,64,768]{3,2,1,0:T(8,128)(2,1)S(1)}, bf16[1,32,64,768]{3,2,1,0:T(8,128)(2,1)}, u32[]{:S(2)}) %copy-start) | copy-done | bytes 3145752
  2.0 1.3 collective-permute-start
  3.4 1.6 collective-permute-start.1
  4.9 4.2 %collective-permute-done.1.rest_1_.r_ref = bf16[32,768]{1,0:T(8,128)(2,1)S(1)} collective-permute-done((bf16[32,768]{1,0:T(8,128)(2,1)S(1)}, bf16[32,768]{1,0:T(8,128)(2,1)S(1)}, u32[]{:S(2)}, u32[]{:S(2)}) %collective-permute-start.1) | collective-permute-done | bytes 49184 | tf_op jit(solution)/shard_map/ppermute | solution.py:298
  9.2 5.5 %collective-permute-start.2 = (bf16[144,768]{1,0:T(8,128)(2,1)S(1)}, bf16[144,768]{1,0:T(8,128)(2,1)S(1)}, u32[]{:S(2)}, u32[]{:S(2)}) collective-permute-start(bf16[144,768]{1,0:T(8,128)(2,1)S(1)} %get-tuple-element.39), channel_id=1, source_target_pairs={{0,4},{1,5},{2,6},{3,7},{4,8},{5,9},{6,10},{7,11},{8,12},{9,13},{1... | collective-permute-start | bytes 663560 | tf_op jit(solution)/shard_map/ppermute | solution.py:298
  14.8 1.4 collective-permute-start.3
  16.2 4.8 %keys_values.2 = (bf16[6,1024,128]{2,1,0:T(8,128)(2,1)S(1)}, bf16[768,1024]{1,0:T(8,128)(2,1)S(1)}) custom-call(bf16[32,64,768]{2,1,0:T(8,128)(2,1)S(1)} %bitcast.8, f32[768]{0:T(1024)S(1)} %copy-done.9, bf16[768,1536]{1,0:T(8,128)(2,1)S(1)} %copy-done.6, f32[1536]{0:T(1024)S(1)} %copy-done.8), custom_call_target="tpu_custom_call" | custom-call | flops 4831838208 | bytes 8388608 | tf_op jit(solution)/shard_map/keys_values/pallas_call | solution.py:41
  21.1 1.1 copy-done.11
  22.2 0.9 collective-permute-done.3.b_ref
  23.2 11.3 %activate.2 = (f32[33,72,768]{2,1,0:T(8,128)S(1)}, bf16[33,72,768]{2,1,0:T(8,128)(2,1)S(1)}, f32[32,8,128]{2,1,0:T(8,128)S(1)}) custom-call(bf16[32,64,768]{2,1,0:T(8,128)(2,1)S(1)} %bitcast.9, bf16[64,768]{1,0:T(8,128)(2,1)S(1)} %collective-permute-done.rest_0_.l_ref, bf16[32,768]{1,0:T(8,128)(2,1)S(1)} %collective-permute-done.1.rest_1_.r_ref, ...), custom_call_target="tpu_custom_call" | custom-call | flops 729907200 | bytes 10948608 | tf_op jit(solution)/shard_map/activate/pallas_call | solution.py:444
  34.5 16.7 %all_to_all.20.sums = f32[32,8,128]{2,1,0:T(8,128)S(1)} all-to-all(f32[32,8,128]{2,1,0:T(8,128)S(1)} %get-tuple-element.46), channel_id=1, replica_groups=mesh['scene'=4,'tile'=32] {'tile'}, dimensions={0} | all-to-all | bytes 262144 | tf_op jit(solution)/shard_map/all_to_all | solution.py:599
  51.2 5.1 %mix0.1 = (bf16[16,32,768]{2,1,0:T(8,128)(2,1)S(1)}, bf16[96,768]{1,0:T(8,128)(2,1)S(1)}, bf16[48,768]{1,0:T(8,128)(2,1)S(1)}) custom-call(f32[32,8,128]{2,1,0:T(8,128)S(1)} %all_to_all.20.sums, bf16[3,192,768]{2,1,0:T(8,128)(2,1)S(1)} %bitcast.13, bf16[3,192,768]{2,1,0:T(8,128)(2,1)S(1)} %copy-done.4, bf16[3,768,768]{2,1,0:T(8,128)(2,1)S(1)} %copy-done.2, ...), custom_call_target="tpu_custom_call" | custom-call | flops 2802843648 | bytes 10948608 | tf_op jit(solution)/shard_map/mix0/pallas_call | solution.py:500
  56.3 2.0 %collective-permute-start.4 = (bf16[96,768]{1,0:T(8,128)(2,1)S(1)}, bf16[96,768]{1,0:T(8,128)(2,1)S(1)}, u32[]{:S(2)}, u32[]{:S(2)}) collective-permute-start(bf16[96,768]{1,0:T(8,128)(2,1)S(1)} %get-tuple-element.50), channel_id=1, source_target_pairs={{0,1},{1,2},{2,3},{4,5},{5,6},{6,7},{8,9},{9,10},{10,11},{12,13},{... | collective-permute-start | bytes 442376 | tf_op jit(solution)/shard_map/ppermute | solution.py:298
  58.3 1.3 collective-permute-start.5
  59.6 1.9 %collective-permute-done.5.rest_1_.r_ref = bf16[48,768]{1,0:T(8,128)(2,1)S(1)} collective-permute-done((bf16[48,768]{1,0:T(8,128)(2,1)S(1)}, bf16[48,768]{1,0:T(8,128)(2,1)S(1)}, u32[]{:S(2)}, u32[]{:S(2)}) %collective-permute-start.5) | collective-permute-done | bytes 73760 | tf_op jit(solution)/shard_map/ppermute | solution.py:298
  61.8 4.1 %collective-permute-start.6 = (bf16[256,768]{1,0:T(8,128)(2,1)S(1)}, bf16[256,768]{1,0:T(8,128)(2,1)S(1)}, u32[]{:S(2)}, u32[]{:S(2)}) collective-permute-start(bf16[256,768]{1,0:T(8,128)(2,1)S(1)} %get-tuple-element.52), channel_id=1, source_target_pairs={{0,4},{1,5},{2,6},{3,7},{4,8},{5,9},{6,10},{7,11},{8,12},{9,13},{1... | collective-permute-start | bytes 1179656 | tf_op jit(solution)/shard_map/ppermute | solution.py:298
  65.8 1.5 collective-permute-start.7
  67.3 4.8 %keys_values.3 = (bf16[6,1024,128]{2,1,0:T(8,128)(2,1)S(1)}, bf16[768,1024]{1,0:T(8,128)(2,1)S(1)}) custom-call(bf16[32,64,768]{2,1,0:T(8,128)(2,1)S(1)} %bitcast.10, f32[768]{0:T(1024)S(1)} %copy-done.9, bf16[768,1536]{1,0:T(8,128)(2,1)S(1)} %copy-done.6, f32[1536]{0:T(1024)S(1)} %copy-done.8), custom_call_target="tpu_custom_call" | custom-call | flops 4831838208 | bytes 8388608 | tf_op jit(solution)/shard_map/keys_values/pallas_call | solution.py:41
  72.1 3.0 %collective-permute-done.7.b_ref = bf16[128,768]{1,0:T(8,128)(2,1)S(1)} collective-permute-done((bf16[128,768]{1,0:T(8,128)(2,1)S(1)}, bf16[128,768]{1,0:T(8,128)(2,1)S(1)}, u32[]{:S(2)}, u32[]{:S(2)}) %collective-permute-start.7) | collective-permute-done | bytes 196640 | tf_op jit(solution)/shard_map/ppermute | solution.py:298
  75.2 2.2 %collective-permute-done.6.a_ref = bf16[256,768]{1,0:T(8,128)(2,1)S(1)} collective-permute-done((bf16[256,768]{1,0:T(8,128)(2,1)S(1)}, bf16[256,768]{1,0:T(8,128)(2,1)S(1)}, u32[]{:S(2)}, u32[]{:S(2)}) %collective-permute-start.6) | collective-permute-done | bytes 393248 | tf_op jit(solution)/shard_map/ppermute | solution.py:298
  77.4 4.6 %activate.3 = (f32[23,40,768]{2,1,0:T(8,128)S(1)}, bf16[23,40,768]{2,1,0:T(8,128)(2,1)S(1)}, f32[32,8,128]{2,1,0:T(8,128)S(1)}) custom-call(bf16[16,32,768]{2,1,0:T(8,128)(2,1)S(1)} %get-tuple-element.49.top_ref.low_ref.x_ref, bf16[96,768]{1,0:T(8,128)(2,1)S(1)} %collective-permute-done.4.rest_0_.l_ref, ...), custom_call_target="tpu_custom_call" | custom-call | flops 282624000 | bytes 4239360 | tf_op jit(solution)/shard_map/activate/pallas_call | solution.py:444
  82.0 15.6 %all_to_all.21.sums = f32[32,8,128]{2,1,0:T(8,128)S(1)} all-to-all(f32[32,8,128]{2,1,0:T(8,128)S(1)} %get-tuple-element.59), channel_id=1, replica_groups=mesh['scene'=4,'tile'=32] {'tile'}, dimensions={0} | all-to-all | bytes 262144 | tf_op jit(solution)/shard_map/all_to_all | solution.py:599
  97.6 3.2 %mix1.1 = (f32[9,24,768]{2,1,0:T(8,128)S(1)}, bf16[9,24,768]{2,1,0:T(8,128)(2,1)S(1)}, f32[32,8,128]{2,1,0:T(8,128)S(1)}) custom-call(f32[32,8,128]{2,1,0:T(8,128)S(1)} %all_to_all.21.sums, bf16[3,192,768]{2,1,0:T(8,128)(2,1)S(1)} %bitcast.14, bf16[3,192,768]{2,1,0:T(8,128)(2,1)S(1)} %copy-done.4, bf16[3,768,768]{2,1,0:T(8,128)(2,1)S(1)} %copy-done.2, ...), custom_call_target="tpu_custom_call" | custom-call | flops 1085276160 | bytes 4239360 | tf_op jit(solution)/shard_map/mix1/pallas_call | solution.py:550
  100.8 11.3 %all_to_all.22.sums = f32[32,8,128]{2,1,0:T(8,128)S(1)} all-to-all(f32[32,8,128]{2,1,0:T(8,128)S(1)} %get-tuple-element.62), channel_id=1, replica_groups=mesh['scene'=4,'tile'=32] {'tile'}, dimensions={0} | all-to-all | bytes 262144 | tf_op jit(solution)/shard_map/all_to_all | solution.py:599
  112.1 0.9 mix2.1
  113.0 11.3 %all_to_all.23 = bf16[8,32,768]{2,1,0:T(8,128)(2,1)S(1)} all-to-all(bf16[8,32,768]{2,1,0:T(8,128)(2,1)S(1)} %mix2.1), channel_id=1, replica_groups={{0,1,2,3,4,5,6,7},{8,9,10,11,12,13,14,15},{16,17,18,19,20,21,22,23},{24..., dimensions={0} | all-to-all | bytes 786432 | tf_op jit(solution)/shard_map/all_to_all | solution.py:622
  124.3 1.1 collective-permute-start.10
  125.5 1.5 collective-permute-start.9
  127.0 1.5 collective-permute-start.8
  128.5 13.6 %attention.2.refs_10_ = bf16[32,64,768]{2,1,0:T(8,128)(2,1)} custom-call(bf16[256,768]{1,0:T(8,128)(2,1)S(1)} %bitcast.19, bf16[6,1024,128]{2,1,0:T(8,128)(2,1)S(1)} %get-tuple-element.65.refs_1_.refs_3_, bf16[6,1024,128]{2,1,0:T(8,128)(2,1)S(1)} %get-tuple-element.66.refs_2_.refs_4_, bf16[768,1024]{1,0:T(8,128)(2,1)S(1)} %copy-done.12, ...), custom_call_target="tpu_custom_call" | custom-call | flops 12884901888 | bytes 12582912 | tf_op jit(solution)/shard_map/attention/pallas_call | solution.py:152
  142.1 2.6 %collective-permute-done.10.refs_2_ = bf16[256,768]{1,0:T(8,128)(2,1)S(1)} collective-permute-done((bf16[256,768]{1,0:T(8,128)(2,1)S(1)}, bf16[256,768]{1,0:T(8,128)(2,1)S(1)}, u32[]{:S(2)}, u32[]{:S(2)}) %collective-permute-start.10) | collective-permute-done | bytes 393248 | tf_op jit(solution)/shard_map/ppermute | solution.py:648
  145.3 38.0 %attention.3 = bf16[32,64,768]{2,1,0:T(8,128)(2,1)} custom-call(bf16[256,768]{1,0:T(8,128)(2,1)S(1)} %collective-permute-done.8.refs_0_, bf16[256,768]{1,0:T(8,128)(2,1)S(1)} %collective-permute-done.9.refs_1_, bf16[256,768]{1,0:T(8,128)(2,1)S(1)} %collective-permute-done.10.refs_2_, ...), custom_call_target="tpu_custom_call", output_to_operand_aliasing={{}: (10, {})} | custom-call | flops 38654705664 | bytes 12582912 | tf_op jit(solution)/shard_map/attention/pallas_call | solution.py:152
  (32 shorter events, 1.2 us)
Async XLA Ops:
  0.0 1.9 %copy-start = (bf16[1,32,64,768]{3,2,1,0:T(8,128)(2,1)S(1)}, bf16[1,32,64,768]{3,2,1,0:T(8,128)(2,1)}, u32[]{:S(2)}) copy-start(bf16[1,32,64,768]{3,2,1,0:T(8,128)(2,1)} %param.10) | copy-start | bytes 9437188
  2.0 7.1 %collective-permute-start = (bf16[64,768]{1,0:T(8,128)(2,1)S(1)}, bf16[64,768]{1,0:T(8,128)(2,1)S(1)}, u32[]{:S(2)}, u32[]{:S(2)}) collective-permute-start(bf16[64,768]{1,0:T(8,128)(2,1)S(1)} %get-tuple-element.37), channel_id=1, source_target_pairs={{0,1},{1,2},{2,3},{4,5},{5,6},{6,7},{8,9},{9,10},{10,11},{12,13},{... | collective-permute-start | bytes 294920 | tf_op jit(solution)/shard_map/ppermute | solution.py:298
  3.3 12.9 %copy-start.1 = (bf16[1,32,64,768]{3,2,1,0:T(8,128)(2,1)S(1)}, bf16[1,32,64,768]{3,2,1,0:T(8,128)(2,1)}, u32[]{:S(2)}) copy-start(bf16[1,32,64,768]{3,2,1,0:T(8,128)(2,1)} %param.10) | copy-start | bytes 9437188
  3.3 12.9 %copy-start.6 = (bf16[768,1536]{1,0:T(8,128)(2,1)S(1)}, bf16[768,1536]{1,0:T(8,128)(2,1)}, u32[]{:S(2)}) copy-start(bf16[768,1536]{1,0:T(8,128)(2,1)} %w_ref.3) | copy-start | bytes 7077892
  3.4 12.9 %copy-start.8 = (f32[1536]{0:T(1024)S(1)}, f32[1536]{0:T(1024)}, u32[]{:S(2)}) copy-start(f32[1536]{0:T(1024)} %b_ref.3) | copy-start | bytes 18436
  3.4 12.9 %copy-start.9 = (f32[768]{0:T(1024)S(1)}, f32[768]{0:T(1024)}, u32[]{:S(2)}) copy-start(f32[768]{0:T(1024)} %gain_ref.3) | copy-start | bytes 9220
  3.4 5.8 %collective-permute-start.1 = (bf16[32,768]{1,0:T(8,128)(2,1)S(1)}, bf16[32,768]{1,0:T(8,128)(2,1)S(1)}, u32[]{:S(2)}, u32[]{:S(2)}) collective-permute-start(bf16[32,768]{1,0:T(8,128)(2,1)S(1)} %get-tuple-element.38), channel_id=1, source_target_pairs={{1,0},{2,1},{3,2},{5,4},{6,5},{7,6},{9,8},{10,9},{11,10},{13,12},{... | collective-permute-start | bytes 147464 | tf_op jit(solution)/shard_map/ppermute | solution.py:298
  9.2 13.9 %collective-permute-start.2 = (bf16[144,768]{1,0:T(8,128)(2,1)S(1)}, bf16[144,768]{1,0:T(8,128)(2,1)S(1)}, u32[]{:S(2)}, u32[]{:S(2)}) collective-permute-start(bf16[144,768]{1,0:T(8,128)(2,1)S(1)} %get-tuple-element.39), channel_id=1, source_target_pairs={{0,4},{1,5},{2,6},{3,7},{4,8},{5,9},{6,10},{7,11},{8,12},{9,13},{1... | collective-permute-start | bytes 663560 | tf_op jit(solution)/shard_map/ppermute | solution.py:298
  14.7 8.4 %copy-start.5 = (bf16[3,3,3,768]{3,2,1,0:T(4,128)(2,1)S(1)}, bf16[3,3,3,768]{3,2,1,0:T(4,128)(2,1)}, u32[]{:S(2)}) copy-start(bf16[3,3,3,768]{3,2,1,0:T(4,128)(2,1)} %kernel.1) | copy-start | bytes 124420
  14.8 8.4 %collective-permute-start.3 = (bf16[80,768]{1,0:T(8,128)(2,1)S(1)}, bf16[80,768]{1,0:T(8,128)(2,1)S(1)}, u32[]{:S(2)}, u32[]{:S(2)}) collective-permute-start(bf16[80,768]{1,0:T(8,128)(2,1)S(1)} %get-tuple-element.40), channel_id=1, source_target_pairs={{4,0},{5,1},{6,2},{7,3},{8,4},{9,5},{10,6},{11,7},{12,8},{13,9},{1... | collective-permute-start | bytes 368648 | tf_op jit(solution)/shard_map/ppermute | solution.py:298
  16.2 35.0 %copy-start.3 = (bf16[3,768,192]{1,2,0:T(8,128)(2,1)S(1)}, bf16[3,768,192]{1,2,0:T(8,128)(2,1)}, u32[]{:S(2)}) copy-start(bf16[3,768,192]{1,2,0:T(8,128)(2,1)} %param.12) | copy-start | bytes 2654212
  16.2 35.0 %copy-start.4 = (bf16[3,192,768]{2,1,0:T(8,128)(2,1)S(1)}, bf16[3,192,768]{2,1,0:T(8,128)(2,1)}, u32[]{:S(2)}) copy-start(bf16[3,192,768]{2,1,0:T(8,128)(2,1)} %exp.5) | copy-start | bytes 2654212
  21.1 1.1 copy-start.11
  22.2 29.0 %copy-start.2 = (bf16[3,768,768]{2,1,0:T(8,128)(2,1)S(1)}, bf16[3,768,768]{2,1,0:T(8,128)(2,1)}, u32[]{:S(2)}) copy-start(bf16[3,768,768]{2,1,0:T(8,128)(2,1)} %mix.5) | copy-start | bytes 10616836
  56.3 5.2 %collective-permute-start.4 = (bf16[96,768]{1,0:T(8,128)(2,1)S(1)}, bf16[96,768]{1,0:T(8,128)(2,1)S(1)}, u32[]{:S(2)}, u32[]{:S(2)}) collective-permute-start(bf16[96,768]{1,0:T(8,128)(2,1)S(1)} %get-tuple-element.50), channel_id=1, source_target_pairs={{0,1},{1,2},{2,3},{4,5},{5,6},{6,7},{8,9},{9,10},{10,11},{12,13},{... | collective-permute-start | bytes 442376 | tf_op jit(solution)/shard_map/ppermute | solution.py:298
  58.3 3.2 %collective-permute-start.5 = (bf16[48,768]{1,0:T(8,128)(2,1)S(1)}, bf16[48,768]{1,0:T(8,128)(2,1)S(1)}, u32[]{:S(2)}, u32[]{:S(2)}) collective-permute-start(bf16[48,768]{1,0:T(8,128)(2,1)S(1)} %get-tuple-element.51), channel_id=1, source_target_pairs={{1,0},{2,1},{3,2},{5,4},{6,5},{7,6},{9,8},{10,9},{11,10},{13,12},{... | collective-permute-start | bytes 221192 | tf_op jit(solution)/shard_map/ppermute | solution.py:298
  61.8 15.6 %collective-permute-start.6 = (bf16[256,768]{1,0:T(8,128)(2,1)S(1)}, bf16[256,768]{1,0:T(8,128)(2,1)S(1)}, u32[]{:S(2)}, u32[]{:S(2)}) collective-permute-start(bf16[256,768]{1,0:T(8,128)(2,1)S(1)} %get-tuple-element.52), channel_id=1, source_target_pairs={{0,4},{1,5},{2,6},{3,7},{4,8},{5,9},{6,10},{7,11},{8,12},{9,13},{1... | collective-permute-start | bytes 1179656 | tf_op jit(solution)/shard_map/ppermute | solution.py:298
  65.8 9.3 %collective-permute-start.7 = (bf16[128,768]{1,0:T(8,128)(2,1)S(1)}, bf16[128,768]{1,0:T(8,128)(2,1)S(1)}, u32[]{:S(2)}, u32[]{:S(2)}) collective-permute-start(bf16[128,768]{1,0:T(8,128)(2,1)S(1)} %get-tuple-element.53), channel_id=1, source_target_pairs={{4,0},{5,1},{6,2},{7,3},{8,4},{9,5},{10,6},{11,7},{12,8},{13,9},{1... | collective-permute-start | bytes 589832 | tf_op jit(solution)/shard_map/ppermute | solution.py:298
  112.1 16.3 %copy-start.7 = (bf16[768,768]{1,0:T(8,128)(2,1)S(1)}, bf16[768,768]{1,0:T(8,128)(2,1)}, u32[]{:S(2)}) copy-start(bf16[768,768]{1,0:T(8,128)(2,1)} %refs_8_.1) | copy-start | bytes 3538948
  112.1 16.3 %copy-start.10 = (f32[768]{0:T(1024)S(1)}, f32[768]{0:T(1024)}, u32[]{:S(2)}) copy-start(f32[768]{0:T(1024)} %refs_9_.1) | copy-start | bytes 9220
  112.1 16.3 %copy-start.12 = (bf16[768,1024]{1,0:T(8,128)(2,1)S(1)}, bf16[768,1024]{1,0:T(8,128)(2,1)}, u32[]{:S(2)}) copy-start(bf16[768,1024]{1,0:T(8,128)(2,1)} %copy-done.11) | copy-start | bytes 4718596
  124.3 20.3 %collective-permute-start.10 = (bf16[256,768]{1,0:T(8,128)(2,1)S(1)}, bf16[256,768]{1,0:T(8,128)(2,1)S(1)}, u32[]{:S(2)}, u32[]{:S(2)}) collective-permute-start(bf16[256,768]{1,0:T(8,128)(2,1)S(1)} %bitcast.16), channel_id=1, source_target_pairs={{0,24},{1,25},{2,26},{3,27},{4,28},{5,29},{6,30},{7,31},{8,16},{9,... | collective-permute-start | bytes 1179656 | tf_op jit(solution)/shard_map/ppermute | solution.py:648
  125.5 19.2 %collective-permute-start.9 = (bf16[256,768]{1,0:T(8,128)(2,1)S(1)}, bf16[256,768]{1,0:T(8,128)(2,1)S(1)}, u32[]{:S(2)}, u32[]{:S(2)}) collective-permute-start(bf16[256,768]{1,0:T(8,128)(2,1)S(1)} %bitcast.17), channel_id=1, source_target_pairs={{0,16},{1,17},{2,18},{3,19},{4,20},{5,21},{6,22},{7,23},{8,24},{9,... | collective-permute-start | bytes 1179656 | tf_op jit(solution)/shard_map/ppermute | solution.py:648
  127.0 18.3 %collective-permute-start.8 = (bf16[256,768]{1,0:T(8,128)(2,1)S(1)}, bf16[256,768]{1,0:T(8,128)(2,1)S(1)}, u32[]{:S(2)}, u32[]{:S(2)}) collective-permute-start(bf16[256,768]{1,0:T(8,128)(2,1)S(1)} %bitcast.18), channel_id=1, source_target_pairs={{0,8},{1,9},{2,10},{3,11},{4,12},{5,13},{6,14},{7,15},{8,0},{9,1},... | collective-permute-start | bytes 1179656 | tf_op jit(solution)/shard_map/ppermute | solution.py:648

commit v4 on v3

--- a/solution.py
+++ b/solution.py
@@ -307,7 +307,7 @@
     right = moved_by(pieces[1], 0, -1)
     down, up = line_pieces(tile, left, right, before, after)
     above, below = moved_by(down, 1, 0), moved_by(up, -1, 0)
-    result = beside(down)
+    result = beside((left, right), down)
     above, below, *result = lax.optimization_barrier((above, below, *result))
     return (left, right, above, below), result
 
@@ -396,7 +396,7 @@
     return 1.0 / (1.0 + jnp.exp(-outer))
 
 
-def mix_lines(g_ref, gate, mix_ref, rest_ref, z_ref, first, bounds):
+def mix_lines(g_ref, gate, mix_ref, rest_ref, z_ref, lines, bounds):
     rows, cols, dim = g_ref.shape
     row_low, row_high, col_low, col_high = bounds
     column = lax.broadcasted_iota(jnp.int32, (cols, 1), 0)
@@ -405,8 +405,8 @@
     product = jnp.dot(u, mix_ref[...], preferred_element_type=F32).reshape(rows, cols, dim)
     for k in range(rows):
         z = (rest_ref[k].astype(F32) + product[k]).astype(BF).astype(F32)
-        keep = inside & (first + k >= row_low) & (first + k < row_high)
-        z_ref[first + k] = jnp.where(keep, z, -jnp.inf)
+        keep = inside & (lines[k] >= row_low) & (lines[k] < row_high)
+        z_ref[lines[k]] = jnp.where(keep, z, -jnp.inf)
 
 
 def pooled_line(z_ref, line_ref, i, count):
@@ -461,18 +461,139 @@
     )(tile, *rims, kernels)
 
 
-def mix0_kernel(cells, before, after, sums, red, exp, mix, g_ref, rest, x_out, to_right, to_left, gates, z, line, keep_r, keep_l):
+def fill_sides(x_ref, left_ref, right_ref, before, after, padded, stage):
+    high, wide, _ = x_ref.shape
+    full = before + wide + after
+
+    def line(r, _):
+        padded[r, before : before + wide, :] = x_ref[r].astype(F32)
+        return 0
+
+    lax.fori_loop(0, high, line, 0)
+    stage[: left_ref.shape[0], :] = left_ref[...].astype(F32)
+    for r in range(high):
+        padded[r, 0:before, :] = stage[r * before : r * before + before, :]
+    stage[: right_ref.shape[0], :] = right_ref[...].astype(F32)
+    for r in range(high):
+        padded[r, before + wide : full, :] = stage[r * after : r * after + after, :]
+
+
+def inner_kernel(before, after, x_ref, l_ref, r_ref, kernel_ref, g_ref, rest_ref, part_ref, padded, stage):
+    _, wide, _ = x_ref.shape
+    step = g_ref.shape[0]
+    turn = pl.program_id(0)
+
+    @pl.when(turn == 0)
+    def _():
+        fill_sides(x_ref, l_ref, r_ref, before, after, padded, stage)
+        part_ref[...] = jnp.zeros_like(part_ref)
+
+    block = padded.at[pl.ds(turn * step, step + 2)]
+    copy_centre(block, rest_ref)
+    conv_gelu(block, kernel_ref, g_ref, (0, step), (before - 1, before - 1 + wide), part_ref)
+
+
+def activate_inner(tile, left, right, kernels, before, after, step):
+    high, wide, dim = tile.shape
+    rows, cols = high - 2, round_up(wide + before + after - 2, 8)
+    copies = lax.axis_size("tile")
+    block = pl.BlockSpec((step, cols, dim), lambda i: (i, 0, 0))
+    return pl.pallas_call(
+        functools.partial(inner_kernel, before, after),
+        grid=(rows // step,),
+        in_specs=wholes(tile, left, right) + [at_level(kernels, 0)],
+        out_specs=[block, block, pl.BlockSpec((copies, 8, 128), lambda i: (0, 0, 0))],
+        out_shape=[
+            jax.ShapeDtypeStruct((rows, cols, dim), F32),
+            jax.ShapeDtypeStruct((rows, cols, dim), BF),
+            jax.ShapeDtypeStruct((copies, 8, 128), F32),
+        ],
+        scratch_shapes=[
+            pltpu.VMEM((high, round_up(cols + 2, 8), dim), F32),
+            pltpu.VMEM((max(left.shape[0], right.shape[0]), dim), F32),
+        ],
+        compiler_params=params(28),
+        cost_estimate=cost(400 * rows * cols * dim, 6 * rows * cols * dim),
+        name="activate_inner",
+    )(tile, left, right, kernels)
+
+
+def edge_kernel(high, top_ref, low_ref, l_ref, r_ref, a_ref, b_ref, kernel_ref, sum_ref, g_ref, rest_ref, part_ref, upper, lower, side_l, side_r, stage):
+    wide = top_ref.shape[1]
+    full = wide + 3
+    own = (1, 1 + wide)
+    side_l[...] = l_ref[...].astype(F32)
+    side_r[...] = r_ref[...].astype(F32)
+
+    def fill(padded, at, r, values):
+        padded[at, 0:2, :] = side_l[2 * r : 2 * r + 2, :]
+        padded[at, 2 : 2 + wide, :] = values.astype(F32)
+        padded[at, 2 + wide : full, :] = side_r[r : r + 1, :]
+
+    for k in range(2):
+        fill(upper, 2 + k, k, top_ref[k])
+        fill(lower, k, high - 2 + k, low_ref[k])
+    stage[: a_ref.shape[0], :] = a_ref[...].astype(F32)
+    for k in range(2):
+        upper[k, 0:full, :] = stage[k * full : k * full + full, :]
+    stage[: b_ref.shape[0], :] = b_ref[...].astype(F32)
+    lower[2, 0:full, :] = stage[0:full, :]
+    part_ref[...] = sum_ref[...]
+    copy_centre(upper, rest_ref.at[pl.ds(0, 2)])
+    copy_centre(lower, rest_ref.at[pl.ds(2, 1)])
+    conv_gelu(upper, kernel_ref, g_ref.at[pl.ds(0, 2)], (1, 2), own, part_ref)
+    conv_gelu(lower, kernel_ref, g_ref.at[pl.ds(2, 1)], (0, 1), own, part_ref)
+
+
+def activate_edge(tile, rims, kernels, part):
+    high, wide, dim = tile.shape
+    cols = round_up(wide + 1, 8)
+    padded = round_up(cols + 2, 8)
+    stage = max(r.shape[0] for r in rims)
+    left, right, above, below = rims
+    outs = [
+        jax.ShapeDtypeStruct((3, cols, dim), F32),
+        jax.ShapeDtypeStruct((3, cols, dim), BF),
+        jax.ShapeDtypeStruct(part.shape, F32),
+    ]
+    return pl.pallas_call(
+        functools.partial(edge_kernel, high),
+        grid=(1,),
+        in_specs=[
+            pl.BlockSpec((2, wide, dim), lambda i: (0, 0, 0)),
+            pl.BlockSpec((2, wide, dim), lambda i: (high // 2 - 1, 0, 0)),
+        ]
+        + wholes(*rims)
+        + [at_level(kernels, 0), whole(part)],
+        out_specs=wholes(*outs),
+        out_shape=outs,
+        scratch_shapes=[
+            pltpu.VMEM((4, padded, dim), F32),
+            pltpu.VMEM((3, padded, dim), F32),
+            pltpu.VMEM(left.shape, F32),
+            pltpu.VMEM(right.shape, F32),
+            pltpu.VMEM((stage, dim), F32),
+        ],
+        compiler_params=params(12),
+        cost_estimate=cost(400 * 3 * cols * dim, 6 * 3 * cols * dim),
+        name="activate_edge",
+    )(tile, tile, *rims, kernels, part)
+
+
+def mix0_kernel(cells, before, after, sums, red, exp, mix, g_ref, rest, g_edge, rest_edge, x_out, to_right, to_left, gates, z, line, keep_r, keep_l):
     step, cols, dim = g_ref.shape
     high, wide, _ = x_out.shape
     turn = pl.program_id(0)
 
+    pos = position()
+    bounds = (jnp.where(pos[0] == 0, 1, 0), z.shape[0], jnp.where(pos[1] == 0, 1, 0), cols)
+
     @pl.when(turn == 0)
     def _():
         gates[...] = jnp.broadcast_to(gate_row(sums, cells, red, exp), gates.shape)
-
-    pos = position()
-    bounds = (jnp.where(pos[0] == 0, 1, 0), z.shape[0], jnp.where(pos[1] == 0, 1, 0), cols)
-    mix_lines(g_ref, gates[:1, :], mix, rest, z, turn * step, bounds)
+        mix_lines(g_edge, gates[:1, :], mix, rest_edge, z, (0, 1, z.shape[0] - 1), bounds)
+
+    mix_lines(g_ref, gates[:1, :], mix, rest, z, [2 + turn * step + k for k in range(step)], bounds)
 
     @pl.when(turn == pl.num_programs(0) - 1)
     def _():
@@ -489,7 +610,7 @@
     return [whole(sums), at_level(red, level), at_level(exp, level), at_level(mix, level)]
 
 
-def mix0(sums, red, exp, mix, g, rest, cells, high, wide, before, after, step):
+def mix0(sums, red, exp, mix, g, rest, edges, cells, high, wide, before, after, step):
     rows, cols, dim = g.shape
     block = pl.BlockSpec((step, cols, dim), lambda i: (i, 0, 0))
     outs = [
@@ -500,12 +621,12 @@
     return pl.pallas_call(
         functools.partial(mix0_kernel, cells, before, after),
         grid=(rows // step,),
-        in_specs=level_specs(sums, red, exp, mix, 0) + [block, block],
+        in_specs=level_specs(sums, red, exp, mix, 0) + [block, block] + wholes(*edges),
         out_specs=wholes(*outs),
         out_shape=outs,
         scratch_shapes=[
             pltpu.VMEM((8, dim), F32),
-            pltpu.VMEM((rows, cols, dim), F32),
+            pltpu.VMEM((rows + 3, cols, dim), F32),
             pltpu.VMEM((dim // 128, cols, 128), F32),
             pltpu.VMEM((high * before, dim), F32),
             pltpu.VMEM((high * after, dim), F32),
@@ -513,7 +634,7 @@
         compiler_params=params(32),
         cost_estimate=cost(2 * rows * cols * dim * dim, 6 * rows * cols * dim),
         name="mix0",
-    )(sums, red, exp, mix, g, rest)
+    )(sums, red, exp, mix, g, rest, *edges)
 
 
 def mix1_kernel(cells, size, before, sums, red, exp, mix, g_ref, rest, kernel, g_out, rest_out, part, z, line, padded):
@@ -524,7 +645,7 @@
     pos = position()
     row_low = shift - pos[0] * side_r
     col_low = shift - pos[1] * side_c
-    mix_lines(g_ref, gate, mix, rest, z, 0, (row_low, row_low + map_side, col_low, col_low + map_side))
+    mix_lines(g_ref, gate, mix, rest, z, range(rows), (row_low, row_low + map_side, col_low, col_low + map_side))
     count_r, count_c = padded.shape[0], (cols - 1) // 2
     row_two = 2 - pos[0] * (side_r // 2)
     col_two = 2 - pos[1] * (side_c // 2)
@@ -569,7 +690,7 @@
     gate = gate_row(sums, cells, red, exp)
     pos = position()
     bounds = (jnp.where(pos[0] == 0, 1, 0), rows, jnp.where(pos[1] == 0, 1, 0), cols)
-    mix_lines(g_ref, gate, mix, rest, z, 0, bounds)
+    mix_lines(g_ref, gate, mix, rest, z, range(rows), bounds)
     for i in range(high):
         keep[i * wide : i * wide + wide, :] = pooled_line(z, line, i, wide)
     x_out[...] = jnp.broadcast_to(keep[...].astype(BF), x_out.shape)
@@ -604,12 +725,14 @@
     tiles = lax.axis_size("tile")
     cells = high * wide * tiles
     group = 2 * TILE_COLS
-    rims, first = exchange_rims(tile_map, side_pieces(tile_map, 2, 1), 2, 1, lambda held: keys_of(0, held))
-    g, rest, part = activate(tile_map, rims, dw_kernel, 0, 2, 1, 11)
+    inner = lambda sides, held: activate_inner(after_these(tile_map, held), *sides, dw_kernel, 2, 1, 10)
+    rims, (g, rest, part) = exchange_rims(tile_map, side_pieces(tile_map, 2, 1), 2, 1, inner)
+    g_edge, rest_edge, part = activate_edge(tile_map, rims, dw_kernel, part)
     coarse, to_right, to_left = mix0(
-        everyones(part), se_reduce, se_expand, mix_weight, g, rest, cells, high // 2, wide // 2, 6, 3, 11
+        everyones(part), se_reduce, se_expand, mix_weight, g, rest, (g_edge, rest_edge), cells, high // 2, wide // 2, 6, 3, 10
     )
-    rims, second = exchange_rims(coarse, (to_right, to_left), 6, 3, lambda held: keys_of(1, held))
+    both = lambda sides, held: keys_of(0, held) + keys_of(1, held)
+    rims, (kt0, vt0, kt1, vt1) = exchange_rims(coarse, (to_right, to_left), 6, 3, both)
     g, rest, part = activate(coarse, rims, dw_kernel, 1, 6, 3, high // 2 + 7)
     size = (high // 2, wide // 2, high // 2 * (tiles // TILE_COLS))
     g, rest, part = mix1(
@@ -620,7 +743,7 @@
     )
     groups = [list(range(group * x, group * x + group)) for x in range(tiles // group)]
     slab = lax.all_to_all(query, "tile", 0, 0, tiled=True, axis_index_groups=groups)
-    return slab.reshape(-1, dim), first, second
+    return slab.reshape(-1, dim), (kt0, kt1), (vt0, vt1)
 
 
 def body(
@@ -641,12 +764,12 @@
     def keys_of(window, held):
         return keys_values(after_these(tile_map, held), norm_gain, kv_weight, kv_bias, window)
 
-    slab, (kt0, vt0), (kt1, vt1) = query_slab(tile_map, dw_kernel, se_reduce, se_expand, mix_weight, keys_of)
+    slab, keys, values = query_slab(tile_map, dw_kernel, se_reduce, se_expand, mix_weight, keys_of)
     tiles = lax.axis_size("tile")
     group = 2 * TILE_COLS
     steps = tuple(range(1, tiles // group))
     others = [lax.ppermute(slab, "tile", [(t, t ^ group * step) for t in range(tiles)]) for step in steps]
-    rest = ((kt0, kt1), (vt0, vt1), tile_map, proj_weight, proj_bias)
+    rest = (keys, values, tile_map, proj_weight, proj_bias)
     started = attention((0,), [slab], *rest)
     return attention(steps, others, *rest, started)[None]
 

time: 184 us -> 179 us (0.973)
  waiting for transfers between devices: 15.5 us -> 9.59 us
    pallas_call x0 -> x2, Pallas kernels: none -> 11.6 us  [the longest x1 10.3 us: activate_inner(): pl.pallas_call(functools.partial(inner_kernel, before, after), grid=(rows...]
    pallas_call x2 -> x1, Pallas kernels: 15.9 us -> 4.58 us  [activate(): pl.pallas_call(functools.partial(act_kernel, before, after), grid=(rows /...]
    ppermute x8, waiting for transfers between devices: 12.3 us -> 6.37 us  [moved_by(): return lax.ppermute(value, 'tile', pairs)]
  transfers between devices with their start and end apart: 11 -> 11, of which waited for: 7 -> 5; matrix products, arithmetic and copies ran while one was open for 0% -> 0% of each run, Pallas kernels for 13% -> 19%
where the time goes in v4:
time: 179 us; the launch traced here: 178 us
  Pallas kernels  87.3 us (49%)
  blocking collectives  56.3 us (31%)
  starting transfers between devices  22.6 us (13%)
  waiting for transfers between devices  9.59 us (5%)
  local copies, waits for them, and re-layouts  1.95 us (1%)
    pallas_call x2, Pallas kernels, attention(): pl.pallas_call(functools.partial(attention_kernel, steps), in_specs=[VM]...  51.7 us
    all_to_all x3, blocking collectives, everyones(): return lax.all_to_all(copies, 'tile', 0, 0, tiled=True)  45 us
    ppermute x8, starting transfers between devices, moved_by(): return lax.ppermute(value, 'tile', pairs)  18.5 us
    all_to_all x1, blocking collectives, query_slab(): lax.all_to_all(query, 'tile', 0, 0, tiled=True, axis_index_groups=groups)  11.3 us
    pallas_call x1, Pallas kernels, activate_inner(): pl.pallas_call(functools.partial(inner_kernel, before, after), grid=(rows...  10.3 us
    pallas_call x2, Pallas kernels, keys_values(): pl.pallas_call(kv_kernel, grid=(win // step,), in_specs=[pl.BlockSpec((st...  9.62 us
    ppermute x8, waiting for transfers between devices, moved_by(): return lax.ppermute(value, 'tile', pairs)  6.37 us
    pallas_call x1, Pallas kernels, mix0(): pl.pallas_call(functools.partial(mix0_kernel, cells, before, after), grid...  5.25 us
  transfers between devices with their start and end apart: 11, of which 5 were waited for; matrix products, arithmetic and copies ran while one was open for 0% of the time, Pallas kernels for 19%

profile of v4, /device:TPU:0, one launch (start us, length us, event | category | flops | bytes accessed | tf_op | source)
XLA Modules:
  0.0 178.2 jit_solution(8572712110056905458)
XLA Ops:
  0.0 1.9 %copy-done = bf16[1,32,64,768]{3,2,1,0:T(8,128)(2,1)S(1)} copy-done((bf16[1,32,64,768]{3,2,1,0:T(8,128)(2,1)S(1)}, bf16[1,32,64,768]{3,2,1,0:T(8,128)(2,1)}, u32[]{:S(2)}) %copy-start) | copy-done | bytes 3145752
  2.0 1.3 collective-permute-start
  3.4 1.6 collective-permute-start.1
  4.9 4.1 %collective-permute-done.1.rest_1_.r_ref = bf16[32,768]{1,0:T(8,128)(2,1)S(1)} collective-permute-done((bf16[32,768]{1,0:T(8,128)(2,1)S(1)}, bf16[32,768]{1,0:T(8,128)(2,1)S(1)}, u32[]{:S(2)}, u32[]{:S(2)}) %collective-permute-start.1) | collective-permute-done | bytes 49184 | tf_op jit(solution)/shard_map/ppermute | solution.py:298
  9.1 5.5 %collective-permute-start.2 = (bf16[144,768]{1,0:T(8,128)(2,1)S(1)}, bf16[144,768]{1,0:T(8,128)(2,1)S(1)}, u32[]{:S(2)}, u32[]{:S(2)}) collective-permute-start(bf16[144,768]{1,0:T(8,128)(2,1)S(1)} %get-tuple-element.45), channel_id=1, source_target_pairs={{0,4},{1,5},{2,6},{3,7},{4,8},{5,9},{6,10},{7,11},{8,12},{9,13},{1... | collective-permute-start | bytes 663560 | tf_op jit(solution)/shard_map/ppermute | solution.py:298
  14.6 1.3 collective-permute-start.3
  15.9 10.3 %activate_inner.1 = (f32[30,72,768]{2,1,0:T(8,128)S(1)}, bf16[30,72,768]{2,1,0:T(8,128)(2,1)S(1)}, f32[32,8,128]{2,1,0:T(8,128)S(1)}) custom-call(bf16[32,64,768]{2,1,0:T(8,128)(2,1)S(1)} %bitcast.8, bf16[64,768]{1,0:T(8,128)(2,1)S(1)} %collective-permute-done.rest_0_.l_ref, bf16[32,768]{1,0:T(8,128)(2,1)S(1)} %collective-permute-done.1.rest_1_.r_ref, ...), custom_call_target="tpu_custom_call" | custom-call | flops 663552000 | bytes 9953280 | tf_op jit(solution)/shard_map/activate_inner/pallas_call | solution.py:501
  26.3 1.3 activate_edge.1
  27.6 17.9 %all_to_all.20.sums = f32[32,8,128]{2,1,0:T(8,128)S(1)} all-to-all(f32[32,8,128]{2,1,0:T(8,128)S(1)} %get-tuple-element.54), channel_id=1, replica_groups=mesh['scene'=4,'tile'=32] {'tile'}, dimensions={0} | all-to-all | bytes 262144 | tf_op jit(solution)/shard_map/all_to_all | solution.py:720
  45.5 5.3 %mix0.1 = (bf16[16,32,768]{2,1,0:T(8,128)(2,1)S(1)}, bf16[96,768]{1,0:T(8,128)(2,1)S(1)}, bf16[48,768]{1,0:T(8,128)(2,1)S(1)}) custom-call(f32[32,8,128]{2,1,0:T(8,128)S(1)} %all_to_all.20.sums, bf16[3,192,768]{2,1,0:T(8,128)(2,1)S(1)} %bitcast.15, bf16[3,192,768]{2,1,0:T(8,128)(2,1)S(1)} %copy-done.4, bf16[3,768,768]{2,1,0:T(8,128)(2,1)S(1)} %copy-done.2, ...), custom_call_target="tpu_custom_call" | custom-call | flops 2548039680 | bytes 9953280 | tf_op jit(solution)/shard_map/mix0/pallas_call | solution.py:621
  50.8 2.0 %collective-permute-start.4 = (bf16[96,768]{1,0:T(8,128)(2,1)S(1)}, bf16[96,768]{1,0:T(8,128)(2,1)S(1)}, u32[]{:S(2)}, u32[]{:S(2)}) collective-permute-start(bf16[96,768]{1,0:T(8,128)(2,1)S(1)} %get-tuple-element.60), channel_id=1, source_target_pairs={{0,1},{1,2},{2,3},{4,5},{5,6},{6,7},{8,9},{9,10},{10,11},{12,13},{... | collective-permute-start | bytes 442376 | tf_op jit(solution)/shard_map/ppermute | solution.py:298
  52.8 1.3 collective-permute-start.5
  54.1 1.9 %collective-permute-done.5.rest_1_.r_ref = bf16[48,768]{1,0:T(8,128)(2,1)S(1)} collective-permute-done((bf16[48,768]{1,0:T(8,128)(2,1)S(1)}, bf16[48,768]{1,0:T(8,128)(2,1)S(1)}, u32[]{:S(2)}, u32[]{:S(2)}) %collective-permute-start.5) | collective-permute-done | bytes 73760 | tf_op jit(solution)/shard_map/ppermute | solution.py:298
  56.0 0.2 line_pieces.3
  56.2 4.1 %collective-permute-start.6 = (bf16[256,768]{1,0:T(8,128)(2,1)S(1)}, bf16[256,768]{1,0:T(8,128)(2,1)S(1)}, u32[]{:S(2)}, u32[]{:S(2)}) collective-permute-start(bf16[256,768]{1,0:T(8,128)(2,1)S(1)} %get-tuple-element.62), channel_id=1, source_target_pairs={{0,4},{1,5},{2,6},{3,7},{4,8},{5,9},{6,10},{7,11},{8,12},{9,13},{1... | collective-permute-start | bytes 1179656 | tf_op jit(solution)/shard_map/ppermute | solution.py:298
  60.3 1.5 collective-permute-start.7
  61.8 4.8 %keys_values.3 = (bf16[6,1024,128]{2,1,0:T(8,128)(2,1)S(1)}, bf16[768,1024]{1,0:T(8,128)(2,1)S(1)}) custom-call(bf16[32,64,768]{2,1,0:T(8,128)(2,1)S(1)} %bitcast.11, f32[768]{0:T(1024)S(1)} %copy-done.9, bf16[768,1536]{1,0:T(8,128)(2,1)S(1)} %copy-done.6, f32[1536]{0:T(1024)S(1)} %copy-done.8), custom_call_target="tpu_custom_call" | custom-call | flops 4831838208 | bytes 8388608 | tf_op jit(solution)/shard_map/keys_values/pallas_call | solution.py:41
  66.6 4.8 %keys_values.2 = (bf16[6,1024,128]{2,1,0:T(8,128)(2,1)S(1)}, bf16[768,1024]{1,0:T(8,128)(2,1)S(1)}) custom-call(bf16[32,64,768]{2,1,0:T(8,128)(2,1)S(1)} %bitcast.12, f32[768]{0:T(1024)S(1)} %copy-done.9, bf16[768,1536]{1,0:T(8,128)(2,1)S(1)} %copy-done.6, f32[1536]{0:T(1024)S(1)} %copy-done.8), custom_call_target="tpu_custom_call" | custom-call | flops 4831838208 | bytes 8388608 | tf_op jit(solution)/shard_map/keys_values/pallas_call | solution.py:41
  71.5 0.4 collective-permute-done.6.a_ref
  71.9 4.6 %activate.1 = (f32[23,40,768]{2,1,0:T(8,128)S(1)}, bf16[23,40,768]{2,1,0:T(8,128)(2,1)S(1)}, f32[32,8,128]{2,1,0:T(8,128)S(1)}) custom-call(bf16[16,32,768]{2,1,0:T(8,128)(2,1)S(1)} %get-tuple-element.59.top_ref.low_ref.x_ref, bf16[96,768]{1,0:T(8,128)(2,1)S(1)} %collective-permute-done.4.rest_0_.l_ref, ...), custom_call_target="tpu_custom_call" | custom-call | flops 282624000 | bytes 4239360 | tf_op jit(solution)/shard_map/activate/pallas_call | solution.py:444
  76.5 15.9 %all_to_all.21.sums = f32[32,8,128]{2,1,0:T(8,128)S(1)} all-to-all(f32[32,8,128]{2,1,0:T(8,128)S(1)} %get-tuple-element.71), channel_id=1, replica_groups=mesh['scene'=4,'tile'=32] {'tile'}, dimensions={0} | all-to-all | bytes 262144 | tf_op jit(solution)/shard_map/all_to_all | solution.py:720
  92.3 3.2 %mix1.1 = (f32[9,24,768]{2,1,0:T(8,128)S(1)}, bf16[9,24,768]{2,1,0:T(8,128)(2,1)S(1)}, f32[32,8,128]{2,1,0:T(8,128)S(1)}) custom-call(f32[32,8,128]{2,1,0:T(8,128)S(1)} %all_to_all.21.sums, bf16[3,192,768]{2,1,0:T(8,128)(2,1)S(1)} %bitcast.16, bf16[3,192,768]{2,1,0:T(8,128)(2,1)S(1)} %copy-done.4, bf16[3,768,768]{2,1,0:T(8,128)(2,1)S(1)} %copy-done.2, ...), custom_call_target="tpu_custom_call" | custom-call | flops 1085276160 | bytes 4239360 | tf_op jit(solution)/shard_map/mix1/pallas_call | solution.py:671
  95.6 11.3 %all_to_all.22.sums = f32[32,8,128]{2,1,0:T(8,128)S(1)} all-to-all(f32[32,8,128]{2,1,0:T(8,128)S(1)} %get-tuple-element.74), channel_id=1, replica_groups=mesh['scene'=4,'tile'=32] {'tile'}, dimensions={0} | all-to-all | bytes 262144 | tf_op jit(solution)/shard_map/all_to_all | solution.py:720
  106.8 0.9 mix2.1
  107.7 11.3 %all_to_all.23 = bf16[8,32,768]{2,1,0:T(8,128)(2,1)S(1)} all-to-all(bf16[8,32,768]{2,1,0:T(8,128)(2,1)S(1)} %mix2.1), channel_id=1, replica_groups={{0,1,2,3,4,5,6,7},{8,9,10,11,12,13,14,15},{16,17,18,19,20,21,22,23},{24..., dimensions={0} | all-to-all | bytes 786432 | tf_op jit(solution)/shard_map/all_to_all | solution.py:745
  119.1 1.1 collective-permute-start.10
  120.2 1.5 collective-permute-start.9
  121.7 1.5 collective-permute-start.8
  123.2 13.6 %attention.2.refs_10_ = bf16[32,64,768]{2,1,0:T(8,128)(2,1)} custom-call(bf16[256,768]{1,0:T(8,128)(2,1)S(1)} %bitcast.21, bf16[6,1024,128]{2,1,0:T(8,128)(2,1)S(1)} %get-tuple-element.77.refs_1_.refs_3_, bf16[6,1024,128]{2,1,0:T(8,128)(2,1)S(1)} %get-tuple-element.78.refs_2_.refs_4_, bf16[768,1024]{1,0:T(8,128)(2,1)S(1)} %get-tuple-element.79.refs_3_.refs_5_, ...), custom_call_target="tpu_custom_call" | custom-call | flops 12884901888 | bytes 12582912 | tf_op jit(solution)/shard_map/attention/pallas_call | solution.py:152
  136.8 2.6 %collective-permute-done.10.refs_2_ = bf16[256,768]{1,0:T(8,128)(2,1)S(1)} collective-permute-done((bf16[256,768]{1,0:T(8,128)(2,1)S(1)}, bf16[256,768]{1,0:T(8,128)(2,1)S(1)}, u32[]{:S(2)}, u32[]{:S(2)}) %collective-permute-start.10) | collective-permute-done | bytes 393248 | tf_op jit(solution)/shard_map/ppermute | solution.py:771
  139.4 0.6 collective-permute-done.8.refs_0_
  140.0 38.1 %attention.3 = bf16[32,64,768]{2,1,0:T(8,128)(2,1)} custom-call(bf16[256,768]{1,0:T(8,128)(2,1)S(1)} %collective-permute-done.8.refs_0_, bf16[256,768]{1,0:T(8,128)(2,1)S(1)} %collective-permute-done.9.refs_1_, bf16[256,768]{1,0:T(8,128)(2,1)S(1)} %collective-permute-done.10.refs_2_, ...), custom_call_target="tpu_custom_call", output_to_operand_aliasing={{}: (10, {})} | custom-call | flops 38654705664 | bytes 12582912 | tf_op jit(solution)/shard_map/attention/pallas_call | solution.py:152
  (29 shorter events, 0.3 us)
Async XLA Ops:
  0.0 1.9 %copy-start = (bf16[1,32,64,768]{3,2,1,0:T(8,128)(2,1)S(1)}, bf16[1,32,64,768]{3,2,1,0:T(8,128)(2,1)}, u32[]{:S(2)}) copy-start(bf16[1,32,64,768]{3,2,1,0:T(8,128)(2,1)} %param.10) | copy-start | bytes 9437188
  2.0 6.9 %collective-permute-start = (bf16[64,768]{1,0:T(8,128)(2,1)S(1)}, bf16[64,768]{1,0:T(8,128)(2,1)S(1)}, u32[]{:S(2)}, u32[]{:S(2)}) collective-permute-start(bf16[64,768]{1,0:T(8,128)(2,1)S(1)} %get-tuple-element.43), channel_id=1, source_target_pairs={{0,1},{1,2},{2,3},{4,5},{5,6},{6,7},{8,9},{9,10},{10,11},{12,13},{... | collective-permute-start | bytes 294920 | tf_op jit(solution)/shard_map/ppermute | solution.py:298
  3.3 12.6 %copy-start.1 = (bf16[1,32,64,768]{3,2,1,0:T(8,128)(2,1)S(1)}, bf16[1,32,64,768]{3,2,1,0:T(8,128)(2,1)}, u32[]{:S(2)}) copy-start(bf16[1,32,64,768]{3,2,1,0:T(8,128)(2,1)} %param.10) | copy-start | bytes 9437188
  3.3 12.6 %copy-start.5 = (bf16[3,3,3,768]{3,2,1,0:T(4,128)(2,1)S(1)}, bf16[3,3,3,768]{3,2,1,0:T(4,128)(2,1)}, u32[]{:S(2)}) copy-start(bf16[3,3,3,768]{3,2,1,0:T(4,128)(2,1)} %kernel.1) | copy-start | bytes 124420
  3.4 5.6 %collective-permute-start.1 = (bf16[32,768]{1,0:T(8,128)(2,1)S(1)}, bf16[32,768]{1,0:T(8,128)(2,1)S(1)}, u32[]{:S(2)}, u32[]{:S(2)}) collective-permute-start(bf16[32,768]{1,0:T(8,128)(2,1)S(1)} %get-tuple-element.44), channel_id=1, source_target_pairs={{1,0},{2,1},{3,2},{5,4},{6,5},{7,6},{9,8},{10,9},{11,10},{13,12},{... | collective-permute-start | bytes 147464 | tf_op jit(solution)/shard_map/ppermute | solution.py:298
  9.1 17.2 %collective-permute-start.2 = (bf16[144,768]{1,0:T(8,128)(2,1)S(1)}, bf16[144,768]{1,0:T(8,128)(2,1)S(1)}, u32[]{:S(2)}, u32[]{:S(2)}) collective-permute-start(bf16[144,768]{1,0:T(8,128)(2,1)S(1)} %get-tuple-element.45), channel_id=1, source_target_pairs={{0,4},{1,5},{2,6},{3,7},{4,8},{5,9},{6,10},{7,11},{8,12},{9,13},{1... | collective-permute-start | bytes 663560 | tf_op jit(solution)/shard_map/ppermute | solution.py:298
  14.6 11.7 %collective-permute-start.3 = (bf16[80,768]{1,0:T(8,128)(2,1)S(1)}, bf16[80,768]{1,0:T(8,128)(2,1)S(1)}, u32[]{:S(2)}, u32[]{:S(2)}) collective-permute-start(bf16[80,768]{1,0:T(8,128)(2,1)S(1)} %get-tuple-element.46), channel_id=1, source_target_pairs={{4,0},{5,1},{6,2},{7,3},{8,4},{9,5},{10,6},{11,7},{12,8},{13,9},{1... | collective-permute-start | bytes 368648 | tf_op jit(solution)/shard_map/ppermute | solution.py:298
  26.3 19.2 %copy-start.2 = (bf16[3,768,768]{2,1,0:T(8,128)(2,1)S(1)}, bf16[3,768,768]{2,1,0:T(8,128)(2,1)}, u32[]{:S(2)}) copy-start(bf16[3,768,768]{2,1,0:T(8,128)(2,1)} %mix.5) | copy-start | bytes 10616836
  26.3 19.2 %copy-start.3 = (bf16[3,768,192]{1,2,0:T(8,128)(2,1)S(1)}, bf16[3,768,192]{1,2,0:T(8,128)(2,1)}, u32[]{:S(2)}) copy-start(bf16[3,768,192]{1,2,0:T(8,128)(2,1)} %param.12) | copy-start | bytes 2654212
  26.3 19.2 %copy-start.4 = (bf16[3,192,768]{2,1,0:T(8,128)(2,1)S(1)}, bf16[3,192,768]{2,1,0:T(8,128)(2,1)}, u32[]{:S(2)}) copy-start(bf16[3,192,768]{2,1,0:T(8,128)(2,1)} %exp.5) | copy-start | bytes 2654212
  45.5 16.3 %copy-start.6 = (bf16[768,1536]{1,0:T(8,128)(2,1)S(1)}, bf16[768,1536]{1,0:T(8,128)(2,1)}, u32[]{:S(2)}) copy-start(bf16[768,1536]{1,0:T(8,128)(2,1)} %w_ref.3) | copy-start | bytes 7077892
  45.5 16.3 %copy-start.8 = (f32[1536]{0:T(1024)S(1)}, f32[1536]{0:T(1024)}, u32[]{:S(2)}) copy-start(f32[1536]{0:T(1024)} %b_ref.3) | copy-start | bytes 18436
  45.5 16.3 %copy-start.9 = (f32[768]{0:T(1024)S(1)}, f32[768]{0:T(1024)}, u32[]{:S(2)}) copy-start(f32[768]{0:T(1024)} %gain_ref.3) | copy-start | bytes 9220
  50.8 5.2 %collective-permute-start.4 = (bf16[96,768]{1,0:T(8,128)(2,1)S(1)}, bf16[96,768]{1,0:T(8,128)(2,1)S(1)}, u32[]{:S(2)}, u32[]{:S(2)}) collective-permute-start(bf16[96,768]{1,0:T(8,128)(2,1)S(1)} %get-tuple-element.60), channel_id=1, source_target_pairs={{0,1},{1,2},{2,3},{4,5},{5,6},{6,7},{8,9},{9,10},{10,11},{12,13},{... | collective-permute-start | bytes 442376 | tf_op jit(solution)/shard_map/ppermute | solution.py:298
  52.8 3.2 %collective-permute-start.5 = (bf16[48,768]{1,0:T(8,128)(2,1)S(1)}, bf16[48,768]{1,0:T(8,128)(2,1)S(1)}, u32[]{:S(2)}, u32[]{:S(2)}) collective-permute-start(bf16[48,768]{1,0:T(8,128)(2,1)S(1)} %get-tuple-element.61), channel_id=1, source_target_pairs={{1,0},{2,1},{3,2},{5,4},{6,5},{7,6},{9,8},{10,9},{11,10},{13,12},{... | collective-permute-start | bytes 221192 | tf_op jit(solution)/shard_map/ppermute | solution.py:298
  56.2 15.6 %collective-permute-start.6 = (bf16[256,768]{1,0:T(8,128)(2,1)S(1)}, bf16[256,768]{1,0:T(8,128)(2,1)S(1)}, u32[]{:S(2)}, u32[]{:S(2)}) collective-permute-start(bf16[256,768]{1,0:T(8,128)(2,1)S(1)} %get-tuple-element.62), channel_id=1, source_target_pairs={{0,4},{1,5},{2,6},{3,7},{4,8},{5,9},{6,10},{7,11},{8,12},{9,13},{1... | collective-permute-start | bytes 1179656 | tf_op jit(solution)/shard_map/ppermute | solution.py:298
  60.3 11.1 %collective-permute-start.7 = (bf16[128,768]{1,0:T(8,128)(2,1)S(1)}, bf16[128,768]{1,0:T(8,128)(2,1)S(1)}, u32[]{:S(2)}, u32[]{:S(2)}) collective-permute-start(bf16[128,768]{1,0:T(8,128)(2,1)S(1)} %get-tuple-element.63), channel_id=1, source_target_pairs={{4,0},{5,1},{6,2},{7,3},{8,4},{9,5},{10,6},{11,7},{12,8},{13,9},{1... | collective-permute-start | bytes 589832 | tf_op jit(solution)/shard_map/ppermute | solution.py:298
  106.8 16.3 %copy-start.7 = (bf16[768,768]{1,0:T(8,128)(2,1)S(1)}, bf16[768,768]{1,0:T(8,128)(2,1)}, u32[]{:S(2)}) copy-start(bf16[768,768]{1,0:T(8,128)(2,1)} %refs_8_.1) | copy-start | bytes 3538948
  106.8 16.3 %copy-start.10 = (f32[768]{0:T(1024)S(1)}, f32[768]{0:T(1024)}, u32[]{:S(2)}) copy-start(f32[768]{0:T(1024)} %refs_9_.1) | copy-start | bytes 9220
  119.1 20.3 %collective-permute-start.10 = (bf16[256,768]{1,0:T(8,128)(2,1)S(1)}, bf16[256,768]{1,0:T(8,128)(2,1)S(1)}, u32[]{:S(2)}, u32[]{:S(2)}) collective-permute-start(bf16[256,768]{1,0:T(8,128)(2,1)S(1)} %bitcast.18), channel_id=1, source_target_pairs={{0,24},{1,25},{2,26},{3,27},{4,28},{5,29},{6,30},{7,31},{8,16},{9,... | collective-permute-start | bytes 1179656 | tf_op jit(solution)/shard_map/ppermute | solution.py:771
  120.2 19.2 %collective-permute-start.9 = (bf16[256,768]{1,0:T(8,128)(2,1)S(1)}, bf16[256,768]{1,0:T(8,128)(2,1)S(1)}, u32[]{:S(2)}, u32[]{:S(2)}) collective-permute-start(bf16[256,768]{1,0:T(8,128)(2,1)S(1)} %bitcast.19), channel_id=1, source_target_pairs={{0,16},{1,17},{2,18},{3,19},{4,20},{5,21},{6,22},{7,23},{8,24},{9,... | collective-permute-start | bytes 1179656 | tf_op jit(solution)/shard_map/ppermute | solution.py:771
  121.7 18.3 %collective-permute-start.8 = (bf16[256,768]{1,0:T(8,128)(2,1)S(1)}, bf16[256,768]{1,0:T(8,128)(2,1)S(1)}, u32[]{:S(2)}, u32[]{:S(2)}) collective-permute-start(bf16[256,768]{1,0:T(8,128)(2,1)S(1)} %bitcast.20), channel_id=1, source_target_pairs={{0,8},{1,9},{2,10},{3,11},{4,12},{5,13},{6,14},{7,15},{8,0},{9,1},... | collective-permute-start | bytes 1179656 | tf_op jit(solution)/shard_map/ppermute | solution.py:771
